TPU v7x, 32 devices: a whole 2x2x4 slice. The times are simulated.
32 devices in a mesh: slab: 8 (over z, x), plane: 4 (over y, core).
Axes of the slice: x: 2, y: 2, z: 4, core: 2. Of those that a mesh axis runs over, the one named last changes fastest.
Arguments:
- displacement: float32 [3, 64, 128, 256], P(None, 'slab', 'plane'), may hold values from -4 to 4
- velocity: float32 [3, 64, 128, 256], P(None, 'slab', 'plane'), may hold values from -4 to 4
- body_load: float32 [3, 64, 128, 256], P(None, 'slab', 'plane'), may hold values from -6 to 6
- damaged: int32 [64, 128, 256], P('slab', 'plane'), may hold values from 0 to 1, as said below
- eroded: int32 [64, 128, 256], P('slab', 'plane'), may hold values 0 or 1
- material: int32 [64, 128, 256], P('slab', 'plane'), may hold values from 0 to 7
- stiff_table: float32 [8], replicated, may hold values from 0.1 to 1
Outputs:
- new_displacement: float32 [3, 64, 128, 256], P(None, 'slab', 'plane')
- new_velocity: float32 [3, 64, 128, 256], P(None, 'slab', 'plane')
Inputs may be any that keep to these rules, and one draw needn't show every extreme that they name: damaged cells cluster in one run of neighbouring blocks of 8 planes along the first dimension (a quarter of all such blocks), whose place is drawn; elsewhere they are rare.
All inputs are finite; a program needn't handle non-finite values. No bound on the sum of `eroded` on one device may be relied on, other than what follows from the above.
Results may differ from a plain program's by a relative error of at most 0.00002.
Values sent between devices are 32-bit elements; how exact they have to be, the bound alone decides.
No kernel may reach another device: no remote copies, remote signals or barrier semaphores. Data moves between devices by JAX's collectives and lax.ppermute only.
A program may use at most 64 MiB of HBM per device.

v0:
```python
import jax
import jax.numpy as jnp
from jax import lax
from jax.sharding import PartitionSpec as P

SUBSTEPS = 4


def with_halo(cells, sides, width):
    for axis, dim in sides:
        count = lax.axis_size(axis)
        ends = count - 1
        head = lax.slice_in_dim(cells, 0, width, axis=dim)
        tail = lax.slice_in_dim(cells, cells.shape[dim] - width, cells.shape[dim], axis=dim)
        cells = jnp.concatenate(
            [
                lax.ppermute(tail, axis, [(i, (i + 1) % count) for i in range(ends)]),
                cells,
                lax.ppermute(head, axis, [((i + 1) % count, i) for i in range(ends)]),
            ],
            axis=dim,
        )
    return cells


def take(arr, dx, dy, dz):
    sx, sy, sz = (arr.shape[-3], arr.shape[-2], arr.shape[-1])
    return arr[..., 1 + dx : sx - 1 + dx, 1 + dy : sy - 1 + dy, 1 + dz : sz - 1 + dz]


def forces(field, stiff):
    field_pad = jnp.pad(field, ((0, 0), (0, 0), (0, 0), (1, 1)))
    stiff_pad = jnp.pad(stiff, ((0, 0), (0, 0), (1, 1)))
    center = take(field_pad, 0, 0, 0)
    kcenter = take(stiff_pad, 0, 0, 0)
    total = jnp.zeros_like(center)
    for shift in ((1, 0, 0), (-1, 0, 0), (0, 1, 0), (0, -1, 0), (0, 0, 1), (0, 0, -1)):
        other = take(field_pad, shift[0], shift[1], shift[2])
        kface = jnp.minimum(kcenter, take(stiff_pad, shift[0], shift[1], shift[2]))
        total = total + kface[None] * (other - center)
    return total


def lookup_stiffness(material, stiff_table):
    total = jnp.zeros(material.shape, jnp.float32)
    for index in range(stiff_table.shape[0]):
        total = total + jnp.where(material == index, stiff_table[index], 0.0)
    return total


def per_device(displacement, velocity, body_load, damaged, eroded, material, stiff_table):
    stiff = lookup_stiffness(material, stiff_table) * (1 - eroded).astype(jnp.float32)
    step = jnp.where(damaged == 1, 0.5 / SUBSTEPS, 0.5).astype(jnp.float32)
    stiff_ext = with_halo(stiff, (("slab", 0), ("plane", 1)), 1)
    for sub in range(SUBSTEPS):
        active = jnp.where((damaged == 1) | (sub == 0), 1.0, 0.0).astype(jnp.float32)
        field_ext = with_halo(displacement, (("slab", 1), ("plane", 2)), 1)
        force = forces(field_ext, stiff_ext)
        rate = (active * step)[None]
        velocity = velocity + rate * (force + body_load - 0.2 * velocity)
        displacement = displacement + rate * velocity
    return (displacement, velocity)


def solution(mesh):
    placed = (
        P(None, "slab", "plane", None),
        P(None, "slab", "plane", None),
        P(None, "slab", "plane", None),
        P("slab", "plane", None),
        P("slab", "plane", None),
        P("slab", "plane", None),
        P(),
    )
    return jax.shard_map(
        per_device,
        mesh=mesh,
        in_specs=placed,
        out_specs=(P(None, "slab", "plane", None), P(None, "slab", "plane", None)),
        check_vma=False,
    )
```

profile of v0, /device:TPU:3, one launch (start us, length us, event | category | flops | bytes accessed | tf_op | source)
XLA Modules:
  0.0 103.6 jit_solution(16886780787304829661)
XLA Ops:
  0.6 0.0 copy-start.1
  0.6 1.0 fusion.90
  1.7 1.9 %collective-permute-start.1 = (f32[3,1,32,256]{3,2,1,0:T(8,128)S(1)}, f32[3,1,32,256]{3,2,1,0:T(8,128)S(1)}, u32[]{:S(2)}, u32[]{:S(2)}) collective-permute-start(f32[3,1,32,256]{3,2,1,0:T(8,128)S(1)} %get-tuple-element.28), channel_id=1, source_target_pairs={{4,0},{8,4},{12,8},{16,12},{20,16},{24,20},{28,24},{5,1},{9,5},{13... | collective-permute-start | bytes 294920 | tf_op jit(solution)/shard_map/ppermute | solution.py:19
  3.6 4.3 %collective-permute-start.3 = (f32[3,1,32,256]{3,2,1,0:T(8,128)S(1)}, f32[3,1,32,256]{3,2,1,0:T(8,128)S(1)}, u32[]{:S(2)}, u32[]{:S(2)}) collective-permute-start(f32[3,1,32,256]{3,2,1,0:T(8,128)S(1)} %get-tuple-element.29), channel_id=1, source_target_pairs={{0,4},{4,8},{8,12},{12,16},{16,20},{20,24},{24,28},{1,5},{5,9},{9,... | collective-permute-start | bytes 294920 | tf_op jit(solution)/shard_map/ppermute | solution.py:17
  7.9 1.6 %fusion.92 = (f32[1]{0:T(128)}, f32[1]{0:T(128)}, f32[1]{0:T(128)}, f32[1]{0:T(128)}, f32[1]{0:T(128)}, /*index=5*/f32[1]{0:T(128)}, f32[1]{0:T(128)}, f32[1]{0:T(128)}) fusion(f32[8]{0:T(128)} %param.13), kind=kLoop, calls=%fused_computation.179 | loop fusion | bytes 64 | tf_op jit(solution)/shard_map/slice | solution.py:47
  9.5 6.2 %convert_multiply_fusion = f32[8,32,256]{2,1,0:T(8,128)S(1)} fusion(s32[8,32,256]{2,1,0:T(8,128)} %param.11, s32[8,32,256]{2,1,0:T(8,128)} %param.12, f32[]{:T(128)} %bitcast.7, f32[]{:T(128)} %bitcast.6, f32[]{:T(128)} %bitcast.5, f32[]{:T(128)} %bitcast.4, f32[]{:T(128)} %bitcast.3, f32[]{:T(128)} %bitcast.2, f32[]{:T(128)} %bitcast.1, f32[]{:T(128)} %bitcast), kind=kLoop, calls=%fused_computation.155 | loop fusion | flops 1703936 | bytes 786464 | tf_op jit(solution)/shard_map/mul | solution.py:52
  15.7 2.3 %collective-permute-start.2 = (f32[1,32,256]{2,1,0:T(8,128)S(1)}, f32[1,32,256]{2,1,0:T(8,128)S(1)}, u32[]{:S(2)}, u32[]{:S(2)}) collective-permute-start(f32[1,32,256]{2,1,0:T(8,128)S(1)} %get-tuple-element.38), channel_id=1, source_target_pairs={{0,4},{4,8},{8,12},{12,16},{16,20},{20,24},{24,28},{1,5},{5,9},{9,... | collective-permute-start | bytes 98312 | tf_op jit(solution)/shard_map/ppermute | solution.py:17
  18.0 3.0 %collective-permute-start = (f32[1,32,256]{2,1,0:T(8,128)S(1)}, f32[1,32,256]{2,1,0:T(8,128)S(1)}, u32[]{:S(2)}, u32[]{:S(2)}) collective-permute-start(f32[1,32,256]{2,1,0:T(8,128)S(1)} %get-tuple-element.39), channel_id=1, source_target_pairs={{4,0},{8,4},{12,8},{16,12},{20,16},{24,20},{28,24},{5,1},{9,5},{13... | collective-permute-start | bytes 98312 | tf_op jit(solution)/shard_map/ppermute | solution.py:19
  21.0 1.0 select_multiply_fusion
  22.0 0.0 collective-permute-done.2
  22.0 1.5 %collective-permute-done = f32[1,32,256]{2,1,0:T(8,128)S(1)} collective-permute-done((f32[1,32,256]{2,1,0:T(8,128)S(1)}, f32[1,32,256]{2,1,0:T(8,128)S(1)}, u32[]{:S(2)}, u32[]{:S(2)}) %collective-permute-start) | collective-permute-done | bytes 32800 | tf_op jit(solution)/shard_map/ppermute | solution.py:19
  23.5 5.7 %collective-permute-start.6 = (f32[10,1,256]{2,1,0:T(1,128)S(1)}, f32[10,1,256]{2,1,0:T(1,128)S(1)}, u32[]{:S(2)}, u32[]{:S(2)}) collective-permute-start(f32[10,1,256]{2,1,0:T(1,128)S(1)} %get-tuple-element.32), channel_id=1, source_target_pairs={{0,1},{1,2},{2,3},{4,5},{5,6},{6,7},{8,9},{9,10},{10,11},{12,13},{... | collective-permute-start | bytes 30728 | tf_op jit(solution)/shard_map/ppermute | solution.py:17
  29.3 1.9 %collective-permute-start.4 = (f32[10,1,256]{2,1,0:T(1,128)S(1)}, f32[10,1,256]{2,1,0:T(1,128)S(1)}, u32[]{:S(2)}, u32[]{:S(2)}) collective-permute-start(f32[10,1,256]{2,1,0:T(1,128)S(1)} %get-tuple-element.33), channel_id=1, source_target_pairs={{1,0},{2,1},{3,2},{5,4},{6,5},{7,6},{9,8},{10,9},{11,10},{13,12},{... | collective-permute-start | bytes 30728 | tf_op jit(solution)/shard_map/ppermute | solution.py:19
  31.2 0.0 collective-permute-done.6
  31.2 3.0 %collective-permute-done.4 = f32[10,1,256]{2,1,0:T(1,128)S(1)} collective-permute-done((f32[10,1,256]{2,1,0:T(1,128)S(1)}, f32[10,1,256]{2,1,0:T(1,128)S(1)}, u32[]{:S(2)}, u32[]{:S(2)}) %collective-permute-start.4) | collective-permute-done | bytes 10272 | tf_op jit(solution)/shard_map/ppermute | solution.py:19
  34.2 0.3 select_maximum_fusion.14
  34.6 0.0 collective-permute-done.3
  34.6 0.0 copy-done.1
  34.6 0.1 constant_dynamic-update-slice_fusion.1
  34.6 0.0 collective-permute-done.1
  34.7 1.9 %collective-permute-start.7 = (f32[3,10,1,256]{3,2,1,0:T(1,128)S(1)}, f32[3,10,1,256]{3,2,1,0:T(1,128)S(1)}, u32[]{:S(2)}, u32[]{:S(2)}) collective-permute-start(f32[3,10,1,256]{3,2,1,0:T(1,128)S(1)} %get-tuple-element.18), channel_id=1, source_target_pairs={{0,1},{1,2},{2,3},{4,5},{5,6},{6,7},{8,9},{9,10},{10,11},{12,13},{... | collective-permute-start | bytes 92168 | tf_op jit(solution)/shard_map/ppermute | solution.py:17
  36.7 2.4 %collective-permute-start.5 = (f32[3,10,1,256]{3,2,1,0:T(1,128)S(1)}, f32[3,10,1,256]{3,2,1,0:T(1,128)S(1)}, u32[]{:S(2)}, u32[]{:S(2)}) collective-permute-start(f32[3,10,1,256]{3,2,1,0:T(1,128)S(1)} %get-tuple-element.19), channel_id=1, source_target_pairs={{1,0},{2,1},{3,2},{5,4},{6,5},{7,6},{9,8},{10,9},{11,10},{13,12},{... | collective-permute-start | bytes 92168 | tf_op jit(solution)/shard_map/ppermute | solution.py:19
  39.1 0.2 fusion.79
  39.3 0.0 copy-start
  39.3 0.0 copy-start.2
  39.3 0.0 collective-permute-done.7
  39.3 2.5 %collective-permute-done.5 = f32[3,10,1,256]{3,2,1,0:T(1,128)S(1)} collective-permute-done((f32[3,10,1,256]{3,2,1,0:T(1,128)S(1)}, f32[3,10,1,256]{3,2,1,0:T(1,128)S(1)}, u32[]{:S(2)}, u32[]{:S(2)}) %collective-permute-start.5) | collective-permute-done | bytes 30752 | tf_op jit(solution)/shard_map/ppermute | solution.py:19
  41.9 0.8 select_maximum_fusion.12
  42.7 0.0 copy-done
  42.7 0.0 copy-done.2
  42.7 1.1 %multiply_add_fusion.3 = (f32[3,8,32,256]{3,2,1,0:T(8,128)S(1)}, f32[3,8,32,256]{3,2,1,0:T(8,128)S(1)}) fusion(f32[3,8,32,256]{3,2,1,0:T(8,128)S(1)} %copy-done.1, f32[8,32,256]{2,1,0:T(8,128)S(1)} %broadcast_select_fusion, f32[3,8,32,256]{3,2,1,0:T(8,128)S(1)} %copy-done.2, f32[3,8,32,256]{3,2,1,0:T(8,128)S(1)} %copy-done, ...), kind=kLoop, calls=%fused_computation.134 | loop fusion | flops 5505024 | bytes 8581120 | tf_op jit(solution)/shard_map/add | solution.py:61
  43.8 3.1 %collective-permute-start.9 = (f32[3,1,32,256]{3,2,1,0:T(8,128)S(1)}, f32[3,1,32,256]{3,2,1,0:T(8,128)S(1)}, u32[]{:S(2)}, u32[]{:S(2)}) collective-permute-start(f32[3,1,32,256]{3,2,1,0:T(8,128)S(1)} %get-tuple-element.26), channel_id=1, source_target_pairs={{0,4},{4,8},{8,12},{12,16},{16,20},{20,24},{24,28},{1,5},{5,9},{9,... | collective-permute-start | bytes 294920 | tf_op jit(solution)/shard_map/ppermute | solution.py:17
  46.9 2.2 %collective-permute-start.8 = (f32[3,1,32,256]{3,2,1,0:T(8,128)S(1)}, f32[3,1,32,256]{3,2,1,0:T(8,128)S(1)}, u32[]{:S(2)}, u32[]{:S(2)}) collective-permute-start(f32[3,1,32,256]{3,2,1,0:T(8,128)S(1)} %get-tuple-element.27), channel_id=1, source_target_pairs={{4,0},{8,4},{12,8},{16,12},{20,16},{24,20},{28,24},{5,1},{9,5},{13... | collective-permute-start | bytes 294920 | tf_op jit(solution)/shard_map/ppermute | solution.py:19
  49.1 0.1 collective-permute-done.9
  49.2 4.2 %collective-permute-done.8 = f32[3,1,32,256]{3,2,1,0:T(8,128)S(1)} collective-permute-done((f32[3,1,32,256]{3,2,1,0:T(8,128)S(1)}, f32[3,1,32,256]{3,2,1,0:T(8,128)S(1)}, u32[]{:S(2)}, u32[]{:S(2)}) %collective-permute-start.8) | collective-permute-done | bytes 98336 | tf_op jit(solution)/shard_map/ppermute | solution.py:19
  53.4 3.2 %collective-permute-start.11 = (f32[3,10,1,256]{3,2,1,0:T(1,128)S(1)}, f32[3,10,1,256]{3,2,1,0:T(1,128)S(1)}, u32[]{:S(2)}, u32[]{:S(2)}) collective-permute-start(f32[3,10,1,256]{3,2,1,0:T(1,128)S(1)} %get-tuple-element.16), channel_id=1, source_target_pairs={{0,1},{1,2},{2,3},{4,5},{5,6},{6,7},{8,9},{9,10},{10,11},{12,13},{... | collective-permute-start | bytes 92168 | tf_op jit(solution)/shard_map/ppermute | solution.py:17
  56.6 1.9 %collective-permute-start.10 = (f32[3,10,1,256]{3,2,1,0:T(1,128)S(1)}, f32[3,10,1,256]{3,2,1,0:T(1,128)S(1)}, u32[]{:S(2)}, u32[]{:S(2)}) collective-permute-start(f32[3,10,1,256]{3,2,1,0:T(1,128)S(1)} %get-tuple-element.17), channel_id=1, source_target_pairs={{1,0},{2,1},{3,2},{5,4},{6,5},{7,6},{9,8},{10,9},{11,10},{13,12},{... | collective-permute-start | bytes 92168 | tf_op jit(solution)/shard_map/ppermute | solution.py:19
  58.5 0.0 collective-permute-done.11
  58.5 3.3 %collective-permute-done.10 = f32[3,10,1,256]{3,2,1,0:T(1,128)S(1)} collective-permute-done((f32[3,10,1,256]{3,2,1,0:T(1,128)S(1)}, f32[3,10,1,256]{3,2,1,0:T(1,128)S(1)}, u32[]{:S(2)}, u32[]{:S(2)}) %collective-permute-start.10) | collective-permute-done | bytes 30752 | tf_op jit(solution)/shard_map/ppermute | solution.py:19
  61.8 0.8 select_maximum_fusion.8
  62.6 1.0 multiply_add_fusion.2
  63.7 2.3 %collective-permute-start.13 = (f32[3,1,32,256]{3,2,1,0:T(8,128)S(1)}, f32[3,1,32,256]{3,2,1,0:T(8,128)S(1)}, u32[]{:S(2)}, u32[]{:S(2)}) collective-permute-start(f32[3,1,32,256]{3,2,1,0:T(8,128)S(1)} %get-tuple-element.24), channel_id=1, source_target_pairs={{0,4},{4,8},{8,12},{12,16},{16,20},{20,24},{24,28},{1,5},{5,9},{9,... | collective-permute-start | bytes 294920 | tf_op jit(solution)/shard_map/ppermute | solution.py:17
  66.0 3.0 %collective-permute-start.12 = (f32[3,1,32,256]{3,2,1,0:T(8,128)S(1)}, f32[3,1,32,256]{3,2,1,0:T(8,128)S(1)}, u32[]{:S(2)}, u32[]{:S(2)}) collective-permute-start(f32[3,1,32,256]{3,2,1,0:T(8,128)S(1)} %get-tuple-element.25), channel_id=1, source_target_pairs={{4,0},{8,4},{12,8},{16,12},{20,16},{24,20},{28,24},{5,1},{9,5},{13... | collective-permute-start | bytes 294920 | tf_op jit(solution)/shard_map/ppermute | solution.py:19
  69.0 0.1 collective-permute-done.13
  69.0 3.2 %collective-permute-done.12 = f32[3,1,32,256]{3,2,1,0:T(8,128)S(1)} collective-permute-done((f32[3,1,32,256]{3,2,1,0:T(8,128)S(1)}, f32[3,1,32,256]{3,2,1,0:T(8,128)S(1)}, u32[]{:S(2)}, u32[]{:S(2)}) %collective-permute-start.12) | collective-permute-done | bytes 98336 | tf_op jit(solution)/shard_map/ppermute | solution.py:19
  72.3 3.3 %collective-permute-start.15 = (f32[3,10,1,256]{3,2,1,0:T(1,128)S(1)}, f32[3,10,1,256]{3,2,1,0:T(1,128)S(1)}, u32[]{:S(2)}, u32[]{:S(2)}) collective-permute-start(f32[3,10,1,256]{3,2,1,0:T(1,128)S(1)} %get-tuple-element.14), channel_id=1, source_target_pairs={{0,1},{1,2},{2,3},{4,5},{5,6},{6,7},{8,9},{9,10},{10,11},{12,13},{... | collective-permute-start | bytes 92168 | tf_op jit(solution)/shard_map/ppermute | solution.py:17
  75.6 1.9 %collective-permute-start.14 = (f32[3,10,1,256]{3,2,1,0:T(1,128)S(1)}, f32[3,10,1,256]{3,2,1,0:T(1,128)S(1)}, u32[]{:S(2)}, u32[]{:S(2)}) collective-permute-start(f32[3,10,1,256]{3,2,1,0:T(1,128)S(1)} %get-tuple-element.15), channel_id=1, source_target_pairs={{1,0},{2,1},{3,2},{5,4},{6,5},{7,6},{9,8},{10,9},{11,10},{13,12},{... | collective-permute-start | bytes 92168 | tf_op jit(solution)/shard_map/ppermute | solution.py:19
  77.5 0.0 collective-permute-done.15
  77.6 3.3 %collective-permute-done.14 = f32[3,10,1,256]{3,2,1,0:T(1,128)S(1)} collective-permute-done((f32[3,10,1,256]{3,2,1,0:T(1,128)S(1)}, f32[3,10,1,256]{3,2,1,0:T(1,128)S(1)}, u32[]{:S(2)}, u32[]{:S(2)}) %collective-permute-start.14) | collective-permute-done | bytes 30752 | tf_op jit(solution)/shard_map/ppermute | solution.py:19
  80.8 0.8 select_maximum_fusion.4
  81.6 1.0 multiply_add_fusion.1
  82.7 3.1 %collective-permute-start.17 = (f32[3,1,32,256]{3,2,1,0:T(8,128)S(1)}, f32[3,1,32,256]{3,2,1,0:T(8,128)S(1)}, u32[]{:S(2)}, u32[]{:S(2)}) collective-permute-start(f32[3,1,32,256]{3,2,1,0:T(8,128)S(1)} %get-tuple-element.22), channel_id=1, source_target_pairs={{0,4},{4,8},{8,12},{12,16},{16,20},{20,24},{24,28},{1,5},{5,9},{9,... | collective-permute-start | bytes 294920 | tf_op jit(solution)/shard_map/ppermute | solution.py:17
  85.8 2.2 %collective-permute-start.16 = (f32[3,1,32,256]{3,2,1,0:T(8,128)S(1)}, f32[3,1,32,256]{3,2,1,0:T(8,128)S(1)}, u32[]{:S(2)}, u32[]{:S(2)}) collective-permute-start(f32[3,1,32,256]{3,2,1,0:T(8,128)S(1)} %get-tuple-element.23), channel_id=1, source_target_pairs={{4,0},{8,4},{12,8},{16,12},{20,16},{24,20},{28,24},{5,1},{9,5},{13... | collective-permute-start | bytes 294920 | tf_op jit(solution)/shard_map/ppermute | solution.py:19
  88.0 0.1 collective-permute-done.17
  88.1 4.0 %collective-permute-done.16 = f32[3,1,32,256]{3,2,1,0:T(8,128)S(1)} collective-permute-done((f32[3,1,32,256]{3,2,1,0:T(8,128)S(1)}, f32[3,1,32,256]{3,2,1,0:T(8,128)S(1)}, u32[]{:S(2)}, u32[]{:S(2)}) %collective-permute-start.16) | collective-permute-done | bytes 98336 | tf_op jit(solution)/shard_map/ppermute | solution.py:19
  92.1 3.3 %collective-permute-start.19 = (f32[3,10,1,256]{3,2,1,0:T(1,128)S(1)}, f32[3,10,1,256]{3,2,1,0:T(1,128)S(1)}, u32[]{:S(2)}, u32[]{:S(2)}) collective-permute-start(f32[3,10,1,256]{3,2,1,0:T(1,128)S(1)} %get-tuple-element.12), channel_id=1, source_target_pairs={{0,1},{1,2},{2,3},{4,5},{5,6},{6,7},{8,9},{9,10},{10,11},{12,13},{... | collective-permute-start | bytes 92168 | tf_op jit(solution)/shard_map/ppermute | solution.py:17
  95.5 1.9 %collective-permute-start.18 = (f32[3,10,1,256]{3,2,1,0:T(1,128)S(1)}, f32[3,10,1,256]{3,2,1,0:T(1,128)S(1)}, u32[]{:S(2)}, u32[]{:S(2)}) collective-permute-start(f32[3,10,1,256]{3,2,1,0:T(1,128)S(1)} %get-tuple-element.13), channel_id=1, source_target_pairs={{1,0},{2,1},{3,2},{5,4},{6,5},{7,6},{9,8},{10,9},{11,10},{13,12},{... | collective-permute-start | bytes 92168 | tf_op jit(solution)/shard_map/ppermute | solution.py:19
  97.4 0.0 collective-permute-done.19
  97.4 3.3 %collective-permute-done.18 = f32[3,10,1,256]{3,2,1,0:T(1,128)S(1)} collective-permute-done((f32[3,10,1,256]{3,2,1,0:T(1,128)S(1)}, f32[3,10,1,256]{3,2,1,0:T(1,128)S(1)}, u32[]{:S(2)}, u32[]{:S(2)}) %collective-permute-start.18) | collective-permute-done | bytes 30752 | tf_op jit(solution)/shard_map/ppermute | solution.py:19
  100.7 0.8 select_maximum_fusion
  101.5 2.1 %multiply_add_fusion = (f32[3,8,32,256]{3,2,1,0:T(8,128)}, f32[3,8,32,256]{3,2,1,0:T(8,128)}) fusion(f32[3,8,32,256]{3,2,1,0:T(8,128)S(1)} %get-tuple-element.4, f32[8,32,256]{2,1,0:T(8,128)S(1)} %get-tuple-element.8, f32[3,8,32,256]{3,2,1,0:T(8,128)S(1)} %get-tuple-element.5, f32[3,8,32,256]{3,2,1,0:T(8,128)S(1)} %copy-done, ...), kind=kLoop, calls=%fused_computation.131 | loop fusion | flops 6291456 | bytes 7598080 | tf_op jit(solution)/shard_map/add | solution.py:61
  (12 shorter events, 0.3 us)
Async XLA Ops:
  0.6 34.0 %copy-start.1 = (f32[3,8,32,256]{3,2,1,0:T(8,128)S(1)}, f32[3,8,32,256]{3,2,1,0:T(8,128)}, u32[]{:S(2)}) copy-start(f32[3,8,32,256]{3,2,1,0:T(8,128)} %param.7) | copy-start | bytes 2359300
  1.7 33.0 %collective-permute-start.1 = (f32[3,1,32,256]{3,2,1,0:T(8,128)S(1)}, f32[3,1,32,256]{3,2,1,0:T(8,128)S(1)}, u32[]{:S(2)}, u32[]{:S(2)}) collective-permute-start(f32[3,1,32,256]{3,2,1,0:T(8,128)S(1)} %get-tuple-element.28), channel_id=1, source_target_pairs={{4,0},{8,4},{12,8},{16,12},{20,16},{24,20},{28,24},{5,1},{9,5},{13... | collective-permute-start | bytes 294920 | tf_op jit(solution)/shard_map/ppermute | solution.py:19
  3.6 31.0 %collective-permute-start.3 = (f32[3,1,32,256]{3,2,1,0:T(8,128)S(1)}, f32[3,1,32,256]{3,2,1,0:T(8,128)S(1)}, u32[]{:S(2)}, u32[]{:S(2)}) collective-permute-start(f32[3,1,32,256]{3,2,1,0:T(8,128)S(1)} %get-tuple-element.29), channel_id=1, source_target_pairs={{0,4},{4,8},{8,12},{12,16},{16,20},{20,24},{24,28},{1,5},{5,9},{9,... | collective-permute-start | bytes 294920 | tf_op jit(solution)/shard_map/ppermute | solution.py:17
  15.7 6.3 %collective-permute-start.2 = (f32[1,32,256]{2,1,0:T(8,128)S(1)}, f32[1,32,256]{2,1,0:T(8,128)S(1)}, u32[]{:S(2)}, u32[]{:S(2)}) collective-permute-start(f32[1,32,256]{2,1,0:T(8,128)S(1)} %get-tuple-element.38), channel_id=1, source_target_pairs={{0,4},{4,8},{8,12},{12,16},{16,20},{20,24},{24,28},{1,5},{5,9},{9,... | collective-permute-start | bytes 98312 | tf_op jit(solution)/shard_map/ppermute | solution.py:17
  18.0 5.6 %collective-permute-start = (f32[1,32,256]{2,1,0:T(8,128)S(1)}, f32[1,32,256]{2,1,0:T(8,128)S(1)}, u32[]{:S(2)}, u32[]{:S(2)}) collective-permute-start(f32[1,32,256]{2,1,0:T(8,128)S(1)} %get-tuple-element.39), channel_id=1, source_target_pairs={{4,0},{8,4},{12,8},{16,12},{20,16},{24,20},{28,24},{5,1},{9,5},{13... | collective-permute-start | bytes 98312 | tf_op jit(solution)/shard_map/ppermute | solution.py:19
  23.5 7.7 %collective-permute-start.6 = (f32[10,1,256]{2,1,0:T(1,128)S(1)}, f32[10,1,256]{2,1,0:T(1,128)S(1)}, u32[]{:S(2)}, u32[]{:S(2)}) collective-permute-start(f32[10,1,256]{2,1,0:T(1,128)S(1)} %get-tuple-element.32), channel_id=1, source_target_pairs={{0,1},{1,2},{2,3},{4,5},{5,6},{6,7},{8,9},{9,10},{10,11},{12,13},{... | collective-permute-start | bytes 30728 | tf_op jit(solution)/shard_map/ppermute | solution.py:17
  29.3 5.0 %collective-permute-start.4 = (f32[10,1,256]{2,1,0:T(1,128)S(1)}, f32[10,1,256]{2,1,0:T(1,128)S(1)}, u32[]{:S(2)}, u32[]{:S(2)}) collective-permute-start(f32[10,1,256]{2,1,0:T(1,128)S(1)} %get-tuple-element.33), channel_id=1, source_target_pairs={{1,0},{2,1},{3,2},{5,4},{6,5},{7,6},{9,8},{10,9},{11,10},{13,12},{... | collective-permute-start | bytes 30728 | tf_op jit(solution)/shard_map/ppermute | solution.py:19
  34.7 4.6 %collective-permute-start.7 = (f32[3,10,1,256]{3,2,1,0:T(1,128)S(1)}, f32[3,10,1,256]{3,2,1,0:T(1,128)S(1)}, u32[]{:S(2)}, u32[]{:S(2)}) collective-permute-start(f32[3,10,1,256]{3,2,1,0:T(1,128)S(1)} %get-tuple-element.18), channel_id=1, source_target_pairs={{0,1},{1,2},{2,3},{4,5},{5,6},{6,7},{8,9},{9,10},{10,11},{12,13},{... | collective-permute-start | bytes 92168 | tf_op jit(solution)/shard_map/ppermute | solution.py:17
  36.7 5.2 %collective-permute-start.5 = (f32[3,10,1,256]{3,2,1,0:T(1,128)S(1)}, f32[3,10,1,256]{3,2,1,0:T(1,128)S(1)}, u32[]{:S(2)}, u32[]{:S(2)}) collective-permute-start(f32[3,10,1,256]{3,2,1,0:T(1,128)S(1)} %get-tuple-element.19), channel_id=1, source_target_pairs={{1,0},{2,1},{3,2},{5,4},{6,5},{7,6},{9,8},{10,9},{11,10},{13,12},{... | collective-permute-start | bytes 92168 | tf_op jit(solution)/shard_map/ppermute | solution.py:19
  39.3 3.4 %copy-start = (f32[3,8,32,256]{3,2,1,0:T(8,128)S(1)}, f32[3,8,32,256]{3,2,1,0:T(8,128)}, u32[]{:S(2)}) copy-start(f32[3,8,32,256]{3,2,1,0:T(8,128)} %param.9) | copy-start | bytes 2359300
  39.3 3.4 %copy-start.2 = (f32[3,8,32,256]{3,2,1,0:T(8,128)S(1)}, f32[3,8,32,256]{3,2,1,0:T(8,128)}, u32[]{:S(2)}) copy-start(f32[3,8,32,256]{3,2,1,0:T(8,128)} %param.8) | copy-start | bytes 2359300
  43.8 5.4 %collective-permute-start.9 = (f32[3,1,32,256]{3,2,1,0:T(8,128)S(1)}, f32[3,1,32,256]{3,2,1,0:T(8,128)S(1)}, u32[]{:S(2)}, u32[]{:S(2)}) collective-permute-start(f32[3,1,32,256]{3,2,1,0:T(8,128)S(1)} %get-tuple-element.26), channel_id=1, source_target_pairs={{0,4},{4,8},{8,12},{12,16},{16,20},{20,24},{24,28},{1,5},{5,9},{9,... | collective-permute-start | bytes 294920 | tf_op jit(solution)/shard_map/ppermute | solution.py:17
  46.9 6.4 %collective-permute-start.8 = (f32[3,1,32,256]{3,2,1,0:T(8,128)S(1)}, f32[3,1,32,256]{3,2,1,0:T(8,128)S(1)}, u32[]{:S(2)}, u32[]{:S(2)}) collective-permute-start(f32[3,1,32,256]{3,2,1,0:T(8,128)S(1)} %get-tuple-element.27), channel_id=1, source_target_pairs={{4,0},{8,4},{12,8},{16,12},{20,16},{24,20},{28,24},{5,1},{9,5},{13... | collective-permute-start | bytes 294920 | tf_op jit(solution)/shard_map/ppermute | solution.py:19
  53.4 5.1 %collective-permute-start.11 = (f32[3,10,1,256]{3,2,1,0:T(1,128)S(1)}, f32[3,10,1,256]{3,2,1,0:T(1,128)S(1)}, u32[]{:S(2)}, u32[]{:S(2)}) collective-permute-start(f32[3,10,1,256]{3,2,1,0:T(1,128)S(1)} %get-tuple-element.16), channel_id=1, source_target_pairs={{0,1},{1,2},{2,3},{4,5},{5,6},{6,7},{8,9},{9,10},{10,11},{12,13},{... | collective-permute-start | bytes 92168 | tf_op jit(solution)/shard_map/ppermute | solution.py:17
  56.6 5.2 %collective-permute-start.10 = (f32[3,10,1,256]{3,2,1,0:T(1,128)S(1)}, f32[3,10,1,256]{3,2,1,0:T(1,128)S(1)}, u32[]{:S(2)}, u32[]{:S(2)}) collective-permute-start(f32[3,10,1,256]{3,2,1,0:T(1,128)S(1)} %get-tuple-element.17), channel_id=1, source_target_pairs={{1,0},{2,1},{3,2},{5,4},{6,5},{7,6},{9,8},{10,9},{11,10},{13,12},{... | collective-permute-start | bytes 92168 | tf_op jit(solution)/shard_map/ppermute | solution.py:19
  63.7 5.4 %collective-permute-start.13 = (f32[3,1,32,256]{3,2,1,0:T(8,128)S(1)}, f32[3,1,32,256]{3,2,1,0:T(8,128)S(1)}, u32[]{:S(2)}, u32[]{:S(2)}) collective-permute-start(f32[3,1,32,256]{3,2,1,0:T(8,128)S(1)} %get-tuple-element.24), channel_id=1, source_target_pairs={{0,4},{4,8},{8,12},{12,16},{16,20},{20,24},{24,28},{1,5},{5,9},{9,... | collective-permute-start | bytes 294920 | tf_op jit(solution)/shard_map/ppermute | solution.py:17
  66.0 6.3 %collective-permute-start.12 = (f32[3,1,32,256]{3,2,1,0:T(8,128)S(1)}, f32[3,1,32,256]{3,2,1,0:T(8,128)S(1)}, u32[]{:S(2)}, u32[]{:S(2)}) collective-permute-start(f32[3,1,32,256]{3,2,1,0:T(8,128)S(1)} %get-tuple-element.25), channel_id=1, source_target_pairs={{4,0},{8,4},{12,8},{16,12},{20,16},{24,20},{28,24},{5,1},{9,5},{13... | collective-permute-start | bytes 294920 | tf_op jit(solution)/shard_map/ppermute | solution.py:19
  72.3 5.3 %collective-permute-start.15 = (f32[3,10,1,256]{3,2,1,0:T(1,128)S(1)}, f32[3,10,1,256]{3,2,1,0:T(1,128)S(1)}, u32[]{:S(2)}, u32[]{:S(2)}) collective-permute-start(f32[3,10,1,256]{3,2,1,0:T(1,128)S(1)} %get-tuple-element.14), channel_id=1, source_target_pairs={{0,1},{1,2},{2,3},{4,5},{5,6},{6,7},{8,9},{9,10},{10,11},{12,13},{... | collective-permute-start | bytes 92168 | tf_op jit(solution)/shard_map/ppermute | solution.py:17
  75.6 5.2 %collective-permute-start.14 = (f32[3,10,1,256]{3,2,1,0:T(1,128)S(1)}, f32[3,10,1,256]{3,2,1,0:T(1,128)S(1)}, u32[]{:S(2)}, u32[]{:S(2)}) collective-permute-start(f32[3,10,1,256]{3,2,1,0:T(1,128)S(1)} %get-tuple-element.15), channel_id=1, source_target_pairs={{1,0},{2,1},{3,2},{5,4},{6,5},{7,6},{9,8},{10,9},{11,10},{13,12},{... | collective-permute-start | bytes 92168 | tf_op jit(solution)/shard_map/ppermute | solution.py:19
  82.7 5.4 %collective-permute-start.17 = (f32[3,1,32,256]{3,2,1,0:T(8,128)S(1)}, f32[3,1,32,256]{3,2,1,0:T(8,128)S(1)}, u32[]{:S(2)}, u32[]{:S(2)}) collective-permute-start(f32[3,1,32,256]{3,2,1,0:T(8,128)S(1)} %get-tuple-element.22), channel_id=1, source_target_pairs={{0,4},{4,8},{8,12},{12,16},{16,20},{20,24},{24,28},{1,5},{5,9},{9,... | collective-permute-start | bytes 294920 | tf_op jit(solution)/shard_map/ppermute | solution.py:17
  85.8 6.3 %collective-permute-start.16 = (f32[3,1,32,256]{3,2,1,0:T(8,128)S(1)}, f32[3,1,32,256]{3,2,1,0:T(8,128)S(1)}, u32[]{:S(2)}, u32[]{:S(2)}) collective-permute-start(f32[3,1,32,256]{3,2,1,0:T(8,128)S(1)} %get-tuple-element.23), channel_id=1, source_target_pairs={{4,0},{8,4},{12,8},{16,12},{20,16},{24,20},{28,24},{5,1},{9,5},{13... | collective-permute-start | bytes 294920 | tf_op jit(solution)/shard_map/ppermute | solution.py:19
  92.1 5.3 %collective-permute-start.19 = (f32[3,10,1,256]{3,2,1,0:T(1,128)S(1)}, f32[3,10,1,256]{3,2,1,0:T(1,128)S(1)}, u32[]{:S(2)}, u32[]{:S(2)}) collective-permute-start(f32[3,10,1,256]{3,2,1,0:T(1,128)S(1)} %get-tuple-element.12), channel_id=1, source_target_pairs={{0,1},{1,2},{2,3},{4,5},{5,6},{6,7},{8,9},{9,10},{10,11},{12,13},{... | collective-permute-start | bytes 92168 | tf_op jit(solution)/shard_map/ppermute | solution.py:17
  95.5 5.2 %collective-permute-start.18 = (f32[3,10,1,256]{3,2,1,0:T(1,128)S(1)}, f32[3,10,1,256]{3,2,1,0:T(1,128)S(1)}, u32[]{:S(2)}, u32[]{:S(2)}) collective-permute-start(f32[3,10,1,256]{3,2,1,0:T(1,128)S(1)} %get-tuple-element.13), channel_id=1, source_target_pairs={{1,0},{2,1},{3,2},{5,4},{6,5},{7,6},{9,8},{10,9},{11,10},{13,12},{... | collective-permute-start | bytes 92168 | tf_op jit(solution)/shard_map/ppermute | solution.py:19
where the time goes:
time: 104 us
  starting transfers between devices  54.9 us (53%)
  waiting for transfers between devices  28.5 us (27%)
  other arithmetic  16.4 us (16%)
  local copies, waits for them, and re-layouts  2.82 us (3%)
    ppermute x10, starting transfers between devices, with_halo(): lax.ppermute(tail, axis, [(i, (i + 1) % count) for i in range(ends)])  32.6 us
    ppermute x10, waiting for transfers between devices, with_halo(): lax.ppermute(head, axis, [((i + 1) % count, i) for i in range(ends)])  28.3 us
    ppermute x10, starting transfers between devices, with_halo(): lax.ppermute(head, axis, [((i + 1) % count, i) for i in range(ends)])  22.3 us
    mul x1, other arithmetic, per_device(): lookup_stiffness(material, stiff_table) * (1 - eroded).astype(jnp.float32)  6.19 us
    add x4, other arithmetic, per_device(): displacement = displacement + rate * velocity  5.24 us
    concatenate x9, other arithmetic, with_halo(): jnp.concatenate([lax.ppermute(tail, axis, [(i, (i + 1) % count) for i in...  3.69 us
  transfers between devices with their start and end apart: 20, of which 12 were waited for; matrix products, arithmetic and copies ran while one was open for 9% of the time, Pallas kernels for 0%

commit v1 on v0

v1 whole, which is shorter than its diff:
```python
import functools

import jax
import jax.numpy as jnp
from jax import lax
from jax.experimental import pallas as pl
from jax.experimental.pallas import tpu as pltpu
from jax.sharding import PartitionSpec as P

SUBSTEPS = 4
COARSE = 0.5
FINE = COARSE / SUBSTEPS
DRAG = 0.2
TILE = 8
AXES = ("slab", "plane")

VMEM = pl.BlockSpec(memory_space=pltpu.VMEM)
HBM = pl.BlockSpec(memory_space=pltpu.HBM)
SMALL = pltpu.CompilerParams(vmem_limit_bytes=2 << 20)


def partner(index, count, second):
    other = ((index - 1) ^ 1) + 1 if second else index ^ 1
    return other if 0 <= other < count and (index or not second) else None


def swap_pairs(slabs, planes, along_slab, second):
    pairs = []
    for s in range(slabs):
        for p in range(planes):
            if along_slab:
                other = partner(s, slabs, second)
                target = (other, p) if other is not None else (s, p ^ 1 if (p ^ 1) < planes else None)
            else:
                other = partner(p, planes, second)
                rest = planes - 1 - p if planes % 2 == 0 else None
                target = (s, other if other is not None else rest)
            if target[1] is not None and target != (s, p):
                pairs.append((s * planes + p, target[0] * planes + target[1]))
    return pairs


def has_partner(index, count, second):
    even = index % 2 == 0
    up = jnp.logical_not(even) if second else even
    return jnp.where(up, index + 1 < count, index > 0)


def pin(arrays, space):
    return [pltpu.with_memory_space_constraint(a, space) for a in arrays]


def call(kernel, shapes, arrays, aliases=None, in_hbm=(), dtypes=None, scratch=(), to_hbm=()):
    dtypes = dtypes or [jnp.float32] * len(shapes)
    out_shape = [pltpu.VMEM(s, t) for s, t in zip(shapes, dtypes)]
    out_shape += [pltpu.HBM(s, jnp.float32) for s in to_hbm]
    return pl.pallas_call(
        kernel,
        in_specs=[VMEM] * len(arrays) + [HBM] * len(in_hbm),
        out_specs=[VMEM] * len(shapes) + [HBM] * len(to_hbm),
        out_shape=out_shape,
        scratch_shapes=scratch,
        input_output_aliases=aliases or {},
        compiler_params=SMALL,
    )(*pin(arrays, pltpu.VMEM), *pin(in_hbm, pltpu.HBM))


def lookup(material, eroded, table):
    total = jnp.zeros(material.shape, jnp.float32)
    for index in range(table.shape[0]):
        total = jnp.where(material == index, table[index : index + 1, :], total)
    return total * (1 - eroded).astype(jnp.float32)


def layer(index, rows):
    return pl.ds(pl.multiple_of(index * rows, rows), rows)


def sides(cx):
    slab = lax.axis_index("slab")
    even = slab % 2 == 0
    return jnp.where(even, cx - 1, 0), jnp.where(even, 0, cx - 1)


def plane_even():
    return lax.axis_index("plane") % 2 == 0


def open_kernel(
    cx, cy, u_hbm, material_hbm, eroded_hbm, table_hbm, a, b, ya, yb, u, material, eroded, table, scalars, sems
):
    copies = [
        pltpu.make_async_copy(source, target, sems.at[i])
        for i, (source, target) in enumerate(
            ((table_hbm, scalars), (material_hbm, material), (eroded_hbm, eroded), (u_hbm, u))
        )
    ]
    for copy in copies:
        copy.start()
    copies[0].wait()
    for index in range(table.shape[0]):
        table[index : index + 1, :] = jnp.full((1, table.shape[1]), scalars[index], jnp.float32)
    for copy in copies[1:]:
        copy.wait()
    fa, fb = sides(cx)
    even = plane_even()
    for face, out in ((fa, a), (fb, b)):
        at = layer(face, cy)
        for c in range(3):
            out[c] = u[c, at, :]
        out[3] = lookup(material[at, :], eroded[at, :], table)
    for x in range(cx):
        top, end = slice(x * cy, x * cy + TILE), slice((x + 1) * cy - TILE, (x + 1) * cy)
        for c in range(4):
            if c < 3:
                first, last = u[c, top, :], u[c, end, :]
            else:
                first = lookup(material[top, :], eroded[top, :], table)
                last = lookup(material[end, :], eroded[end, :], table)
            put_rows(even, x, c, first, last, ya, yb)


def put_rows(even, x, c, first, last, ya, yb):
    first, last = first[0:1, :], last[TILE - 1 : TILE, :]
    ya[c, x : x + 1, :] = jnp.where(even, last, first)
    yb[c, x : x + 1, :] = jnp.where(even, first, last)


def advance(cx, cy, u, v, load, kx, ky, kz, rate, u_out, v_out):
    nz = u.shape[-1]

    def component(c, carry):
        here = u[c, 0:cy, :]
        below = None
        for x in range(cx):
            at = slice(x * cy, (x + 1) * cy)
            flux_y = ky[at, :] * (pltpu.roll(here, cy - 1, 0) - here)
            flux_z = kz[at, :] * (pltpu.roll(here, nz - 1, 1) - here)
            force = flux_y - pltpu.roll(flux_y, 1, 0)
            force = force + (flux_z - pltpu.roll(flux_z, 1, 1))
            if x < cx - 1:
                above = u[c, (x + 1) * cy : (x + 2) * cy, :]
                flux_x = kx[at, :] * (above - here)
                force = force + flux_x
            if x > 0:
                force = force - below
            r = rate[at, :]
            speed = v[c, at, :]
            speed = speed + r * (force + load[c, at, :] - DRAG * speed)
            v_out[c, at, :] = speed
            u_out[c, at, :] = here + r * speed
            if x < cx - 1:
                here, below = above, flux_x
        return carry

    lax.fori_loop(0, 3, component, 0)


def first_kernel(
    cx, cy, u, material, eroded, table, v_hbm, load_hbm, damaged_hbm,
    u_out, v_out, load, kx, ky, kz, coarse, fine, damaged, sems,
):
    copies = [
        pltpu.make_async_copy(source, target, sems.at[i])
        for i, (source, target) in enumerate(((damaged_hbm, damaged), (v_hbm, v_out), (load_hbm, load)))
    ]
    for copy in copies:
        copy.start()
    nz = u.shape[-1]
    row = lax.broadcasted_iota(jnp.int32, (cy, nz), 0)
    lane = lax.broadcasted_iota(jnp.int32, (cy, nz), 1)
    below = None
    for x in range(cx):
        at = slice(x * cy, (x + 1) * cy)
        k = lookup(material[at, :], eroded[at, :], table)
        ky[at, :] = jnp.where(row < cy - 1, jnp.minimum(k, pltpu.roll(k, cy - 1, 0)), 0.0)
        kz[at, :] = jnp.where(lane < nz - 1, jnp.minimum(k, pltpu.roll(k, nz - 1, 1)), 0.0)
        if x > 0:
            kx[(x - 1) * cy : x * cy, :] = jnp.minimum(below, k)
        below = k
    kx[(cx - 1) * cy : cx * cy, :] = jnp.zeros((cy, nz), jnp.float32)
    copies[0].wait()
    for x in range(cx):
        at = slice(x * cy, (x + 1) * cy)
        hit = damaged[at, :] == 1
        coarse[at, :] = jnp.where(hit, FINE, COARSE)
        fine[at, :] = jnp.where(hit, FINE, 0.0)
    for copy in copies[1:]:
        copy.wait()
    advance(cx, cy, u, v_out, load, kx, ky, kz, coarse, u_out, v_out)


def fix_face(at, u, rate, k, halo, u_new, v_new, send):
    r = rate[at, :]
    for c in range(3):
        push = r * (k * (halo[c] - u[c, at, :]))
        v_new[c, at, :] += push
        moved = u_new[c, at, :] + r * push
        u_new[c, at, :] = moved
        if send is not None:
            send[c] = moved


def fix_rows(cx, cy, u, rate, k_low, k_high, ya, yb, u_new, v_new):
    even = plane_even()
    for c in range(3):
        low = jnp.where(even, yb[c], ya[c])
        high = jnp.where(even, ya[c], yb[c])
        for x in range(cx):
            tile = slice(x * TILE, (x + 1) * TILE)
            for start, k, halo in ((x * cy, k_low, low), ((x + 1) * cy - TILE, k_high, high)):
                at = slice(start, start + TILE)
                r = rate[at, :]
                push = r * (k[tile, :] * (halo[x : x + 1, :] - u[c, at, :]))
                v_new[c, at, :] += push
                u_new[c, at, :] += r * push


def pack_rows(cx, cy, u_new, ya_send, yb_send):
    even = plane_even()
    for c in range(3):
        for x in range(cx):
            first = u_new[c, x * cy : x * cy + TILE, :]
            last = u_new[c, (x + 1) * cy - TILE : (x + 1) * cy, :]
            put_rows(even, x, c, first, last, ya_send, yb_send)


def flag(axis, second):
    return has_partner(lax.axis_index(axis), lax.axis_size(axis), second).astype(jnp.float32)


def face_stiffness(sent, received, second):
    return jnp.minimum(sent[3], received[3]) * flag("slab", second)


def row_stiffness(cx, ya_sent, yb_sent, ya, yb, k_low, k_high):
    even = plane_even()
    k_a = jnp.minimum(ya_sent[3], ya[3]) * flag("plane", False)
    k_b = jnp.minimum(yb_sent[3], yb[3]) * flag("plane", True)
    low, high = jnp.where(even, k_b, k_a), jnp.where(even, k_a, k_b)
    row = lax.broadcasted_iota(jnp.int32, (TILE, ya.shape[-1]), 0)
    for x in range(cx):
        tile = slice(x * TILE, (x + 1) * TILE)
        k_low[tile, :] = jnp.where(row == 0, low[x : x + 1, :], 0.0)
        k_high[tile, :] = jnp.where(row == TILE - 1, high[x : x + 1, :], 0.0)


def fix_a_first(
    cx, cy, u1, v1, u, rate, ha, ya, yb, a_sent, ya_sent, yb_sent, u_new, v_new, send, ka, k_low, k_high
):
    at = layer(sides(cx)[0], cy)
    row_stiffness(cx, ya_sent, yb_sent, ya, yb, k_low, k_high)
    fix_rows(cx, cy, u, rate, k_low, k_high, ya, yb, u_new, v_new)
    k = face_stiffness(a_sent, ha, False)
    ka[...] = k
    fix_face(at, u, rate, k, ha, u_new, v_new, send)


def fix_b_first(cx, cy, u1, v1, u, rate, hb, b_sent, u_new, v_new, send, ya_send, yb_send, kb):
    at = layer(sides(cx)[1], cy)
    k = face_stiffness(b_sent, hb, True)
    kb[...] = k
    fix_face(at, u, rate, k, hb, u_new, v_new, send)
    pack_rows(cx, cy, u_new, ya_send, yb_send)


def fix_a(cx, cy, u1, v1, u, rate, ha, ya, yb, ka, k_low, k_high, u_new, v_new, send):
    fix_rows(cx, cy, u, rate, k_low, k_high, ya, yb, u_new, v_new)
    fix_face(layer(sides(cx)[0], cy), u, rate, ka[...], ha, u_new, v_new, send)


def fix_b(cx, cy, u1, v1, u, rate, hb, kb, u_new, v_new, send, ya_send, yb_send):
    fix_face(layer(sides(cx)[1], cy), u, rate, kb[...], hb, u_new, v_new, send)
    pack_rows(cx, cy, u_new, ya_send, yb_send)


def last_kernel(cx, cy, u1, v1, u, rate, ha, hb, ya, yb, ka, kb, k_low, k_high, u_new, v_new, u_out, v_out, sems):
    fix_rows(cx, cy, u, rate, k_low, k_high, ya, yb, u_new, v_new)
    fa, fb = sides(cx)
    fix_face(layer(fa, cy), u, rate, ka[...], ha, u_new, v_new, None)
    fix_face(layer(fb, cy), u, rate, kb[...], hb, u_new, v_new, None)
    copies = [
        pltpu.make_async_copy(u_new, u_out, sems.at[0]),
        pltpu.make_async_copy(v_new, v_out, sems.at[1]),
    ]
    for copy in copies:
        copy.start()
    for copy in copies:
        copy.wait()


def per_device(displacement, velocity, body_load, damaged, eroded, material, stiff_table):
    _, cx, cy, nz = displacement.shape
    rows = cx * cy
    slabs, planes = lax.axis_size("slab"), lax.axis_size("plane")
    xa = swap_pairs(slabs, planes, True, False)
    xb = swap_pairs(slabs, planes, True, True)
    pa = swap_pairs(slabs, planes, False, False)
    pb = swap_pairs(slabs, planes, False, True)

    field, face, side, cells = (3, rows, nz), (3, cy, nz), (3, cx, nz), (rows, nz)
    u = displacement.reshape(field)
    v = velocity.reshape(field)
    load = body_load.reshape(field)
    damaged, eroded, material = (a.reshape(cells) for a in (damaged, eroded, material))

    def bind(kernel):
        return functools.partial(kernel, cx, cy)

    table_shape = (stiff_table.shape[0], nz)
    a, b, ya, yb, u, material, eroded, table = call(
        bind(open_kernel),
        [(4, cy, nz)] * 2 + [(4, cx, nz)] * 2 + [field, cells, cells, table_shape],
        (),
        in_hbm=(u, material, eroded, stiff_table),
        dtypes=[jnp.float32] * 5 + [jnp.int32] * 2 + [jnp.float32],
        scratch=[pltpu.SMEM(stiff_table.shape, jnp.float32), pltpu.SemaphoreType.DMA((4,))],
    )
    for sub in range(SUBSTEPS):
        ha = lax.ppermute(a, AXES, xa)
        hb = lax.ppermute(b, AXES, xb)
        hya = lax.ppermute(ya, AXES, pa)
        hyb = lax.ppermute(yb, AXES, pb)
        if sub == 0:
            u_new, v, load, kx, ky, kz, coarse, fine = call(
                bind(first_kernel),
                [field] * 3 + [cells] * 5,
                (u, material, eroded, table),
                in_hbm=(v, load, damaged),
                scratch=[pltpu.VMEM(cells, jnp.int32), pltpu.SemaphoreType.DMA((3,))],
            )
            u_new, v, a_next, ka, k_low, k_high = call(
                bind(fix_a_first),
                [field, field, face, (cy, nz), (cx * TILE, nz), (cx * TILE, nz)],
                (u_new, v, u, coarse, ha, hya, hyb, a, ya, yb),
                {0: 0, 1: 1},
            )
            u_new, v, b, ya, yb, kb = call(
                bind(fix_b_first),
                [field, field, face, side, side, (cy, nz)],
                (u_new, v, u, coarse, hb, b),
                {0: 0, 1: 1},
            )
            a = a_next
        else:
            u_new, v = call(bind(advance), [field, field], (u, v, load, kx, ky, kz, fine), {1: 1})
            if sub < SUBSTEPS - 1:
                u_new, v, a = call(
                    bind(fix_a),
                    [field, field, face],
                    (u_new, v, u, fine, ha, hya, hyb, ka, k_low, k_high),
                    {0: 0, 1: 1},
                )
                u_new, v, b, ya, yb = call(
                    bind(fix_b),
                    [field, field, face, side, side],
                    (u_new, v, u, fine, hb, kb),
                    {0: 0, 1: 1},
                )
        if sub < SUBSTEPS - 1:
            u = u_new
    out = call(
        bind(last_kernel),
        [field, field],
        (u_new, v, u, fine, ha, hb, hya, hyb, ka, kb, k_low, k_high),
        {0: 0, 1: 1},
        scratch=[pltpu.SemaphoreType.DMA((2,))],
        to_hbm=[field, field],
    )
    return out[2].reshape(displacement.shape), out[3].reshape(displacement.shape)


def solution(mesh):
    field, cells = P(None, "slab", "plane", None), P("slab", "plane", None)
    return jax.shard_map(
        per_device,
        mesh=mesh,
        in_specs=(field, field, field, cells, cells, cells, P()),
        out_specs=(field, field),
        check_vma=False,
    )
```

time: 104 us -> 34.3 us (0.33)
  the two profiles are of different devices: /device:TPU:3 before, /device:TPU:0 now
where the time goes in v1:
time: 34.3 us; the launch traced here: 34.2 us
  starting transfers between devices  19.2 us (56%)
  Pallas kernels  9.18 us (27%)
  waiting for transfers between devices  5.01 us (15%)
  between operations  0.76 us (2%)
    ppermute x4, starting transfers between devices, per_device(): ha = lax.ppermute(a, AXES, xa)  12.2 us
    pallas_call x12, Pallas kernels, call(): pl.pallas_call(kernel, in_specs=[VMEM] * len(arrays) + [HBM] * len(in_hbm...  9.18 us
    ppermute x4, starting transfers between devices, per_device(): hyb = lax.ppermute(yb, AXES, pb)  5.37 us
    ppermute x4, waiting for transfers between devices, per_device(): ha = lax.ppermute(a, AXES, xa)  2.69 us
    ppermute x4, waiting for transfers between devices, per_device(): hyb = lax.ppermute(yb, AXES, pb)  2.3 us
    ppermute x4, starting transfers between devices, per_device(): hya = lax.ppermute(ya, AXES, pa)  1.23 us
  transfers between devices with their start and end apart: 16, of which 6 were waited for; matrix products, arithmetic and copies ran while one was open for 0% of the time, Pallas kernels for 18%

profile of v1, /device:TPU:0, one launch (start us, length us, event | category | flops | bytes accessed | tf_op | source)
XLA Modules:
  0.0 34.2 jit_solution(8960600079626967800)
XLA Ops:
  0.6 1.5 %shard_map.86 = (f32[4,32,256]{2,1,0:T(8,128)S(1)}, f32[4,32,256]{2,1,0:T(8,128)S(1)}, f32[4,8,256]{2,1,0:T(8,128)S(1)}, f32[4,8,256]{2,1,0:T(8,128)S(1)}, f32[3...) custom-call(f32[3,256,256]{2,1,0:T(8,128)} %bitcast.8, ...), custom_call_target="tpu_custom_call" | custom-call | tf_op jit(solution)/shard_map/pallas_call | solution.py:57
  2.2 3.0 %collective-permute-start = (f32[4,32,256]{2,1,0:T(8,128)S(1)}, f32[4,32,256]{2,1,0:T(8,128)S(1)}, u32[]{:S(2)}, u32[]{:S(2)}) collective-permute-start(f32[4,32,256]{2,1,0:T(8,128)S(1)} %get-tuple-element.61.a_sent), channel_id=1, source_target_pairs={{0,4},{1,5},{2,6},{3,7},{4,0},{5,1},{6,2},{7,3},{8,12},{9,13},{10,... | collective-permute-start | bytes 393224 | tf_op jit(solution)/shard_map/ppermute | solution.py:320
  5.2 0.0 collective-permute-start.3
  5.2 0.5 %collective-permute-start.1 = (f32[4,8,256]{2,1,0:T(8,128)S(1)}, f32[4,8,256]{2,1,0:T(8,128)S(1)}, u32[]{:S(2)}, u32[]{:S(2)}) collective-permute-start(f32[4,8,256]{2,1,0:T(8,128)S(1)} %get-tuple-element.62.ya_sent), channel_id=1, source_target_pairs={{0,1},{1,0},{2,3},{3,2},{4,5},{5,4},{6,7},{7,6},{8,9},{9,8},{10,11... | collective-permute-start | bytes 98312 | tf_op jit(solution)/shard_map/ppermute | solution.py:322
  5.7 1.1 %collective-permute-start.2 = (f32[4,8,256]{2,1,0:T(8,128)S(1)}, f32[4,8,256]{2,1,0:T(8,128)S(1)}, u32[]{:S(2)}, u32[]{:S(2)}) collective-permute-start(f32[4,8,256]{2,1,0:T(8,128)S(1)} %get-tuple-element.63.yb_sent), channel_id=1, source_target_pairs={{0,3},{1,2},{2,1},{3,0},{4,7},{5,6},{6,5},{7,4},{8,11},{9,10},{10,... | collective-permute-start | bytes 98312 | tf_op jit(solution)/shard_map/ppermute | solution.py:323
  6.8 2.5 %shard_map.87 = (f32[3,256,256]{2,1,0:T(8,128)S(1)}, f32[3,256,256]{2,1,0:T(8,128)S(1)}, f32[3,256,256]{2,1,0:T(8,128)S(1)}, f32[256,256]{1,0:T(8,128)S(1)}, f32...) custom-call(f32[3,256,256]{2,1,0:T(8,128)S(1)} %get-tuple-element.54.u, ...), custom_call_target="tpu_custom_call" | custom-call | tf_op jit(solution)/shard_map/pallas_call | solution.py:57
  9.4 0.0 collective-permute-done.1.ya
  9.4 0.0 collective-permute-done.2.yb
  9.4 1.4 %collective-permute-done.ha = f32[4,32,256]{2,1,0:T(8,128)S(1)} collective-permute-done((f32[4,32,256]{2,1,0:T(8,128)S(1)}, f32[4,32,256]{2,1,0:T(8,128)S(1)}, u32[]{:S(2)}, u32[]{:S(2)}) %collective-permute-start) | collective-permute-done | bytes 131104 | tf_op jit(solution)/shard_map/ppermute | solution.py:320
  10.8 0.2 shard_map.88
  10.9 2.5 %collective-permute-start.4 = (f32[3,32,256]{2,1,0:T(8,128)S(1)}, f32[3,32,256]{2,1,0:T(8,128)S(1)}, u32[]{:S(2)}, u32[]{:S(2)}) collective-permute-start(f32[3,32,256]{2,1,0:T(8,128)S(1)} %get-tuple-element.76), channel_id=1, source_target_pairs={{0,4},{1,5},{2,6},{3,7},{4,0},{5,1},{6,2},{7,3},{8,12},{9,13},{10,... | collective-permute-start | bytes 294920 | tf_op jit(solution)/shard_map/ppermute | solution.py:320
  13.5 0.0 collective-permute-done.3.hb
  13.5 0.1 shard_map.89
  13.6 0.1 collective-permute-start.7
  13.7 0.5 %collective-permute-start.5 = (f32[3,8,256]{2,1,0:T(8,128)S(1)}, f32[3,8,256]{2,1,0:T(8,128)S(1)}, u32[]{:S(2)}, u32[]{:S(2)}) collective-permute-start(f32[3,8,256]{2,1,0:T(8,128)S(1)} %get-tuple-element.77), channel_id=1, source_target_pairs={{0,1},{1,0},{2,3},{3,2},{4,5},{5,4},{6,7},{7,6},{8,9},{9,8},{10,11... | collective-permute-start | bytes 73736 | tf_op jit(solution)/shard_map/ppermute | solution.py:322
  14.2 1.2 %collective-permute-start.6 = (f32[3,8,256]{2,1,0:T(8,128)S(1)}, f32[3,8,256]{2,1,0:T(8,128)S(1)}, u32[]{:S(2)}, u32[]{:S(2)}) collective-permute-start(f32[3,8,256]{2,1,0:T(8,128)S(1)} %get-tuple-element.78), channel_id=1, source_target_pairs={{0,3},{1,2},{2,1},{3,0},{4,7},{5,6},{6,5},{7,4},{8,11},{9,10},{10,... | collective-permute-start | bytes 73736 | tf_op jit(solution)/shard_map/ppermute | solution.py:323
  15.4 1.0 %shard_map.90 = (f32[3,256,256]{2,1,0:T(8,128)S(1)}, f32[3,256,256]{2,1,0:T(8,128)S(1)}) custom-call(f32[3,256,256]{2,1,0:T(8,128)S(1)} %get-tuple-element.67.u, f32[3,256,256]{2,1,0:T(8,128)S(1)} %get-tuple-element.68.v, f32[3,256,256]{2,1,0:T(8,128)S(1)} %get-tuple-element.69.load, ...), custom_call_target="tpu_custom_call", output_to_operand_aliasing={{1}: (1, {})} | custom-call | tf_op jit(solution)/shard_map/pallas_call | solution.py:57
  16.4 0.0 collective-permute-done.5.ya
  16.4 1.0 %collective-permute-done.6.yb = f32[3,8,256]{2,1,0:T(8,128)S(1)} collective-permute-done((f32[3,8,256]{2,1,0:T(8,128)S(1)}, f32[3,8,256]{2,1,0:T(8,128)S(1)}, u32[]{:S(2)}, u32[]{:S(2)}) %collective-permute-start.6) | collective-permute-done | bytes 24608 | tf_op jit(solution)/shard_map/ppermute | solution.py:323
  17.4 0.0 collective-permute-done.4.ha
  17.4 0.2 shard_map.91
  17.6 2.6 %collective-permute-start.8 = (f32[3,32,256]{2,1,0:T(8,128)S(1)}, f32[3,32,256]{2,1,0:T(8,128)S(1)}, u32[]{:S(2)}, u32[]{:S(2)}) collective-permute-start(f32[3,32,256]{2,1,0:T(8,128)S(1)} %get-tuple-element.90), channel_id=1, source_target_pairs={{0,4},{1,5},{2,6},{3,7},{4,0},{5,1},{6,2},{7,3},{8,12},{9,13},{10,... | collective-permute-start | bytes 294920 | tf_op jit(solution)/shard_map/ppermute | solution.py:320
  20.2 0.0 collective-permute-done.7.hb
  20.2 0.1 shard_map.92
  20.3 0.3 collective-permute-start.11
  20.6 1.4 %collective-permute-start.10 = (f32[3,8,256]{2,1,0:T(8,128)S(1)}, f32[3,8,256]{2,1,0:T(8,128)S(1)}, u32[]{:S(2)}, u32[]{:S(2)}) collective-permute-start(f32[3,8,256]{2,1,0:T(8,128)S(1)} %get-tuple-element.92), channel_id=1, source_target_pairs={{0,3},{1,2},{2,1},{3,0},{4,7},{5,6},{6,5},{7,4},{8,11},{9,10},{10,... | collective-permute-start | bytes 73736 | tf_op jit(solution)/shard_map/ppermute | solution.py:323
  22.0 0.2 collective-permute-start.9
  22.2 1.0 %shard_map.93 = (f32[3,256,256]{2,1,0:T(8,128)S(1)}, f32[3,256,256]{2,1,0:T(8,128)S(1)}) custom-call(f32[3,256,256]{2,1,0:T(8,128)S(1)} %get-tuple-element.86.u, f32[3,256,256]{2,1,0:T(8,128)S(1)} %get-tuple-element.87.v, f32[3,256,256]{2,1,0:T(8,128)S(1)} %get-tuple-element.69.load, ...), custom_call_target="tpu_custom_call", output_to_operand_aliasing={{1}: (1, {})} | custom-call | tf_op jit(solution)/shard_map/pallas_call | solution.py:57
  23.2 0.6 %collective-permute-done.10.yb = f32[3,8,256]{2,1,0:T(8,128)S(1)} collective-permute-done((f32[3,8,256]{2,1,0:T(8,128)S(1)}, f32[3,8,256]{2,1,0:T(8,128)S(1)}, u32[]{:S(2)}, u32[]{:S(2)}) %collective-permute-start.10) | collective-permute-done | bytes 24608 | tf_op jit(solution)/shard_map/ppermute | solution.py:323
  23.8 0.0 collective-permute-done.9.ya
  23.8 1.2 %collective-permute-done.8.ha = f32[3,32,256]{2,1,0:T(8,128)S(1)} collective-permute-done((f32[3,32,256]{2,1,0:T(8,128)S(1)}, f32[3,32,256]{2,1,0:T(8,128)S(1)}, u32[]{:S(2)}, u32[]{:S(2)}) %collective-permute-start.8) | collective-permute-done | bytes 98336 | tf_op jit(solution)/shard_map/ppermute | solution.py:320
  25.0 0.2 shard_map.94
  25.2 0.0 collective-permute-done.11.hb
  25.2 0.1 shard_map.95
  25.3 0.1 collective-permute-start.13
  25.4 4.0 %collective-permute-start.12 = (f32[3,32,256]{2,1,0:T(8,128)S(1)}, f32[3,32,256]{2,1,0:T(8,128)S(1)}, u32[]{:S(2)}, u32[]{:S(2)}) collective-permute-start(f32[3,32,256]{2,1,0:T(8,128)S(1)} %get-tuple-element.100), channel_id=1, source_target_pairs={{0,4},{1,5},{2,6},{3,7},{4,0},{5,1},{6,2},{7,3},{8,12},{9,13},{10,... | collective-permute-start | bytes 294920 | tf_op jit(solution)/shard_map/ppermute | solution.py:320
  29.4 0.0 collective-permute-start.14
  29.4 1.6 %collective-permute-start.15 = (f32[3,8,256]{2,1,0:T(8,128)S(1)}, f32[3,8,256]{2,1,0:T(8,128)S(1)}, u32[]{:S(2)}, u32[]{:S(2)}) collective-permute-start(f32[3,8,256]{2,1,0:T(8,128)S(1)} %get-tuple-element.103), channel_id=1, source_target_pairs={{0,3},{1,2},{2,1},{3,0},{4,7},{5,6},{6,5},{7,4},{8,11},{9,10},{10,... | collective-permute-start | bytes 73736 | tf_op jit(solution)/shard_map/ppermute | solution.py:323
  31.0 1.0 %shard_map.96 = (f32[3,256,256]{2,1,0:T(8,128)S(1)}, f32[3,256,256]{2,1,0:T(8,128)S(1)}) custom-call(f32[3,256,256]{2,1,0:T(8,128)S(1)} %get-tuple-element.96.u, f32[3,256,256]{2,1,0:T(8,128)S(1)} %get-tuple-element.97.v, f32[3,256,256]{2,1,0:T(8,128)S(1)} %get-tuple-element.69.load, ...), custom_call_target="tpu_custom_call", output_to_operand_aliasing={{1}: (1, {})} | custom-call | tf_op jit(solution)/shard_map/pallas_call | solution.py:57
  32.0 0.0 collective-permute-done.14.ya
  32.0 0.6 %collective-permute-done.15.yb = f32[3,8,256]{2,1,0:T(8,128)S(1)} collective-permute-done((f32[3,8,256]{2,1,0:T(8,128)S(1)}, f32[3,8,256]{2,1,0:T(8,128)S(1)}, u32[]{:S(2)}, u32[]{:S(2)}) %collective-permute-start.15) | collective-permute-done | bytes 24608 | tf_op jit(solution)/shard_map/ppermute | solution.py:323
  32.7 0.0 collective-permute-done.13.hb
  32.7 0.1 collective-permute-done.12.ha
  32.8 1.3 %shard_map.97 = (f32[3,256,256]{2,1,0:T(8,128)S(1)}, f32[3,256,256]{2,1,0:T(8,128)S(1)}, f32[3,256,256]{2,1,0:T(8,128)}, f32[3,256,256]{2,1,0:T(8,128)}) custom-call(f32[3,256,256]{2,1,0:T(8,128)S(1)} %get-tuple-element.98.u1, f32[3,256,256]{2,1,0:T(8,128)S(1)} %get-tuple-element.99.v1, ...), custom_call_target="tpu_custom_call", output_to_operand_aliasing={{0}: (0, {}), {1}: (1, {})} | custom-call | tf_op jit(solution)/shard_map/pallas_call | solution.py:57
Async XLA Ops:
  2.2 8.6 %collective-permute-start = (f32[4,32,256]{2,1,0:T(8,128)S(1)}, f32[4,32,256]{2,1,0:T(8,128)S(1)}, u32[]{:S(2)}, u32[]{:S(2)}) collective-permute-start(f32[4,32,256]{2,1,0:T(8,128)S(1)} %get-tuple-element.61.a_sent), channel_id=1, source_target_pairs={{0,4},{1,5},{2,6},{3,7},{4,0},{5,1},{6,2},{7,3},{8,12},{9,13},{10,... | collective-permute-start | bytes 393224 | tf_op jit(solution)/shard_map/ppermute | solution.py:320
  5.2 8.3 %collective-permute-start.3 = (f32[4,32,256]{2,1,0:T(8,128)S(1)}, f32[4,32,256]{2,1,0:T(8,128)S(1)}, u32[]{:S(2)}, u32[]{:S(2)}) collective-permute-start(f32[4,32,256]{2,1,0:T(8,128)S(1)} %get-tuple-element.66.b_sent), channel_id=1, source_target_pairs={{0,1},{1,0},{2,3},{3,2},{4,8},{5,9},{6,10},{7,11},{8,4},{9,5},{10,... | collective-permute-start | bytes 393224 | tf_op jit(solution)/shard_map/ppermute | solution.py:321
  5.2 4.2 %collective-permute-start.1 = (f32[4,8,256]{2,1,0:T(8,128)S(1)}, f32[4,8,256]{2,1,0:T(8,128)S(1)}, u32[]{:S(2)}, u32[]{:S(2)}) collective-permute-start(f32[4,8,256]{2,1,0:T(8,128)S(1)} %get-tuple-element.62.ya_sent), channel_id=1, source_target_pairs={{0,1},{1,0},{2,3},{3,2},{4,5},{5,4},{6,7},{7,6},{8,9},{9,8},{10,11... | collective-permute-start | bytes 98312 | tf_op jit(solution)/shard_map/ppermute | solution.py:322
  5.7 3.7 %collective-permute-start.2 = (f32[4,8,256]{2,1,0:T(8,128)S(1)}, f32[4,8,256]{2,1,0:T(8,128)S(1)}, u32[]{:S(2)}, u32[]{:S(2)}) collective-permute-start(f32[4,8,256]{2,1,0:T(8,128)S(1)} %get-tuple-element.63.yb_sent), channel_id=1, source_target_pairs={{0,3},{1,2},{2,1},{3,0},{4,7},{5,6},{6,5},{7,4},{8,11},{9,10},{10,... | collective-permute-start | bytes 98312 | tf_op jit(solution)/shard_map/ppermute | solution.py:323
  10.9 6.5 %collective-permute-start.4 = (f32[3,32,256]{2,1,0:T(8,128)S(1)}, f32[3,32,256]{2,1,0:T(8,128)S(1)}, u32[]{:S(2)}, u32[]{:S(2)}) collective-permute-start(f32[3,32,256]{2,1,0:T(8,128)S(1)} %get-tuple-element.76), channel_id=1, source_target_pairs={{0,4},{1,5},{2,6},{3,7},{4,0},{5,1},{6,2},{7,3},{8,12},{9,13},{10,... | collective-permute-start | bytes 294920 | tf_op jit(solution)/shard_map/ppermute | solution.py:320
  13.6 6.6 %collective-permute-start.7 = (f32[3,32,256]{2,1,0:T(8,128)S(1)}, f32[3,32,256]{2,1,0:T(8,128)S(1)}, u32[]{:S(2)}, u32[]{:S(2)}) collective-permute-start(f32[3,32,256]{2,1,0:T(8,128)S(1)} %get-tuple-element.84), channel_id=1, source_target_pairs={{0,1},{1,0},{2,3},{3,2},{4,8},{5,9},{6,10},{7,11},{8,4},{9,5},{10,... | collective-permute-start | bytes 294920 | tf_op jit(solution)/shard_map/ppermute | solution.py:321
  13.7 2.7 %collective-permute-start.5 = (f32[3,8,256]{2,1,0:T(8,128)S(1)}, f32[3,8,256]{2,1,0:T(8,128)S(1)}, u32[]{:S(2)}, u32[]{:S(2)}) collective-permute-start(f32[3,8,256]{2,1,0:T(8,128)S(1)} %get-tuple-element.77), channel_id=1, source_target_pairs={{0,1},{1,0},{2,3},{3,2},{4,5},{5,4},{6,7},{7,6},{8,9},{9,8},{10,11... | collective-permute-start | bytes 73736 | tf_op jit(solution)/shard_map/ppermute | solution.py:322
  14.2 3.3 %collective-permute-start.6 = (f32[3,8,256]{2,1,0:T(8,128)S(1)}, f32[3,8,256]{2,1,0:T(8,128)S(1)}, u32[]{:S(2)}, u32[]{:S(2)}) collective-permute-start(f32[3,8,256]{2,1,0:T(8,128)S(1)} %get-tuple-element.78), channel_id=1, source_target_pairs={{0,3},{1,2},{2,1},{3,0},{4,7},{5,6},{6,5},{7,4},{8,11},{9,10},{10,... | collective-permute-start | bytes 73736 | tf_op jit(solution)/shard_map/ppermute | solution.py:323
  17.6 7.4 %collective-permute-start.8 = (f32[3,32,256]{2,1,0:T(8,128)S(1)}, f32[3,32,256]{2,1,0:T(8,128)S(1)}, u32[]{:S(2)}, u32[]{:S(2)}) collective-permute-start(f32[3,32,256]{2,1,0:T(8,128)S(1)} %get-tuple-element.90), channel_id=1, source_target_pairs={{0,4},{1,5},{2,6},{3,7},{4,0},{5,1},{6,2},{7,3},{8,12},{9,13},{10,... | collective-permute-start | bytes 294920 | tf_op jit(solution)/shard_map/ppermute | solution.py:320
  20.3 4.9 %collective-permute-start.11 = (f32[3,32,256]{2,1,0:T(8,128)S(1)}, f32[3,32,256]{2,1,0:T(8,128)S(1)}, u32[]{:S(2)}, u32[]{:S(2)}) collective-permute-start(f32[3,32,256]{2,1,0:T(8,128)S(1)} %get-tuple-element.95), channel_id=1, source_target_pairs={{0,1},{1,0},{2,3},{3,2},{4,8},{5,9},{6,10},{7,11},{8,4},{9,5},{10,... | collective-permute-start | bytes 294920 | tf_op jit(solution)/shard_map/ppermute | solution.py:321
  20.6 3.3 %collective-permute-start.10 = (f32[3,8,256]{2,1,0:T(8,128)S(1)}, f32[3,8,256]{2,1,0:T(8,128)S(1)}, u32[]{:S(2)}, u32[]{:S(2)}) collective-permute-start(f32[3,8,256]{2,1,0:T(8,128)S(1)} %get-tuple-element.92), channel_id=1, source_target_pairs={{0,3},{1,2},{2,1},{3,0},{4,7},{5,6},{6,5},{7,4},{8,11},{9,10},{10,... | collective-permute-start | bytes 73736 | tf_op jit(solution)/shard_map/ppermute | solution.py:323
  22.0 1.8 %collective-permute-start.9 = (f32[3,8,256]{2,1,0:T(8,128)S(1)}, f32[3,8,256]{2,1,0:T(8,128)S(1)}, u32[]{:S(2)}, u32[]{:S(2)}) collective-permute-start(f32[3,8,256]{2,1,0:T(8,128)S(1)} %get-tuple-element.91), channel_id=1, source_target_pairs={{0,1},{1,0},{2,3},{3,2},{4,5},{5,4},{6,7},{7,6},{8,9},{9,8},{10,11... | collective-permute-start | bytes 73736 | tf_op jit(solution)/shard_map/ppermute | solution.py:322
  25.3 7.4 %collective-permute-start.13 = (f32[3,32,256]{2,1,0:T(8,128)S(1)}, f32[3,32,256]{2,1,0:T(8,128)S(1)}, u32[]{:S(2)}, u32[]{:S(2)}) collective-permute-start(f32[3,32,256]{2,1,0:T(8,128)S(1)} %get-tuple-element.101), channel_id=1, source_target_pairs={{0,1},{1,0},{2,3},{3,2},{4,8},{5,9},{6,10},{7,11},{8,4},{9,5},{10,... | collective-permute-start | bytes 294920 | tf_op jit(solution)/shard_map/ppermute | solution.py:321
  25.4 7.4 %collective-permute-start.12 = (f32[3,32,256]{2,1,0:T(8,128)S(1)}, f32[3,32,256]{2,1,0:T(8,128)S(1)}, u32[]{:S(2)}, u32[]{:S(2)}) collective-permute-start(f32[3,32,256]{2,1,0:T(8,128)S(1)} %get-tuple-element.100), channel_id=1, source_target_pairs={{0,4},{1,5},{2,6},{3,7},{4,0},{5,1},{6,2},{7,3},{8,12},{9,13},{10,... | collective-permute-start | bytes 294920 | tf_op jit(solution)/shard_map/ppermute | solution.py:320
  29.4 2.6 %collective-permute-start.14 = (f32[3,8,256]{2,1,0:T(8,128)S(1)}, f32[3,8,256]{2,1,0:T(8,128)S(1)}, u32[]{:S(2)}, u32[]{:S(2)}) collective-permute-start(f32[3,8,256]{2,1,0:T(8,128)S(1)} %get-tuple-element.102), channel_id=1, source_target_pairs={{0,1},{1,0},{2,3},{3,2},{4,5},{5,4},{6,7},{7,6},{8,9},{9,8},{10,11... | collective-permute-start | bytes 73736 | tf_op jit(solution)/shard_map/ppermute | solution.py:322
  29.4 3.3 %collective-permute-start.15 = (f32[3,8,256]{2,1,0:T(8,128)S(1)}, f32[3,8,256]{2,1,0:T(8,128)S(1)}, u32[]{:S(2)}, u32[]{:S(2)}) collective-permute-start(f32[3,8,256]{2,1,0:T(8,128)S(1)} %get-tuple-element.103), channel_id=1, source_target_pairs={{0,3},{1,2},{2,1},{3,0},{4,7},{5,6},{6,5},{7,4},{8,11},{9,10},{10,... | collective-permute-start | bytes 73736 | tf_op jit(solution)/shard_map/ppermute | solution.py:323

commit v2 on v1

--- a/solution.py
+++ b/solution.py
@@ -12,6 +12,7 @@
 FINE = COARSE / SUBSTEPS
 DRAG = 0.2
 TILE = 8
+LONG = 1 << 30
 AXES = ("slab", "plane")
 
 VMEM = pl.BlockSpec(memory_space=pltpu.VMEM)
@@ -50,7 +51,7 @@
     return [pltpu.with_memory_space_constraint(a, space) for a in arrays]
 
 
-def call(kernel, shapes, arrays, aliases=None, in_hbm=(), dtypes=None, scratch=(), to_hbm=()):
+def call(kernel, shapes, arrays, aliases=None, in_hbm=(), dtypes=None, scratch=(), to_hbm=(), weight=1):
     dtypes = dtypes or [jnp.float32] * len(shapes)
     out_shape = [pltpu.VMEM(s, t) for s, t in zip(shapes, dtypes)]
     out_shape += [pltpu.HBM(s, jnp.float32) for s in to_hbm]
@@ -62,6 +63,7 @@
         scratch_shapes=scratch,
         input_output_aliases=aliases or {},
         compiler_params=SMALL,
+        cost_estimate=pl.CostEstimate(flops=weight, bytes_accessed=weight, transcendentals=0),
     )(*pin(arrays, pltpu.VMEM), *pin(in_hbm, pltpu.HBM))
 
 
@@ -245,40 +247,47 @@
         k_high[tile, :] = jnp.where(row == TILE - 1, high[x : x + 1, :], 0.0)
 
 
-def fix_a_first(
-    cx, cy, u1, v1, u, rate, ha, ya, yb, a_sent, ya_sent, yb_sent, u_new, v_new, send, ka, k_low, k_high
+def fix_b_first(
+    cx, cy, u1, v1, u, rate, hb, ya, yb, b_sent, ya_sent, yb_sent, u_new, v_new, send, kb, k_low, k_high
 ):
-    at = layer(sides(cx)[0], cy)
     row_stiffness(cx, ya_sent, yb_sent, ya, yb, k_low, k_high)
     fix_rows(cx, cy, u, rate, k_low, k_high, ya, yb, u_new, v_new)
+    k = face_stiffness(b_sent, hb, True)
+    kb[...] = k
+    fix_face(layer(sides(cx)[1], cy), u, rate, k, hb, u_new, v_new, send)
+
+
+def fix_a_first(cx, cy, u1, v1, u, rate, ha, a_sent, u_new, v_new, send, ya_send, yb_send, ka):
     k = face_stiffness(a_sent, ha, False)
     ka[...] = k
-    fix_face(at, u, rate, k, ha, u_new, v_new, send)
-
-
-def fix_b_first(cx, cy, u1, v1, u, rate, hb, b_sent, u_new, v_new, send, ya_send, yb_send, kb):
-    at = layer(sides(cx)[1], cy)
-    k = face_stiffness(b_sent, hb, True)
-    kb[...] = k
-    fix_face(at, u, rate, k, hb, u_new, v_new, send)
+    fix_face(layer(sides(cx)[0], cy), u, rate, k, ha, u_new, v_new, send)
     pack_rows(cx, cy, u_new, ya_send, yb_send)
 
 
-def fix_a(cx, cy, u1, v1, u, rate, ha, ya, yb, ka, k_low, k_high, u_new, v_new, send):
+def fix_b(cx, cy, u1, v1, u, rate, hb, ya, yb, kb, k_low, k_high, u_new, v_new, send):
     fix_rows(cx, cy, u, rate, k_low, k_high, ya, yb, u_new, v_new)
+    fix_face(layer(sides(cx)[1], cy), u, rate, kb[...], hb, u_new, v_new, send)
+
+
+def fix_a(cx, cy, u1, v1, u, rate, ha, ka, u_new, v_new, send, ya_send, yb_send):
     fix_face(layer(sides(cx)[0], cy), u, rate, ka[...], ha, u_new, v_new, send)
-
-
-def fix_b(cx, cy, u1, v1, u, rate, hb, kb, u_new, v_new, send, ya_send, yb_send):
-    fix_face(layer(sides(cx)[1], cy), u, rate, kb[...], hb, u_new, v_new, send)
     pack_rows(cx, cy, u_new, ya_send, yb_send)
 
 
-def last_kernel(cx, cy, u1, v1, u, rate, ha, hb, ya, yb, ka, kb, k_low, k_high, u_new, v_new, u_out, v_out, sems):
-    fix_rows(cx, cy, u, rate, k_low, k_high, ya, yb, u_new, v_new)
-    fa, fb = sides(cx)
-    fix_face(layer(fa, cy), u, rate, ka[...], ha, u_new, v_new, None)
-    fix_face(layer(fb, cy), u, rate, kb[...], hb, u_new, v_new, None)
+def hand_on(*refs):
+    del refs
+
+
+def after(array, other):
+    return call(hand_on, [array.shape], (array, other), {0: 0})[0]
+
+
+def fix_b_last(cx, cy, u1, v1, u, rate, hb, ya, yb, kb, k_low, k_high, u_new, v_new):
+    fix_b(cx, cy, u1, v1, u, rate, hb, ya, yb, kb, k_low, k_high, u_new, v_new, None)
+
+
+def last_kernel(cx, cy, u1, v1, u, rate, ha, ka, u_new, v_new, u_out, v_out, sems):
+    fix_face(layer(sides(cx)[0], cy), u, rate, ka[...], ha, u_new, v_new, None)
     copies = [
         pltpu.make_async_copy(u_new, u_out, sems.at[0]),
         pltpu.make_async_copy(v_new, v_out, sems.at[1]),
@@ -317,10 +326,14 @@
         scratch=[pltpu.SMEM(stiff_table.shape, jnp.float32), pltpu.SemaphoreType.DMA((4,))],
     )
     for sub in range(SUBSTEPS):
+        hb = lax.ppermute(b, AXES, xb)
+        if sub == 0:
+            yb = after(yb, b)
+        hyb = lax.ppermute(yb, AXES, pb)
+        a = after(a, yb)
         ha = lax.ppermute(a, AXES, xa)
-        hb = lax.ppermute(b, AXES, xb)
+        ya = after(ya, a)
         hya = lax.ppermute(ya, AXES, pa)
-        hyb = lax.ppermute(yb, AXES, pb)
         if sub == 0:
             u_new, v, load, kx, ky, kz, coarse, fine = call(
                 bind(first_kernel),
@@ -329,40 +342,42 @@
                 in_hbm=(v, load, damaged),
                 scratch=[pltpu.VMEM(cells, jnp.int32), pltpu.SemaphoreType.DMA((3,))],
             )
-            u_new, v, a_next, ka, k_low, k_high = call(
+            u_new, v, b, kb, k_low, k_high = call(
+                bind(fix_b_first),
+                [field, field, face, (cy, nz), (cx * TILE, nz), (cx * TILE, nz)],
+                (u_new, v, u, coarse, hb, hya, hyb, b, ya, yb),
+                {0: 0, 1: 1}, weight=LONG,
+            )
+            u_new, v, a, ya, yb, ka = call(
                 bind(fix_a_first),
-                [field, field, face, (cy, nz), (cx * TILE, nz), (cx * TILE, nz)],
-                (u_new, v, u, coarse, ha, hya, hyb, a, ya, yb),
+                [field, field, face, side, side, (cy, nz)],
+                (u_new, v, u, coarse, ha, a),
                 {0: 0, 1: 1},
             )
-            u_new, v, b, ya, yb, kb = call(
-                bind(fix_b_first),
-                [field, field, face, side, side, (cy, nz)],
-                (u_new, v, u, coarse, hb, b),
-                {0: 0, 1: 1},
-            )
-            a = a_next
         else:
             u_new, v = call(bind(advance), [field, field], (u, v, load, kx, ky, kz, fine), {1: 1})
             if sub < SUBSTEPS - 1:
-                u_new, v, a = call(
+                u_new, v, b = call(
+                    bind(fix_b),
+                    [field, field, face],
+                    (u_new, v, u, fine, hb, hya, hyb, kb, k_low, k_high),
+                    {0: 0, 1: 1}, weight=LONG,
+                )
+                u_new, v, a, ya, yb = call(
                     bind(fix_a),
-                    [field, field, face],
-                    (u_new, v, u, fine, ha, hya, hyb, ka, k_low, k_high),
-                    {0: 0, 1: 1},
-                )
-                u_new, v, b, ya, yb = call(
-                    bind(fix_b),
                     [field, field, face, side, side],
-                    (u_new, v, u, fine, hb, kb),
+                    (u_new, v, u, fine, ha, ka),
                     {0: 0, 1: 1},
                 )
         if sub < SUBSTEPS - 1:
             u = u_new
+    u_new, v = call(
+        bind(fix_b_last), [field, field], (u_new, v, u, fine, hb, hya, hyb, kb, k_low, k_high), {0: 0, 1: 1}, weight=LONG
+    )
     out = call(
         bind(last_kernel),
         [field, field],
-        (u_new, v, u, fine, ha, hb, hya, hyb, ka, kb, k_low, k_high),
+        (u_new, v, u, fine, ha, ka),
         {0: 0, 1: 1},
         scratch=[pltpu.SemaphoreType.DMA((2,))],
         to_hbm=[field, field],

time: 34.3 us -> 32.6 us (0.950)
  starting transfers between devices: 19.2 us -> 16.3 us
  waiting for transfers between devices: 5.01 us -> 5.94 us
    ppermute x4, starting transfers between devices: 12.2 us -> 8.9 us  [per_device(): ha = lax.ppermute(a, AXES, xa)]
    ppermute x4, waiting for transfers between devices: 2.69 us -> 5.9 us  [per_device(): ha = lax.ppermute(a, AXES, xa)]
    ppermute x4, waiting for transfers between devices: 2.3 us -> 0.01 us  [per_device(): hyb = lax.ppermute(yb, AXES, pb)]
    ppermute x4, starting transfers between devices: 1.23 us -> 0.32 us  [per_device(): hya = lax.ppermute(ya, AXES, pa)]
    ppermute x4, starting transfers between devices: 5.37 us -> 6.14 us  [per_device(): hyb = lax.ppermute(yb, AXES, pb)]
    ppermute x4, starting transfers between devices: 0.44 us -> 0.96 us  [per_device(): hb = lax.ppermute(b, AXES, xb)]
    pallas_call x12 -> x22, Pallas kernels: 9.18 us -> 9.25 us  [call(): pl.pallas_call(kernel, in_specs=[VMEM] * len(arrays) + [HBM] * len(in_hbm...]
  transfers between devices with their start and end apart: 16 -> 16, of which waited for: 6 -> 4; matrix products, arithmetic and copies ran while one was open for 0% -> 0% of each run, Pallas kernels for 18% -> 20%
where the time goes in v2:
time: 32.6 us; the launch traced here: 32.4 us
  starting transfers between devices  16.3 us (50%)
  Pallas kernels  9.25 us (28%)
  waiting for transfers between devices  5.94 us (18%)
  between operations  0.88 us (3%)
    pallas_call x22, Pallas kernels, call(): pl.pallas_call(kernel, in_specs=[VMEM] * len(arrays) + [HBM] * len(in_hbm...  9.25 us
    ppermute x4, starting transfers between devices, per_device(): ha = lax.ppermute(a, AXES, xa)  8.9 us
    ppermute x4, starting transfers between devices, per_device(): hyb = lax.ppermute(yb, AXES, pb)  6.14 us
    ppermute x4, waiting for transfers between devices, per_device(): ha = lax.ppermute(a, AXES, xa)  5.9 us
    ppermute x4, starting transfers between devices, per_device(): hb = lax.ppermute(b, AXES, xb)  0.96 us
  transfers between devices with their start and end apart: 16, of which 4 were waited for; matrix products, arithmetic and copies ran while one was open for 0% of the time, Pallas kernels for 20%

profile of v2, /device:TPU:0, one launch (start us, length us, event | category | flops | bytes accessed | tf_op | source)
XLA Modules:
  0.0 32.4 jit_solution(13626048816227406445)
XLA Ops:
  0.6 1.5 %shard_map.86 = (f32[4,32,256]{2,1,0:T(8,128)S(1)}, f32[4,32,256]{2,1,0:T(8,128)S(1)}, f32[4,8,256]{2,1,0:T(8,128)S(1)}, f32[4,8,256]{2,1,0:T(8,128)S(1)}, f32[3...) custom-call(f32[3,256,256]{2,1,0:T(8,128)} %bitcast.8, ...), custom_call_target="tpu_custom_call" | custom-call | flops 1 | bytes 1 | tf_op jit(solution)/shard_map/pallas_call | solution.py:58
  2.2 0.5 %collective-permute-start = (f32[4,32,256]{2,1,0:T(8,128)S(1)}, f32[4,32,256]{2,1,0:T(8,128)S(1)}, u32[]{:S(2)}, u32[]{:S(2)}) collective-permute-start(f32[4,32,256]{2,1,0:T(8,128)S(1)} %get-tuple-element.63.refs_1_.b_sent), channel_id=1, source_target_pairs={{0,1},{1,0},{2,3},{3,2},{4,8},{5,9},{6,10},{7,11},{8,4},{9,5},{10,... | collective-permute-start | bytes 393224 | tf_op jit(solution)/shard_map/ppermute | solution.py:329
  2.7 0.1 collective-permute-start.1
  2.8 2.6 %collective-permute-start.2 = (f32[4,8,256]{2,1,0:T(8,128)S(1)}, f32[4,8,256]{2,1,0:T(8,128)S(1)}, u32[]{:S(2)}, u32[]{:S(2)}) collective-permute-start(f32[4,8,256]{2,1,0:T(8,128)S(1)} %shard_map.88.refs_1_.yb_sent), channel_id=1, source_target_pairs={{0,3},{1,2},{2,1},{3,0},{4,7},{5,6},{6,5},{7,4},{8,11},{9,10},{10,... | collective-permute-start | bytes 98312 | tf_op jit(solution)/shard_map/ppermute | solution.py:332
  5.4 2.9 %collective-permute-start.3 = (f32[4,32,256]{2,1,0:T(8,128)S(1)}, f32[4,32,256]{2,1,0:T(8,128)S(1)}, u32[]{:S(2)}, u32[]{:S(2)}) collective-permute-start(f32[4,32,256]{2,1,0:T(8,128)S(1)} %shard_map.89.refs_1_.a_sent), channel_id=1, source_target_pairs={{0,4},{1,5},{2,6},{3,7},{4,0},{5,1},{6,2},{7,3},{8,12},{9,13},{10,... | collective-permute-start | bytes 393224 | tf_op jit(solution)/shard_map/ppermute | solution.py:334
  8.4 2.5 %shard_map.87 = (f32[3,256,256]{2,1,0:T(8,128)S(1)}, f32[3,256,256]{2,1,0:T(8,128)S(1)}, f32[3,256,256]{2,1,0:T(8,128)S(1)}, f32[256,256]{1,0:T(8,128)S(1)}, f32...) custom-call(f32[3,256,256]{2,1,0:T(8,128)S(1)} %get-tuple-element.56.u, ...), custom_call_target="tpu_custom_call" | custom-call | flops 1 | bytes 1 | tf_op jit(solution)/shard_map/pallas_call | solution.py:58
  10.9 0.0 collective-permute-done.1.ya
  10.9 0.0 collective-permute-done.2.yb
  10.9 0.0 collective-permute-done.hb
  11.0 0.2 shard_map.91
  11.1 0.1 collective-permute-start.4
  11.2 0.8 %collective-permute-done.3.ha = f32[4,32,256]{2,1,0:T(8,128)S(1)} collective-permute-done((f32[4,32,256]{2,1,0:T(8,128)S(1)}, f32[4,32,256]{2,1,0:T(8,128)S(1)}, u32[]{:S(2)}, u32[]{:S(2)}) %collective-permute-start.3) | collective-permute-done | bytes 131104 | tf_op jit(solution)/shard_map/ppermute | solution.py:334
  12.0 0.1 shard_map.92
  12.2 0.1 collective-permute-start.5
  12.3 1.2 %collective-permute-start.6 = (f32[3,8,256]{2,1,0:T(8,128)S(1)}, f32[3,8,256]{2,1,0:T(8,128)S(1)}, u32[]{:S(2)}, u32[]{:S(2)}) collective-permute-start(f32[3,8,256]{2,1,0:T(8,128)S(1)} %get-tuple-element.81.refs_1_), channel_id=1, source_target_pairs={{0,3},{1,2},{2,1},{3,0},{4,7},{5,6},{6,5},{7,4},{8,11},{9,10},{10,... | collective-permute-start | bytes 73736 | tf_op jit(solution)/shard_map/ppermute | solution.py:332
  13.5 2.5 %collective-permute-start.7 = (f32[3,32,256]{2,1,0:T(8,128)S(1)}, f32[3,32,256]{2,1,0:T(8,128)S(1)}, u32[]{:S(2)}, u32[]{:S(2)}) collective-permute-start(f32[3,32,256]{2,1,0:T(8,128)S(1)} %shard_map.94.refs_1_), channel_id=1, source_target_pairs={{0,4},{1,5},{2,6},{3,7},{4,0},{5,1},{6,2},{7,3},{8,12},{9,13},{10,... | collective-permute-start | bytes 294920 | tf_op jit(solution)/shard_map/ppermute | solution.py:334
  16.0 1.0 %shard_map.93 = (f32[3,256,256]{2,1,0:T(8,128)S(1)}, f32[3,256,256]{2,1,0:T(8,128)S(1)}) custom-call(f32[3,256,256]{2,1,0:T(8,128)S(1)} %get-tuple-element.69.u, f32[3,256,256]{2,1,0:T(8,128)S(1)} %get-tuple-element.70.v, f32[3,256,256]{2,1,0:T(8,128)S(1)} %get-tuple-element.71.load, ...), custom_call_target="tpu_custom_call", output_to_operand_aliasing={{1}: (1, {})} | custom-call | flops 1 | bytes 1 | tf_op jit(solution)/shard_map/pallas_call | solution.py:58
  17.0 0.0 collective-permute-done.5.ya
  17.0 0.0 collective-permute-done.6.yb
  17.0 0.0 collective-permute-done.4.hb
  17.0 0.2 shard_map.96
  17.2 0.1 collective-permute-start.8
  17.3 1.7 %collective-permute-done.7.ha = f32[3,32,256]{2,1,0:T(8,128)S(1)} collective-permute-done((f32[3,32,256]{2,1,0:T(8,128)S(1)}, f32[3,32,256]{2,1,0:T(8,128)S(1)}, u32[]{:S(2)}, u32[]{:S(2)}) %collective-permute-start.7) | collective-permute-done | bytes 98336 | tf_op jit(solution)/shard_map/ppermute | solution.py:334
  19.0 0.1 shard_map.97
  19.1 0.1 collective-permute-start.9
  19.2 0.7 %collective-permute-start.10 = (f32[3,8,256]{2,1,0:T(8,128)S(1)}, f32[3,8,256]{2,1,0:T(8,128)S(1)}, u32[]{:S(2)}, u32[]{:S(2)}) collective-permute-start(f32[3,8,256]{2,1,0:T(8,128)S(1)} %get-tuple-element.95.refs_1_), channel_id=1, source_target_pairs={{0,3},{1,2},{2,1},{3,0},{4,7},{5,6},{6,5},{7,4},{8,11},{9,10},{10,... | collective-permute-start | bytes 73736 | tf_op jit(solution)/shard_map/ppermute | solution.py:332
  20.0 1.7 %collective-permute-start.11 = (f32[3,32,256]{2,1,0:T(8,128)S(1)}, f32[3,32,256]{2,1,0:T(8,128)S(1)}, u32[]{:S(2)}, u32[]{:S(2)}) collective-permute-start(f32[3,32,256]{2,1,0:T(8,128)S(1)} %shard_map.99.refs_1_), channel_id=1, source_target_pairs={{0,4},{1,5},{2,6},{3,7},{4,0},{5,1},{6,2},{7,3},{8,12},{9,13},{10,... | collective-permute-start | bytes 294920 | tf_op jit(solution)/shard_map/ppermute | solution.py:334
  21.7 1.0 %shard_map.98 = (f32[3,256,256]{2,1,0:T(8,128)S(1)}, f32[3,256,256]{2,1,0:T(8,128)S(1)}) custom-call(f32[3,256,256]{2,1,0:T(8,128)S(1)} %get-tuple-element.88.u, f32[3,256,256]{2,1,0:T(8,128)S(1)} %get-tuple-element.89.v, f32[3,256,256]{2,1,0:T(8,128)S(1)} %get-tuple-element.71.load, ...), custom_call_target="tpu_custom_call", output_to_operand_aliasing={{1}: (1, {})} | custom-call | flops 1 | bytes 1 | tf_op jit(solution)/shard_map/pallas_call | solution.py:58
  22.7 0.0 collective-permute-done.9.ya
  22.7 0.0 collective-permute-done.10.yb
  22.7 0.0 collective-permute-done.8.hb
  22.7 0.2 shard_map.101
  22.9 0.3 collective-permute-start.12
  23.2 1.5 %collective-permute-done.11.ha = f32[3,32,256]{2,1,0:T(8,128)S(1)} collective-permute-done((f32[3,32,256]{2,1,0:T(8,128)S(1)}, f32[3,32,256]{2,1,0:T(8,128)S(1)}, u32[]{:S(2)}, u32[]{:S(2)}) %collective-permute-start.11) | collective-permute-done | bytes 98336 | tf_op jit(solution)/shard_map/ppermute | solution.py:334
  24.7 0.1 shard_map.102
  24.9 0.1 collective-permute-start.13
  24.9 1.5 %collective-permute-start.14 = (f32[3,8,256]{2,1,0:T(8,128)S(1)}, f32[3,8,256]{2,1,0:T(8,128)S(1)}, u32[]{:S(2)}, u32[]{:S(2)}) collective-permute-start(f32[3,8,256]{2,1,0:T(8,128)S(1)} %get-tuple-element.105.refs_1_), channel_id=1, source_target_pairs={{0,3},{1,2},{2,1},{3,0},{4,7},{5,6},{6,5},{7,4},{8,11},{9,10},{10,... | collective-permute-start | bytes 73736 | tf_op jit(solution)/shard_map/ppermute | solution.py:332
  26.4 1.7 %collective-permute-start.15 = (f32[3,32,256]{2,1,0:T(8,128)S(1)}, f32[3,32,256]{2,1,0:T(8,128)S(1)}, u32[]{:S(2)}, u32[]{:S(2)}) collective-permute-start(f32[3,32,256]{2,1,0:T(8,128)S(1)} %shard_map.104.refs_1_), channel_id=1, source_target_pairs={{0,4},{1,5},{2,6},{3,7},{4,0},{5,1},{6,2},{7,3},{8,12},{9,13},{10,... | collective-permute-start | bytes 294920 | tf_op jit(solution)/shard_map/ppermute | solution.py:334
  28.2 1.0 %shard_map.103 = (f32[3,256,256]{2,1,0:T(8,128)S(1)}, f32[3,256,256]{2,1,0:T(8,128)S(1)}) custom-call(f32[3,256,256]{2,1,0:T(8,128)S(1)} %get-tuple-element.98.u, f32[3,256,256]{2,1,0:T(8,128)S(1)} %get-tuple-element.99.v, f32[3,256,256]{2,1,0:T(8,128)S(1)} %get-tuple-element.71.load, ...), custom_call_target="tpu_custom_call", output_to_operand_aliasing={{1}: (1, {})} | custom-call | flops 1 | bytes 1 | tf_op jit(solution)/shard_map/pallas_call | solution.py:58
  29.2 0.0 collective-permute-done.13.ya
  29.2 0.0 collective-permute-done.14.yb
  29.2 0.0 collective-permute-done.12.hb
  29.2 0.2 shard_map.106
  29.4 1.8 %collective-permute-done.15.ha = f32[3,32,256]{2,1,0:T(8,128)S(1)} collective-permute-done((f32[3,32,256]{2,1,0:T(8,128)S(1)}, f32[3,32,256]{2,1,0:T(8,128)S(1)}, u32[]{:S(2)}, u32[]{:S(2)}) %collective-permute-start.15) | collective-permute-done | bytes 98336 | tf_op jit(solution)/shard_map/ppermute | solution.py:334
  31.2 1.2 %shard_map.107 = (f32[3,256,256]{2,1,0:T(8,128)S(1)}, f32[3,256,256]{2,1,0:T(8,128)S(1)}, f32[3,256,256]{2,1,0:T(8,128)}, f32[3,256,256]{2,1,0:T(8,128)}) custom-call(f32[3,256,256]{2,1,0:T(8,128)S(1)} %get-tuple-element.106.u1, f32[3,256,256]{2,1,0:T(8,128)S(1)} %get-tuple-element.107.v1, ...), custom_call_target="tpu_custom_call", output_to_operand_aliasing={{0}: (0, {}), {1}: (1, {})} | custom-call | flops 1 | bytes 1 | tf_op jit(solution)/shard_map/pallas_call | solution.py:58
  (9 shorter events, 0.0 us)
Async XLA Ops:
  2.2 8.8 %collective-permute-start = (f32[4,32,256]{2,1,0:T(8,128)S(1)}, f32[4,32,256]{2,1,0:T(8,128)S(1)}, u32[]{:S(2)}, u32[]{:S(2)}) collective-permute-start(f32[4,32,256]{2,1,0:T(8,128)S(1)} %get-tuple-element.63.refs_1_.b_sent), channel_id=1, source_target_pairs={{0,1},{1,0},{2,3},{3,2},{4,8},{5,9},{6,10},{7,11},{8,4},{9,5},{10,... | collective-permute-start | bytes 393224 | tf_op jit(solution)/shard_map/ppermute | solution.py:329
  2.7 8.2 %collective-permute-start.1 = (f32[4,8,256]{2,1,0:T(8,128)S(1)}, f32[4,8,256]{2,1,0:T(8,128)S(1)}, u32[]{:S(2)}, u32[]{:S(2)}) collective-permute-start(f32[4,8,256]{2,1,0:T(8,128)S(1)} %shard_map.90.ya_sent), channel_id=1, source_target_pairs={{0,1},{1,0},{2,3},{3,2},{4,5},{5,4},{6,7},{7,6},{8,9},{9,8},{10,11... | collective-permute-start | bytes 98312 | tf_op jit(solution)/shard_map/ppermute | solution.py:336
  2.8 8.1 %collective-permute-start.2 = (f32[4,8,256]{2,1,0:T(8,128)S(1)}, f32[4,8,256]{2,1,0:T(8,128)S(1)}, u32[]{:S(2)}, u32[]{:S(2)}) collective-permute-start(f32[4,8,256]{2,1,0:T(8,128)S(1)} %shard_map.88.refs_1_.yb_sent), channel_id=1, source_target_pairs={{0,3},{1,2},{2,1},{3,0},{4,7},{5,6},{6,5},{7,4},{8,11},{9,10},{10,... | collective-permute-start | bytes 98312 | tf_op jit(solution)/shard_map/ppermute | solution.py:332
  5.4 6.6 %collective-permute-start.3 = (f32[4,32,256]{2,1,0:T(8,128)S(1)}, f32[4,32,256]{2,1,0:T(8,128)S(1)}, u32[]{:S(2)}, u32[]{:S(2)}) collective-permute-start(f32[4,32,256]{2,1,0:T(8,128)S(1)} %shard_map.89.refs_1_.a_sent), channel_id=1, source_target_pairs={{0,4},{1,5},{2,6},{3,7},{4,0},{5,1},{6,2},{7,3},{8,12},{9,13},{10,... | collective-permute-start | bytes 393224 | tf_op jit(solution)/shard_map/ppermute | solution.py:334
  11.1 5.9 %collective-permute-start.4 = (f32[3,32,256]{2,1,0:T(8,128)S(1)}, f32[3,32,256]{2,1,0:T(8,128)S(1)}, u32[]{:S(2)}, u32[]{:S(2)}) collective-permute-start(f32[3,32,256]{2,1,0:T(8,128)S(1)} %get-tuple-element.78), channel_id=1, source_target_pairs={{0,1},{1,0},{2,3},{3,2},{4,8},{5,9},{6,10},{7,11},{8,4},{9,5},{10,... | collective-permute-start | bytes 294920 | tf_op jit(solution)/shard_map/ppermute | solution.py:329
  12.2 4.8 %collective-permute-start.5 = (f32[3,8,256]{2,1,0:T(8,128)S(1)}, f32[3,8,256]{2,1,0:T(8,128)S(1)}, u32[]{:S(2)}, u32[]{:S(2)}) collective-permute-start(f32[3,8,256]{2,1,0:T(8,128)S(1)} %shard_map.95), channel_id=1, source_target_pairs={{0,1},{1,0},{2,3},{3,2},{4,5},{5,4},{6,7},{7,6},{8,9},{9,8},{10,11... | collective-permute-start | bytes 73736 | tf_op jit(solution)/shard_map/ppermute | solution.py:336
  12.3 4.7 %collective-permute-start.6 = (f32[3,8,256]{2,1,0:T(8,128)S(1)}, f32[3,8,256]{2,1,0:T(8,128)S(1)}, u32[]{:S(2)}, u32[]{:S(2)}) collective-permute-start(f32[3,8,256]{2,1,0:T(8,128)S(1)} %get-tuple-element.81.refs_1_), channel_id=1, source_target_pairs={{0,3},{1,2},{2,1},{3,0},{4,7},{5,6},{6,5},{7,4},{8,11},{9,10},{10,... | collective-permute-start | bytes 73736 | tf_op jit(solution)/shard_map/ppermute | solution.py:332
  13.5 5.5 %collective-permute-start.7 = (f32[3,32,256]{2,1,0:T(8,128)S(1)}, f32[3,32,256]{2,1,0:T(8,128)S(1)}, u32[]{:S(2)}, u32[]{:S(2)}) collective-permute-start(f32[3,32,256]{2,1,0:T(8,128)S(1)} %shard_map.94.refs_1_), channel_id=1, source_target_pairs={{0,4},{1,5},{2,6},{3,7},{4,0},{5,1},{6,2},{7,3},{8,12},{9,13},{10,... | collective-permute-start | bytes 294920 | tf_op jit(solution)/shard_map/ppermute | solution.py:334
  17.2 5.5 %collective-permute-start.8 = (f32[3,32,256]{2,1,0:T(8,128)S(1)}, f32[3,32,256]{2,1,0:T(8,128)S(1)}, u32[]{:S(2)}, u32[]{:S(2)}) collective-permute-start(f32[3,32,256]{2,1,0:T(8,128)S(1)} %get-tuple-element.92), channel_id=1, source_target_pairs={{0,1},{1,0},{2,3},{3,2},{4,8},{5,9},{6,10},{7,11},{8,4},{9,5},{10,... | collective-permute-start | bytes 294920 | tf_op jit(solution)/shard_map/ppermute | solution.py:329
  19.1 3.6 %collective-permute-start.9 = (f32[3,8,256]{2,1,0:T(8,128)S(1)}, f32[3,8,256]{2,1,0:T(8,128)S(1)}, u32[]{:S(2)}, u32[]{:S(2)}) collective-permute-start(f32[3,8,256]{2,1,0:T(8,128)S(1)} %shard_map.100), channel_id=1, source_target_pairs={{0,1},{1,0},{2,3},{3,2},{4,5},{5,4},{6,7},{7,6},{8,9},{9,8},{10,11... | collective-permute-start | bytes 73736 | tf_op jit(solution)/shard_map/ppermute | solution.py:336
  19.2 3.5 %collective-permute-start.10 = (f32[3,8,256]{2,1,0:T(8,128)S(1)}, f32[3,8,256]{2,1,0:T(8,128)S(1)}, u32[]{:S(2)}, u32[]{:S(2)}) collective-permute-start(f32[3,8,256]{2,1,0:T(8,128)S(1)} %get-tuple-element.95.refs_1_), channel_id=1, source_target_pairs={{0,3},{1,2},{2,1},{3,0},{4,7},{5,6},{6,5},{7,4},{8,11},{9,10},{10,... | collective-permute-start | bytes 73736 | tf_op jit(solution)/shard_map/ppermute | solution.py:332
  20.0 4.8 %collective-permute-start.11 = (f32[3,32,256]{2,1,0:T(8,128)S(1)}, f32[3,32,256]{2,1,0:T(8,128)S(1)}, u32[]{:S(2)}, u32[]{:S(2)}) collective-permute-start(f32[3,32,256]{2,1,0:T(8,128)S(1)} %shard_map.99.refs_1_), channel_id=1, source_target_pairs={{0,4},{1,5},{2,6},{3,7},{4,0},{5,1},{6,2},{7,3},{8,12},{9,13},{10,... | collective-permute-start | bytes 294920 | tf_op jit(solution)/shard_map/ppermute | solution.py:334
  22.9 6.3 %collective-permute-start.12 = (f32[3,32,256]{2,1,0:T(8,128)S(1)}, f32[3,32,256]{2,1,0:T(8,128)S(1)}, u32[]{:S(2)}, u32[]{:S(2)}) collective-permute-start(f32[3,32,256]{2,1,0:T(8,128)S(1)} %get-tuple-element.102), channel_id=1, source_target_pairs={{0,1},{1,0},{2,3},{3,2},{4,8},{5,9},{6,10},{7,11},{8,4},{9,5},{10,... | collective-permute-start | bytes 294920 | tf_op jit(solution)/shard_map/ppermute | solution.py:329
  24.9 4.3 %collective-permute-start.13 = (f32[3,8,256]{2,1,0:T(8,128)S(1)}, f32[3,8,256]{2,1,0:T(8,128)S(1)}, u32[]{:S(2)}, u32[]{:S(2)}) collective-permute-start(f32[3,8,256]{2,1,0:T(8,128)S(1)} %shard_map.105), channel_id=1, source_target_pairs={{0,1},{1,0},{2,3},{3,2},{4,5},{5,4},{6,7},{7,6},{8,9},{9,8},{10,11... | collective-permute-start | bytes 73736 | tf_op jit(solution)/shard_map/ppermute | solution.py:336
  24.9 4.3 %collective-permute-start.14 = (f32[3,8,256]{2,1,0:T(8,128)S(1)}, f32[3,8,256]{2,1,0:T(8,128)S(1)}, u32[]{:S(2)}, u32[]{:S(2)}) collective-permute-start(f32[3,8,256]{2,1,0:T(8,128)S(1)} %get-tuple-element.105.refs_1_), channel_id=1, source_target_pairs={{0,3},{1,2},{2,1},{3,0},{4,7},{5,6},{6,5},{7,4},{8,11},{9,10},{10,... | collective-permute-start | bytes 73736 | tf_op jit(solution)/shard_map/ppermute | solution.py:332
  26.4 4.8 %collective-permute-start.15 = (f32[3,32,256]{2,1,0:T(8,128)S(1)}, f32[3,32,256]{2,1,0:T(8,128)S(1)}, u32[]{:S(2)}, u32[]{:S(2)}) collective-permute-start(f32[3,32,256]{2,1,0:T(8,128)S(1)} %shard_map.104.refs_1_), channel_id=1, source_target_pairs={{0,4},{1,5},{2,6},{3,7},{4,0},{5,1},{6,2},{7,3},{8,12},{9,13},{10,... | collective-permute-start | bytes 294920 | tf_op jit(solution)/shard_map/ppermute | solution.py:334

commit v3 on v2

--- a/solution.py
+++ b/solution.py
@@ -89,7 +89,7 @@
 
 
 def open_kernel(
-    cx, cy, u_hbm, material_hbm, eroded_hbm, table_hbm, a, b, ya, yb, u, material, eroded, table, scalars, sems
+    cx, cy, u_hbm, material_hbm, eroded_hbm, table_hbm, a, b, ya, yb, u, material, eroded, table, scalars, edge, sems
 ):
     copies = [
         pltpu.make_async_copy(source, target, sems.at[i])
@@ -102,24 +102,25 @@
     copies[0].wait()
     for index in range(table.shape[0]):
         table[index : index + 1, :] = jnp.full((1, table.shape[1]), scalars[index], jnp.float32)
-    for copy in copies[1:]:
-        copy.wait()
+    copies[1].wait()
+    copies[2].wait()
     fa, fb = sides(cx)
     even = plane_even()
     for face, out in ((fa, a), (fb, b)):
         at = layer(face, cy)
-        for c in range(3):
-            out[c] = u[c, at, :]
         out[3] = lookup(material[at, :], eroded[at, :], table)
     for x in range(cx):
         top, end = slice(x * cy, x * cy + TILE), slice((x + 1) * cy - TILE, (x + 1) * cy)
-        for c in range(4):
-            if c < 3:
-                first, last = u[c, top, :], u[c, end, :]
-            else:
-                first = lookup(material[top, :], eroded[top, :], table)
-                last = lookup(material[end, :], eroded[end, :], table)
-            put_rows(even, x, c, first, last, ya, yb)
+        for i, cells in enumerate((material, eroded)):
+            put_rows(even, x, i, cells[top, :], cells[end, :], edge.at[0], edge.at[1])
+    for side, out in enumerate((ya, yb)):
+        out[3] = lookup(edge[side, 0], edge[side, 1], table)
+    copies[3].wait()
+    for face, out in ((fa, a), (fb, b)):
+        at = layer(face, cy)
+        for c in range(3):
+            out[c] = u[c, at, :]
+    pack_rows(cx, cy, u, ya, yb)
 
 
 def put_rows(even, x, c, first, last, ya, yb):
@@ -128,39 +129,80 @@
     yb[c, x : x + 1, :] = jnp.where(even, first, last)
 
 
-def advance(cx, cy, u, v, load, kx, ky, kz, rate, u_out, v_out):
+def advance(cx, cy, first, count, u, v, load, stiff, rate, u_out, v_out, halo=None):
+    kx, ky_down, ky_up, kz_down, kz_up, total = stiff
     nz = u.shape[-1]
-
-    def component(c, carry):
-        here = u[c, 0:cy, :]
-        below = None
-        for x in range(cx):
-            at = slice(x * cy, (x + 1) * cy)
-            flux_y = ky[at, :] * (pltpu.roll(here, cy - 1, 0) - here)
-            flux_z = kz[at, :] * (pltpu.roll(here, nz - 1, 1) - here)
-            force = flux_y - pltpu.roll(flux_y, 1, 0)
-            force = force + (flux_z - pltpu.roll(flux_z, 1, 1))
-            if x < cx - 1:
-                above = u[c, (x + 1) * cy : (x + 2) * cy, :]
-                flux_x = kx[at, :] * (above - here)
-                force = force + flux_x
-            if x > 0:
-                force = force - below
+    row = lax.broadcasted_iota(jnp.int32, (TILE, nz), 0)
+    even = plane_even()
+
+    def tile(x, t):
+        return pl.ds(pl.multiple_of(x * cy + t * TILE, TILE), TILE)
+
+    for i in range(count):
+        x = first + i
+        for t in range(cy // TILE):
+            at = tile(x, t)
+            x_down, x_up = tile(jnp.maximum(x - 1, 0), t), tile(jnp.minimum(x + 1, cx - 1), t)
             r = rate[at, :]
-            speed = v[c, at, :]
-            speed = speed + r * (force + load[c, at, :] - DRAG * speed)
-            v_out[c, at, :] = speed
-            u_out[c, at, :] = here + r * speed
-            if x < cx - 1:
-                here, below = above, flux_x
-        return carry
-
-    lax.fori_loop(0, 3, component, 0)
-
-
-def first_kernel(
+            for c in range(3):
+                here = u[c, at, :]
+                one, two = (h[c, pl.ds(x, 1), :] for h in halo) if halo else (here, here)
+                if t > 0:
+                    down = pltpu.roll(u[c, tile(x, t - 1), :], 1, 0)
+                else:
+                    down = jnp.where(even, two, one)
+                if t < cy // TILE - 1:
+                    up = pltpu.roll(u[c, tile(x, t + 1), :], TILE - 1, 0)
+                else:
+                    up = jnp.where(even, one, two)
+                down = jnp.where(row == 0, down, pltpu.roll(here, 1, 0))
+                up = jnp.where(row == TILE - 1, up, pltpu.roll(here, TILE - 1, 0))
+                force = (kx[at, :] * u[c, x_down, :] + kx[tile(x + 1, t), :] * u[c, x_up, :]) - total[at, :] * here
+                force = force + (ky_down[at, :] * down + ky_up[at, :] * up)
+                force = force + (
+                    kz_down[at, :] * pltpu.roll(here, 1, 1) + kz_up[at, :] * pltpu.roll(here, nz - 1, 1)
+                )
+                speed = v[c, at, :]
+                speed = speed + r * (force + load[c, at, :] - DRAG * speed)
+                v_out[c, at, :] = speed
+                u_out[c, at, :] = here + r * speed
+
+
+def edge_kernel(cx, cy, u, v, load, kx, kyd, kyu, kzd, kzu, total, rate, u_out, v_out):
+    advance(cx, cy, sides(cx)[1], 1, u, v, load, (kx, kyd, kyu, kzd, kzu, total), rate, u_out, v_out)
+
+
+def rest_first(cx):
+    return jnp.where(sides(cx)[1] == 0, 1, 0)
+
+
+def rest_kernel(cx, cy, u1, v, u, load, kx, kyd, kyu, kzd, kzu, total, rate, ya, yb, u_out, v_out):
+    stiff = kx, kyd, kyu, kzd, kzu, total
+    advance(cx, cy, rest_first(cx), cx - 1, u, v, load, stiff, rate, u_out, v_out, (ya, yb))
+
+
+def rest_kernel_first(
+    cx, cy, u1, v, kyd, kyu, total, u, load, kx, kzd, kzu, rate, ya, yb, ya_sent, yb_sent,
+    u_out, v_out, kyd_out, kyu_out, total_out,
+):
+    low, high = row_stiffness(ya_sent, yb_sent, ya, yb)
+    row = lax.broadcasted_iota(jnp.int32, (TILE, u.shape[-1]), 0)
+    for x in range(cx):
+        for start, edge, k, out in (
+            (x * cy, 0, low, kyd_out),
+            ((x + 1) * cy - TILE, TILE - 1, high, kyu_out),
+        ):
+            at = slice(start, start + TILE)
+            extra = jnp.where(row == edge, k[x : x + 1, :], 0.0)
+            out[at, :] += extra
+            total_out[at, :] += extra
+    stiff = kx, kyd_out, kyu_out, kzd, kzu, total_out
+    advance(cx, cy, rest_first(cx), cx - 1, u, v, load, stiff, rate, u_out, v_out, (ya, yb))
+
+
+def prepare_kernel(
     cx, cy, u, material, eroded, table, v_hbm, load_hbm, damaged_hbm,
-    u_out, v_out, load, kx, ky, kz, coarse, fine, damaged, sems,
+    u_out, v_out, load, kx, kyd, kyu, kzd, kzu, total, coarse, fine, damaged, sems,
 ):
     copies = [
         pltpu.make_async_copy(source, target, sems.at[i])
@@ -171,16 +213,26 @@
     nz = u.shape[-1]
     row = lax.broadcasted_iota(jnp.int32, (cy, nz), 0)
     lane = lax.broadcasted_iota(jnp.int32, (cy, nz), 1)
-    below = None
+    nothing = jnp.zeros((cy, nz), jnp.float32)
+
+    def stiffness(x):
+        at = slice(x * cy, (x + 1) * cy)
+        return lookup(material[at, :], eroded[at, :], table) if 0 <= x < cx else nothing
+
+    face, k = nothing, stiffness(0)
     for x in range(cx):
         at = slice(x * cy, (x + 1) * cy)
-        k = lookup(material[at, :], eroded[at, :], table)
-        ky[at, :] = jnp.where(row < cy - 1, jnp.minimum(k, pltpu.roll(k, cy - 1, 0)), 0.0)
-        kz[at, :] = jnp.where(lane < nz - 1, jnp.minimum(k, pltpu.roll(k, nz - 1, 1)), 0.0)
-        if x > 0:
-            kx[(x - 1) * cy : x * cy, :] = jnp.minimum(below, k)
-        below = k
-    kx[(cx - 1) * cy : cx * cy, :] = jnp.zeros((cy, nz), jnp.float32)
+        y_up = jnp.where(row < cy - 1, jnp.minimum(k, pltpu.roll(k, cy - 1, 0)), 0.0)
+        y_down = jnp.where(row > 0, jnp.minimum(k, pltpu.roll(k, 1, 0)), 0.0)
+        z_up = jnp.where(lane < nz - 1, jnp.minimum(k, pltpu.roll(k, nz - 1, 1)), 0.0)
+        z_down = jnp.where(lane > 0, jnp.minimum(k, pltpu.roll(k, 1, 1)), 0.0)
+        above = stiffness(x + 1)
+        face_up = jnp.minimum(k, above)
+        for out, value in ((kx, face), (kyu, y_up), (kyd, y_down), (kzu, z_up), (kzd, z_down)):
+            out[at, :] = value
+        total[at, :] = ((face + face_up) + (y_up + y_down)) + (z_up + z_down)
+        face, k = face_up, above
+    kx[cx * cy : (cx + 1) * cy, :] = nothing
     copies[0].wait()
     for x in range(cx):
         at = slice(x * cy, (x + 1) * cy)
@@ -189,7 +241,8 @@
         fine[at, :] = jnp.where(hit, FINE, 0.0)
     for copy in copies[1:]:
         copy.wait()
-    advance(cx, cy, u, v_out, load, kx, ky, kz, coarse, u_out, v_out)
+    stiff = kx, kyd, kyu, kzd, kzu, total
+    advance(cx, cy, sides(cx)[1], 1, u, v_out, load, stiff, coarse, u_out, v_out)
 
 
 def fix_face(at, u, rate, k, halo, u_new, v_new, send):
@@ -203,19 +256,17 @@
             send[c] = moved
 
 
-def fix_rows(cx, cy, u, rate, k_low, k_high, ya, yb, u_new, v_new):
+def fix_rows(cy, x, u, rate, k_low, k_high, ya, yb, u_new, v_new):
     even = plane_even()
-    for c in range(3):
-        low = jnp.where(even, yb[c], ya[c])
-        high = jnp.where(even, ya[c], yb[c])
-        for x in range(cx):
-            tile = slice(x * TILE, (x + 1) * TILE)
-            for start, k, halo in ((x * cy, k_low, low), ((x + 1) * cy - TILE, k_high, high)):
-                at = slice(start, start + TILE)
-                r = rate[at, :]
-                push = r * (k[tile, :] * (halo[x : x + 1, :] - u[c, at, :]))
-                v_new[c, at, :] += push
-                u_new[c, at, :] += r * push
+    for start, k, flip in ((x * cy, k_low, False), ((x + 1) * cy - TILE, k_high, True)):
+        at = pl.ds(pl.multiple_of(start, TILE), TILE)
+        r = rate[at, :]
+        for c in range(3):
+            one, two = ya[c, pl.ds(x, 1), :], yb[c, pl.ds(x, 1), :]
+            halo = jnp.where(even, one, two) if flip else jnp.where(even, two, one)
+            push = r * (k[...] * (halo - u[c, at, :]))
+            v_new[c, at, :] += push
+            u_new[c, at, :] += r * push
 
 
 def pack_rows(cx, cy, u_new, ya_send, yb_send):
@@ -235,38 +286,38 @@
     return jnp.minimum(sent[3], received[3]) * flag("slab", second)
 
 
-def row_stiffness(cx, ya_sent, yb_sent, ya, yb, k_low, k_high):
+def row_stiffness(ya_sent, yb_sent, ya, yb):
     even = plane_even()
     k_a = jnp.minimum(ya_sent[3], ya[3]) * flag("plane", False)
     k_b = jnp.minimum(yb_sent[3], yb[3]) * flag("plane", True)
-    low, high = jnp.where(even, k_b, k_a), jnp.where(even, k_a, k_b)
-    row = lax.broadcasted_iota(jnp.int32, (TILE, ya.shape[-1]), 0)
-    for x in range(cx):
-        tile = slice(x * TILE, (x + 1) * TILE)
-        k_low[tile, :] = jnp.where(row == 0, low[x : x + 1, :], 0.0)
-        k_high[tile, :] = jnp.where(row == TILE - 1, high[x : x + 1, :], 0.0)
+    return jnp.where(even, k_b, k_a), jnp.where(even, k_a, k_b)
 
 
 def fix_b_first(
-    cx, cy, u1, v1, u, rate, hb, ya, yb, b_sent, ya_sent, yb_sent, u_new, v_new, send, kb, k_low, k_high
+    cx, cy, u1, v1, u, rate, hb, ya, yb, b_sent, ya_sent, yb_sent, u_new, v_new, send, kb, k_low, k_high, sides_k
 ):
-    row_stiffness(cx, ya_sent, yb_sent, ya, yb, k_low, k_high)
-    fix_rows(cx, cy, u, rate, k_low, k_high, ya, yb, u_new, v_new)
-    k = face_stiffness(b_sent, hb, True)
-    kb[...] = k
-    fix_face(layer(sides(cx)[1], cy), u, rate, k, hb, u_new, v_new, send)
+    sides_k[0], sides_k[1] = row_stiffness(ya_sent, yb_sent, ya, yb)
+    row = lax.broadcasted_iota(jnp.int32, k_low.shape, 0)
+    face = sides(cx)[1]
+    k_low[...] = jnp.where(row == 0, sides_k[0, pl.ds(face, 1), :], 0.0)
+    k_high[...] = jnp.where(row == TILE - 1, sides_k[1, pl.ds(face, 1), :], 0.0)
+    kb[...] = face_stiffness(b_sent, hb, True)
+    fix_b(cx, cy, u1, v1, u, rate, hb, ya, yb, kb, k_low, k_high, u_new, v_new, send)
 
 
 def fix_a_first(cx, cy, u1, v1, u, rate, ha, a_sent, u_new, v_new, send, ya_send, yb_send, ka):
-    k = face_stiffness(a_sent, ha, False)
-    ka[...] = k
-    fix_face(layer(sides(cx)[0], cy), u, rate, k, ha, u_new, v_new, send)
-    pack_rows(cx, cy, u_new, ya_send, yb_send)
+    ka[...] = face_stiffness(a_sent, ha, False)
+    fix_a(cx, cy, u1, v1, u, rate, ha, ka, u_new, v_new, send, ya_send, yb_send)
 
 
 def fix_b(cx, cy, u1, v1, u, rate, hb, ya, yb, kb, k_low, k_high, u_new, v_new, send):
-    fix_rows(cx, cy, u, rate, k_low, k_high, ya, yb, u_new, v_new)
-    fix_face(layer(sides(cx)[1], cy), u, rate, kb[...], hb, u_new, v_new, send)
+    face = sides(cx)[1]
+    fix_rows(cy, face, u, rate, k_low, k_high, ya, yb, u_new, v_new)
+    fix_face(layer(face, cy), u, rate, kb[...], hb, u_new, v_new, send)
+
+
+def fix_b_last(cx, cy, u1, v1, u, rate, hb, ya, yb, kb, k_low, k_high, u_new, v_new):
+    fix_b(cx, cy, u1, v1, u, rate, hb, ya, yb, kb, k_low, k_high, u_new, v_new, None)
 
 
 def fix_a(cx, cy, u1, v1, u, rate, ha, ka, u_new, v_new, send, ya_send, yb_send):
@@ -280,10 +331,6 @@
 
 def after(array, other):
     return call(hand_on, [array.shape], (array, other), {0: 0})[0]
-
-
-def fix_b_last(cx, cy, u1, v1, u, rate, hb, ya, yb, kb, k_low, k_high, u_new, v_new):
-    fix_b(cx, cy, u1, v1, u, rate, hb, ya, yb, kb, k_low, k_high, u_new, v_new, None)
 
 
 def last_kernel(cx, cy, u1, v1, u, rate, ha, ka, u_new, v_new, u_out, v_out, sems):
@@ -323,8 +370,13 @@
         (),
         in_hbm=(u, material, eroded, stiff_table),
         dtypes=[jnp.float32] * 5 + [jnp.int32] * 2 + [jnp.float32],
-        scratch=[pltpu.SMEM(stiff_table.shape, jnp.float32), pltpu.SemaphoreType.DMA((4,))],
+        scratch=[
+            pltpu.SMEM(stiff_table.shape, jnp.float32),
+            pltpu.VMEM((2, 2, cx, nz), jnp.int32),
+            pltpu.SemaphoreType.DMA((4,)),
+        ],
     )
+    both = {0: 0, 1: 1}
     for sub in range(SUBSTEPS):
         hb = lax.ppermute(b, AXES, xb)
         if sub == 0:
@@ -335,45 +387,55 @@
         ya = after(ya, a)
         hya = lax.ppermute(ya, AXES, pa)
         if sub == 0:
-            u_new, v, load, kx, ky, kz, coarse, fine = call(
-                bind(first_kernel),
-                [field] * 3 + [cells] * 5,
+            u_new, v, load, kx, kyd, kyu, kzd, kzu, total, coarse, fine = call(
+                bind(prepare_kernel),
+                [field] * 3 + [((cx + 1) * cy, nz)] + [cells] * 7,
                 (u, material, eroded, table),
                 in_hbm=(v, load, damaged),
                 scratch=[pltpu.VMEM(cells, jnp.int32), pltpu.SemaphoreType.DMA((3,))],
             )
-            u_new, v, b, kb, k_low, k_high = call(
+            rate = coarse
+            u_new, v, b_next, kb, k_low, k_high = call(
                 bind(fix_b_first),
-                [field, field, face, (cy, nz), (cx * TILE, nz), (cx * TILE, nz)],
-                (u_new, v, u, coarse, hb, hya, hyb, b, ya, yb),
-                {0: 0, 1: 1}, weight=LONG,
-            )
+                [field, field, face, (cy, nz), (TILE, nz), (TILE, nz)],
+                (u_new, v, u, rate, hb, hya, hyb, b, ya, yb),
+                both,
+                weight=LONG,
+                scratch=[pltpu.VMEM((2, cx, nz), jnp.float32)],
+            )
+            u_new, v, kyd, kyu, total = call(
+                bind(rest_kernel_first),
+                [field, field] + [cells] * 3,
+                (u_new, v, kyd, kyu, total, u, load, kx, kzd, kzu, rate, hya, hyb, ya, yb),
+                {i: i for i in range(5)},
+            )
+        else:
+            rate = fine
+            stiff = kx, kyd, kyu, kzd, kzu, total
+            u_new, v = call(bind(edge_kernel), [field, field], (u, v, load, *stiff, rate), {1: 1})
+            last = sub == SUBSTEPS - 1
+            u_new, v, *sent = call(
+                bind(fix_b_last if last else fix_b),
+                [field, field] if last else [field, field, face],
+                (u_new, v, u, rate, hb, hya, hyb, kb, k_low, k_high),
+                both,
+                weight=LONG,
+            )
+            b_next = None if last else sent[0]
+            u_new, v = call(
+                bind(rest_kernel), [field, field], (u_new, v, u, load, *stiff, rate, hya, hyb), both
+            )
+        b = b_next
+        if sub == 0:
             u_new, v, a, ya, yb, ka = call(
-                bind(fix_a_first),
-                [field, field, face, side, side, (cy, nz)],
-                (u_new, v, u, coarse, ha, a),
-                {0: 0, 1: 1},
-            )
-        else:
-            u_new, v = call(bind(advance), [field, field], (u, v, load, kx, ky, kz, fine), {1: 1})
-            if sub < SUBSTEPS - 1:
-                u_new, v, b = call(
-                    bind(fix_b),
-                    [field, field, face],
-                    (u_new, v, u, fine, hb, hya, hyb, kb, k_low, k_high),
-                    {0: 0, 1: 1}, weight=LONG,
-                )
-                u_new, v, a, ya, yb = call(
-                    bind(fix_a),
-                    [field, field, face, side, side],
-                    (u_new, v, u, fine, ha, ka),
-                    {0: 0, 1: 1},
-                )
+                bind(fix_a_first), [field, field, face, side, side, (cy, nz)], (u_new, v, u, rate, ha, a), both
+            )
+        elif sub < SUBSTEPS - 1:
+            u_new, v, a, ya, yb = call(
+                bind(fix_a), [field, field, face, side, side], (u_new, v, u, rate, ha, ka), both
+            )
         if sub < SUBSTEPS - 1:
             u = u_new
-    u_new, v = call(
-        bind(fix_b_last), [field, field], (u_new, v, u, fine, hb, hya, hyb, kb, k_low, k_high), {0: 0, 1: 1}, weight=LONG
-    )
     out = call(
         bind(last_kernel),
         [field, field],

time: 32.6 us -> 32.4 us (level)
  Pallas kernels: 9.25 us -> 8.48 us
  waiting for transfers between devices: 5.94 us -> 6.48 us
    pallas_call x22 -> x26, Pallas kernels: 9.25 us -> 8.48 us  [call(): pl.pallas_call(kernel, in_specs=[VMEM] * len(arrays) + [HBM] * len(in_hbm...]
    ppermute x4, waiting for transfers between devices: 0.01 us -> 0.71 us  [per_device(): hyb = lax.ppermute(yb, AXES, pb)]
    ppermute x4, starting transfers between devices: 6.14 us -> 5.78 us  [per_device(): hyb = lax.ppermute(yb, AXES, pb)]
  transfers between devices with their start and end apart: 16 -> 16, of which waited for: 4 -> 6; matrix products, arithmetic and copies ran while one was open for 0% -> 0% of each run, Pallas kernels for 20% -> 18%
where the time goes in v3:
time: 32.4 us; the launch traced here: 32.2 us
  starting transfers between devices  16.4 us (51%)
  Pallas kernels  8.48 us (26%)
  waiting for transfers between devices  6.48 us (20%)
  between operations  0.86 us (3%)
    ppermute x4, starting transfers between devices, per_device(): ha = lax.ppermute(a, AXES, xa)  9.15 us
    pallas_call x26, Pallas kernels, call(): pl.pallas_call(kernel, in_specs=[VMEM] * len(arrays) + [HBM] * len(in_hbm...  8.48 us
    ppermute x4, starting transfers between devices, per_device(): hyb = lax.ppermute(yb, AXES, pb)  5.78 us
    ppermute x4, waiting for transfers between devices, per_device(): ha = lax.ppermute(a, AXES, xa)  5.76 us
    ppermute x4, starting transfers between devices, per_device(): hb = lax.ppermute(b, AXES, xb)  1.17 us
    ppermute x4, waiting for transfers between devices, per_device(): hyb = lax.ppermute(yb, AXES, pb)  0.71 us
  transfers between devices with their start and end apart: 16, of which 6 were waited for; matrix products, arithmetic and copies ran while one was open for 0% of the time, Pallas kernels for 18%

profile of v3, /device:TPU:0, one launch (start us, length us, event | category | flops | bytes accessed | tf_op | source)
XLA Modules:
  0.0 32.2 jit_solution(12167845090984324182)
XLA Ops:
  0.6 1.4 %shard_map.86 = (f32[4,32,256]{2,1,0:T(8,128)S(1)}, f32[4,32,256]{2,1,0:T(8,128)S(1)}, f32[4,8,256]{2,1,0:T(8,128)S(1)}, f32[4,8,256]{2,1,0:T(8,128)S(1)}, f32[3...) custom-call(f32[3,256,256]{2,1,0:T(8,128)} %bitcast.8, ...), custom_call_target="tpu_custom_call" | custom-call | flops 1 | bytes 1 | tf_op jit(solution)/shard_map/pallas_call | solution.py:58
  2.0 0.5 %collective-permute-start = (f32[4,32,256]{2,1,0:T(8,128)S(1)}, f32[4,32,256]{2,1,0:T(8,128)S(1)}, u32[]{:S(2)}, u32[]{:S(2)}) collective-permute-start(f32[4,32,256]{2,1,0:T(8,128)S(1)} %get-tuple-element.77.refs_1_.b_sent), channel_id=1, source_target_pairs={{0,1},{1,0},{2,3},{3,2},{4,8},{5,9},{6,10},{7,11},{8,4},{9,5},{10,... | collective-permute-start | bytes 393224 | tf_op jit(solution)/shard_map/ppermute | solution.py:381
  2.6 0.1 collective-permute-start.1
  2.7 2.6 %collective-permute-start.2 = (f32[4,8,256]{2,1,0:T(8,128)S(1)}, f32[4,8,256]{2,1,0:T(8,128)S(1)}, u32[]{:S(2)}, u32[]{:S(2)}) collective-permute-start(f32[4,8,256]{2,1,0:T(8,128)S(1)} %shard_map.88.refs_1_.yb_sent), channel_id=1, source_target_pairs={{0,3},{1,2},{2,1},{3,0},{4,7},{5,6},{6,5},{7,4},{8,11},{9,10},{10,... | collective-permute-start | bytes 98312 | tf_op jit(solution)/shard_map/ppermute | solution.py:384
  5.3 2.9 %collective-permute-start.3 = (f32[4,32,256]{2,1,0:T(8,128)S(1)}, f32[4,32,256]{2,1,0:T(8,128)S(1)}, u32[]{:S(2)}, u32[]{:S(2)}) collective-permute-start(f32[4,32,256]{2,1,0:T(8,128)S(1)} %shard_map.89.refs_1_.a_sent), channel_id=1, source_target_pairs={{0,4},{1,5},{2,6},{3,7},{4,0},{5,1},{6,2},{7,3},{8,12},{9,13},{10,... | collective-permute-start | bytes 393224 | tf_op jit(solution)/shard_map/ppermute | solution.py:386
  8.2 1.8 %shard_map.87 = (f32[3,256,256]{2,1,0:T(8,128)S(1)}, f32[3,256,256]{2,1,0:T(8,128)S(1)}, f32[3,256,256]{2,1,0:T(8,128)S(1)}, f32[288,256]{1,0:T(8,128)S(1)}, f32...) custom-call(f32[3,256,256]{2,1,0:T(8,128)S(1)} %get-tuple-element.70, ...), custom_call_target="tpu_custom_call" | custom-call | flops 1 | bytes 1 | tf_op jit(solution)/shard_map/pallas_call | solution.py:58
  10.1 0.0 collective-permute-done.1.ya
  10.1 0.0 collective-permute-done.2.yb
  10.1 0.0 collective-permute-done.hb
  10.1 0.1 shard_map.91
  10.2 0.1 collective-permute-start.4
  10.3 0.8 %shard_map.92 = (f32[3,256,256]{2,1,0:T(8,128)S(1)}, f32[3,256,256]{2,1,0:T(8,128)S(1)}, f32[256,256]{1,0:T(8,128)S(1)}, f32[256,256]{1,0:T(8,128)S(1)}, f32[256,256]{1,0:T(8,128)S(1)}) custom-call(f32[3,256,256]{2,1,0:T(8,128)S(1)} %get-tuple-element.81.u1, ...), custom_call_target="tpu_custom_call", output_to_operand_aliasing={{0}: (0, {}), {1}: (1, {}), {2}: (2, {}), {3}: (3, {}), {4}... | custom-call | flops 1 | bytes 1 | tf_op jit(solution)/shard_map/pallas_call | solution.py:58
  11.1 0.8 %collective-permute-done.3.ha = f32[4,32,256]{2,1,0:T(8,128)S(1)} collective-permute-done((f32[4,32,256]{2,1,0:T(8,128)S(1)}, f32[4,32,256]{2,1,0:T(8,128)S(1)}, u32[]{:S(2)}, u32[]{:S(2)}) %collective-permute-start.3) | collective-permute-done | bytes 131104 | tf_op jit(solution)/shard_map/ppermute | solution.py:386
  11.9 0.1 shard_map.93
  12.0 0.1 collective-permute-start.5
  12.1 1.2 %collective-permute-start.6 = (f32[3,8,256]{2,1,0:T(8,128)S(1)}, f32[3,8,256]{2,1,0:T(8,128)S(1)}, u32[]{:S(2)}, u32[]{:S(2)}) collective-permute-start(f32[3,8,256]{2,1,0:T(8,128)S(1)} %get-tuple-element.103.refs_1_), channel_id=1, source_target_pairs={{0,3},{1,2},{2,1},{3,0},{4,7},{5,6},{6,5},{7,4},{8,11},{9,10},{10,... | collective-permute-start | bytes 73736 | tf_op jit(solution)/shard_map/ppermute | solution.py:384
  13.4 2.5 %collective-permute-start.7 = (f32[3,32,256]{2,1,0:T(8,128)S(1)}, f32[3,32,256]{2,1,0:T(8,128)S(1)}, u32[]{:S(2)}, u32[]{:S(2)}) collective-permute-start(f32[3,32,256]{2,1,0:T(8,128)S(1)} %shard_map.95.refs_1_), channel_id=1, source_target_pairs={{0,4},{1,5},{2,6},{3,7},{4,0},{5,1},{6,2},{7,3},{8,12},{9,13},{10,... | collective-permute-start | bytes 294920 | tf_op jit(solution)/shard_map/ppermute | solution.py:386
  15.8 0.1 shard_map.94
  16.0 0.0 collective-permute-done.5.ya
  16.0 0.0 collective-permute-done.6.yb
  16.0 0.0 collective-permute-done.4.hb
  16.0 0.1 shard_map.97
  16.1 0.1 collective-permute-start.8
  16.2 0.8 %shard_map.98 = (f32[3,256,256]{2,1,0:T(8,128)S(1)}, f32[3,256,256]{2,1,0:T(8,128)S(1)}) custom-call(f32[3,256,256]{2,1,0:T(8,128)S(1)} %get-tuple-element.107.u1, f32[3,256,256]{2,1,0:T(8,128)S(1)} %get-tuple-element.108.v, f32[3,256,256]{2,1,0:T(8,128)S(1)} %get-tuple-element.92.u, ...), custom_call_target="tpu_custom_call", output_to_operand_aliasing={{0}: (0, {}), {1}: (1, {})} | custom-call | flops 1 | bytes 1 | tf_op jit(solution)/shard_map/pallas_call | solution.py:58
  16.9 1.9 %collective-permute-done.7.ha = f32[3,32,256]{2,1,0:T(8,128)S(1)} collective-permute-done((f32[3,32,256]{2,1,0:T(8,128)S(1)}, f32[3,32,256]{2,1,0:T(8,128)S(1)}, u32[]{:S(2)}, u32[]{:S(2)}) %collective-permute-start.7) | collective-permute-done | bytes 98336 | tf_op jit(solution)/shard_map/ppermute | solution.py:386
  18.9 0.1 shard_map.99
  19.0 0.1 collective-permute-start.9
  19.1 0.7 %collective-permute-start.10 = (f32[3,8,256]{2,1,0:T(8,128)S(1)}, f32[3,8,256]{2,1,0:T(8,128)S(1)}, u32[]{:S(2)}, u32[]{:S(2)}) collective-permute-start(f32[3,8,256]{2,1,0:T(8,128)S(1)} %get-tuple-element.119.refs_1_), channel_id=1, source_target_pairs={{0,3},{1,2},{2,1},{3,0},{4,7},{5,6},{6,5},{7,4},{8,11},{9,10},{10,... | collective-permute-start | bytes 73736 | tf_op jit(solution)/shard_map/ppermute | solution.py:384
  19.8 2.0 %collective-permute-start.11 = (f32[3,32,256]{2,1,0:T(8,128)S(1)}, f32[3,32,256]{2,1,0:T(8,128)S(1)}, u32[]{:S(2)}, u32[]{:S(2)}) collective-permute-start(f32[3,32,256]{2,1,0:T(8,128)S(1)} %shard_map.101.refs_1_), channel_id=1, source_target_pairs={{0,4},{1,5},{2,6},{3,7},{4,0},{5,1},{6,2},{7,3},{8,12},{9,13},{10,... | collective-permute-start | bytes 294920 | tf_op jit(solution)/shard_map/ppermute | solution.py:386
  21.8 0.1 shard_map.100
  21.9 0.0 collective-permute-done.9.ya
  21.9 0.5 %collective-permute-done.10.yb = f32[3,8,256]{2,1,0:T(8,128)S(1)} collective-permute-done((f32[3,8,256]{2,1,0:T(8,128)S(1)}, f32[3,8,256]{2,1,0:T(8,128)S(1)}, u32[]{:S(2)}, u32[]{:S(2)}) %collective-permute-start.10) | collective-permute-done | bytes 24608 | tf_op jit(solution)/shard_map/ppermute | solution.py:384
  22.4 0.0 collective-permute-done.8.hb
  22.4 0.1 shard_map.103
  22.4 0.5 %collective-permute-start.12 = (f32[3,32,256]{2,1,0:T(8,128)S(1)}, f32[3,32,256]{2,1,0:T(8,128)S(1)}, u32[]{:S(2)}, u32[]{:S(2)}) collective-permute-start(f32[3,32,256]{2,1,0:T(8,128)S(1)} %get-tuple-element.128), channel_id=1, source_target_pairs={{0,1},{1,0},{2,3},{3,2},{4,8},{5,9},{6,10},{7,11},{8,4},{9,5},{10,... | collective-permute-start | bytes 294920 | tf_op jit(solution)/shard_map/ppermute | solution.py:381
  23.0 0.7 %shard_map.104 = (f32[3,256,256]{2,1,0:T(8,128)S(1)}, f32[3,256,256]{2,1,0:T(8,128)S(1)}) custom-call(f32[3,256,256]{2,1,0:T(8,128)S(1)} %get-tuple-element.120.u1, f32[3,256,256]{2,1,0:T(8,128)S(1)} %get-tuple-element.121.v, f32[3,256,256]{2,1,0:T(8,128)S(1)} %get-tuple-element.112.u, ...), custom_call_target="tpu_custom_call", output_to_operand_aliasing={{0}: (0, {}), {1}: (1, {})} | custom-call | flops 1 | bytes 1 | tf_op jit(solution)/shard_map/pallas_call | solution.py:58
  23.7 1.2 %collective-permute-done.11.ha = f32[3,32,256]{2,1,0:T(8,128)S(1)} collective-permute-done((f32[3,32,256]{2,1,0:T(8,128)S(1)}, f32[3,32,256]{2,1,0:T(8,128)S(1)}, u32[]{:S(2)}, u32[]{:S(2)}) %collective-permute-start.11) | collective-permute-done | bytes 98336 | tf_op jit(solution)/shard_map/ppermute | solution.py:386
  24.9 0.1 shard_map.105
  25.0 0.1 collective-permute-start.13
  25.1 1.2 %collective-permute-start.14 = (f32[3,8,256]{2,1,0:T(8,128)S(1)}, f32[3,8,256]{2,1,0:T(8,128)S(1)}, u32[]{:S(2)}, u32[]{:S(2)}) collective-permute-start(f32[3,8,256]{2,1,0:T(8,128)S(1)} %get-tuple-element.131.refs_1_), channel_id=1, source_target_pairs={{0,3},{1,2},{2,1},{3,0},{4,7},{5,6},{6,5},{7,4},{8,11},{9,10},{10,... | collective-permute-start | bytes 73736 | tf_op jit(solution)/shard_map/ppermute | solution.py:384
  26.3 1.7 %collective-permute-start.15 = (f32[3,32,256]{2,1,0:T(8,128)S(1)}, f32[3,32,256]{2,1,0:T(8,128)S(1)}, u32[]{:S(2)}, u32[]{:S(2)}) collective-permute-start(f32[3,32,256]{2,1,0:T(8,128)S(1)} %shard_map.107.refs_1_), channel_id=1, source_target_pairs={{0,4},{1,5},{2,6},{3,7},{4,0},{5,1},{6,2},{7,3},{8,12},{9,13},{10,... | collective-permute-start | bytes 294920 | tf_op jit(solution)/shard_map/ppermute | solution.py:386
  28.0 0.1 shard_map.106
  28.2 0.0 collective-permute-done.13.ya
  28.2 0.2 collective-permute-done.14.yb
  28.4 0.0 collective-permute-done.12.hb
  28.5 0.8 %shard_map.110 = (f32[3,256,256]{2,1,0:T(8,128)S(1)}, f32[3,256,256]{2,1,0:T(8,128)S(1)}) custom-call(f32[3,256,256]{2,1,0:T(8,128)S(1)} %get-tuple-element.132.u1, f32[3,256,256]{2,1,0:T(8,128)S(1)} %get-tuple-element.133.v, f32[3,256,256]{2,1,0:T(8,128)S(1)} %get-tuple-element.124.u, ...), custom_call_target="tpu_custom_call", output_to_operand_aliasing={{0}: (0, {}), {1}: (1, {})} | custom-call | flops 1 | bytes 1 | tf_op jit(solution)/shard_map/pallas_call | solution.py:58
  29.3 1.8 %collective-permute-done.15.ha = f32[3,32,256]{2,1,0:T(8,128)S(1)} collective-permute-done((f32[3,32,256]{2,1,0:T(8,128)S(1)}, f32[3,32,256]{2,1,0:T(8,128)S(1)}, u32[]{:S(2)}, u32[]{:S(2)}) %collective-permute-start.15) | collective-permute-done | bytes 98336 | tf_op jit(solution)/shard_map/ppermute | solution.py:386
  31.1 1.2 %shard_map.111 = (f32[3,256,256]{2,1,0:T(8,128)S(1)}, f32[3,256,256]{2,1,0:T(8,128)S(1)}, f32[3,256,256]{2,1,0:T(8,128)}, f32[3,256,256]{2,1,0:T(8,128)}) custom-call(f32[3,256,256]{2,1,0:T(8,128)S(1)} %get-tuple-element.134.u1, f32[3,256,256]{2,1,0:T(8,128)S(1)} %get-tuple-element.135.v1, ...), custom_call_target="tpu_custom_call", output_to_operand_aliasing={{0}: (0, {}), {1}: (1, {})} | custom-call | flops 1 | bytes 1 | tf_op jit(solution)/shard_map/pallas_call | solution.py:58
  (10 shorter events, 0.1 us)
Async XLA Ops:
  2.0 8.1 %collective-permute-start = (f32[4,32,256]{2,1,0:T(8,128)S(1)}, f32[4,32,256]{2,1,0:T(8,128)S(1)}, u32[]{:S(2)}, u32[]{:S(2)}) collective-permute-start(f32[4,32,256]{2,1,0:T(8,128)S(1)} %get-tuple-element.77.refs_1_.b_sent), channel_id=1, source_target_pairs={{0,1},{1,0},{2,3},{3,2},{4,8},{5,9},{6,10},{7,11},{8,4},{9,5},{10,... | collective-permute-start | bytes 393224 | tf_op jit(solution)/shard_map/ppermute | solution.py:381
  2.6 7.5 %collective-permute-start.1 = (f32[4,8,256]{2,1,0:T(8,128)S(1)}, f32[4,8,256]{2,1,0:T(8,128)S(1)}, u32[]{:S(2)}, u32[]{:S(2)}) collective-permute-start(f32[4,8,256]{2,1,0:T(8,128)S(1)} %shard_map.90.ya_sent), channel_id=1, source_target_pairs={{0,1},{1,0},{2,3},{3,2},{4,5},{5,4},{6,7},{7,6},{8,9},{9,8},{10,11... | collective-permute-start | bytes 98312 | tf_op jit(solution)/shard_map/ppermute | solution.py:388
  2.7 7.4 %collective-permute-start.2 = (f32[4,8,256]{2,1,0:T(8,128)S(1)}, f32[4,8,256]{2,1,0:T(8,128)S(1)}, u32[]{:S(2)}, u32[]{:S(2)}) collective-permute-start(f32[4,8,256]{2,1,0:T(8,128)S(1)} %shard_map.88.refs_1_.yb_sent), channel_id=1, source_target_pairs={{0,3},{1,2},{2,1},{3,0},{4,7},{5,6},{6,5},{7,4},{8,11},{9,10},{10,... | collective-permute-start | bytes 98312 | tf_op jit(solution)/shard_map/ppermute | solution.py:384
  5.3 6.6 %collective-permute-start.3 = (f32[4,32,256]{2,1,0:T(8,128)S(1)}, f32[4,32,256]{2,1,0:T(8,128)S(1)}, u32[]{:S(2)}, u32[]{:S(2)}) collective-permute-start(f32[4,32,256]{2,1,0:T(8,128)S(1)} %shard_map.89.refs_1_.a_sent), channel_id=1, source_target_pairs={{0,4},{1,5},{2,6},{3,7},{4,0},{5,1},{6,2},{7,3},{8,12},{9,13},{10,... | collective-permute-start | bytes 393224 | tf_op jit(solution)/shard_map/ppermute | solution.py:386
  10.2 5.8 %collective-permute-start.4 = (f32[3,32,256]{2,1,0:T(8,128)S(1)}, f32[3,32,256]{2,1,0:T(8,128)S(1)}, u32[]{:S(2)}, u32[]{:S(2)}) collective-permute-start(f32[3,32,256]{2,1,0:T(8,128)S(1)} %get-tuple-element.100), channel_id=1, source_target_pairs={{0,1},{1,0},{2,3},{3,2},{4,8},{5,9},{6,10},{7,11},{8,4},{9,5},{10,... | collective-permute-start | bytes 294920 | tf_op jit(solution)/shard_map/ppermute | solution.py:381
  12.0 3.9 %collective-permute-start.5 = (f32[3,8,256]{2,1,0:T(8,128)S(1)}, f32[3,8,256]{2,1,0:T(8,128)S(1)}, u32[]{:S(2)}, u32[]{:S(2)}) collective-permute-start(f32[3,8,256]{2,1,0:T(8,128)S(1)} %shard_map.96), channel_id=1, source_target_pairs={{0,1},{1,0},{2,3},{3,2},{4,5},{5,4},{6,7},{7,6},{8,9},{9,8},{10,11... | collective-permute-start | bytes 73736 | tf_op jit(solution)/shard_map/ppermute | solution.py:388
  12.1 3.9 %collective-permute-start.6 = (f32[3,8,256]{2,1,0:T(8,128)S(1)}, f32[3,8,256]{2,1,0:T(8,128)S(1)}, u32[]{:S(2)}, u32[]{:S(2)}) collective-permute-start(f32[3,8,256]{2,1,0:T(8,128)S(1)} %get-tuple-element.103.refs_1_), channel_id=1, source_target_pairs={{0,3},{1,2},{2,1},{3,0},{4,7},{5,6},{6,5},{7,4},{8,11},{9,10},{10,... | collective-permute-start | bytes 73736 | tf_op jit(solution)/shard_map/ppermute | solution.py:384
  13.4 5.5 %collective-permute-start.7 = (f32[3,32,256]{2,1,0:T(8,128)S(1)}, f32[3,32,256]{2,1,0:T(8,128)S(1)}, u32[]{:S(2)}, u32[]{:S(2)}) collective-permute-start(f32[3,32,256]{2,1,0:T(8,128)S(1)} %shard_map.95.refs_1_), channel_id=1, source_target_pairs={{0,4},{1,5},{2,6},{3,7},{4,0},{5,1},{6,2},{7,3},{8,12},{9,13},{10,... | collective-permute-start | bytes 294920 | tf_op jit(solution)/shard_map/ppermute | solution.py:386
  16.1 6.3 %collective-permute-start.8 = (f32[3,32,256]{2,1,0:T(8,128)S(1)}, f32[3,32,256]{2,1,0:T(8,128)S(1)}, u32[]{:S(2)}, u32[]{:S(2)}) collective-permute-start(f32[3,32,256]{2,1,0:T(8,128)S(1)} %get-tuple-element.116), channel_id=1, source_target_pairs={{0,1},{1,0},{2,3},{3,2},{4,8},{5,9},{6,10},{7,11},{8,4},{9,5},{10,... | collective-permute-start | bytes 294920 | tf_op jit(solution)/shard_map/ppermute | solution.py:381
  19.0 2.9 %collective-permute-start.9 = (f32[3,8,256]{2,1,0:T(8,128)S(1)}, f32[3,8,256]{2,1,0:T(8,128)S(1)}, u32[]{:S(2)}, u32[]{:S(2)}) collective-permute-start(f32[3,8,256]{2,1,0:T(8,128)S(1)} %shard_map.102), channel_id=1, source_target_pairs={{0,1},{1,0},{2,3},{3,2},{4,5},{5,4},{6,7},{7,6},{8,9},{9,8},{10,11... | collective-permute-start | bytes 73736 | tf_op jit(solution)/shard_map/ppermute | solution.py:388
  19.1 3.3 %collective-permute-start.10 = (f32[3,8,256]{2,1,0:T(8,128)S(1)}, f32[3,8,256]{2,1,0:T(8,128)S(1)}, u32[]{:S(2)}, u32[]{:S(2)}) collective-permute-start(f32[3,8,256]{2,1,0:T(8,128)S(1)} %get-tuple-element.119.refs_1_), channel_id=1, source_target_pairs={{0,3},{1,2},{2,1},{3,0},{4,7},{5,6},{6,5},{7,4},{8,11},{9,10},{10,... | collective-permute-start | bytes 73736 | tf_op jit(solution)/shard_map/ppermute | solution.py:384
  19.8 5.1 %collective-permute-start.11 = (f32[3,32,256]{2,1,0:T(8,128)S(1)}, f32[3,32,256]{2,1,0:T(8,128)S(1)}, u32[]{:S(2)}, u32[]{:S(2)}) collective-permute-start(f32[3,32,256]{2,1,0:T(8,128)S(1)} %shard_map.101.refs_1_), channel_id=1, source_target_pairs={{0,4},{1,5},{2,6},{3,7},{4,0},{5,1},{6,2},{7,3},{8,12},{9,13},{10,... | collective-permute-start | bytes 294920 | tf_op jit(solution)/shard_map/ppermute | solution.py:386
  22.4 6.0 %collective-permute-start.12 = (f32[3,32,256]{2,1,0:T(8,128)S(1)}, f32[3,32,256]{2,1,0:T(8,128)S(1)}, u32[]{:S(2)}, u32[]{:S(2)}) collective-permute-start(f32[3,32,256]{2,1,0:T(8,128)S(1)} %get-tuple-element.128), channel_id=1, source_target_pairs={{0,1},{1,0},{2,3},{3,2},{4,8},{5,9},{6,10},{7,11},{8,4},{9,5},{10,... | collective-permute-start | bytes 294920 | tf_op jit(solution)/shard_map/ppermute | solution.py:381
  25.0 3.1 %collective-permute-start.13 = (f32[3,8,256]{2,1,0:T(8,128)S(1)}, f32[3,8,256]{2,1,0:T(8,128)S(1)}, u32[]{:S(2)}, u32[]{:S(2)}) collective-permute-start(f32[3,8,256]{2,1,0:T(8,128)S(1)} %shard_map.108), channel_id=1, source_target_pairs={{0,1},{1,0},{2,3},{3,2},{4,5},{5,4},{6,7},{7,6},{8,9},{9,8},{10,11... | collective-permute-start | bytes 73736 | tf_op jit(solution)/shard_map/ppermute | solution.py:388
  25.1 3.3 %collective-permute-start.14 = (f32[3,8,256]{2,1,0:T(8,128)S(1)}, f32[3,8,256]{2,1,0:T(8,128)S(1)}, u32[]{:S(2)}, u32[]{:S(2)}) collective-permute-start(f32[3,8,256]{2,1,0:T(8,128)S(1)} %get-tuple-element.131.refs_1_), channel_id=1, source_target_pairs={{0,3},{1,2},{2,1},{3,0},{4,7},{5,6},{6,5},{7,4},{8,11},{9,10},{10,... | collective-permute-start | bytes 73736 | tf_op jit(solution)/shard_map/ppermute | solution.py:384
  26.3 4.8 %collective-permute-start.15 = (f32[3,32,256]{2,1,0:T(8,128)S(1)}, f32[3,32,256]{2,1,0:T(8,128)S(1)}, u32[]{:S(2)}, u32[]{:S(2)}) collective-permute-start(f32[3,32,256]{2,1,0:T(8,128)S(1)} %shard_map.107.refs_1_), channel_id=1, source_target_pairs={{0,4},{1,5},{2,6},{3,7},{4,0},{5,1},{6,2},{7,3},{8,12},{9,13},{10,... | collective-permute-start | bytes 294920 | tf_op jit(solution)/shard_map/ppermute | solution.py:386

commit v4 on v3

--- a/solution.py
+++ b/solution.py
@@ -88,17 +88,18 @@
     return lax.axis_index("plane") % 2 == 0
 
 
+def start_copies(moves, sems):
+    copies = [pltpu.make_async_copy(source, target, sems.at[i]) for i, (source, target) in enumerate(moves)]
+    for copy in copies:
+        copy.start()
+    return copies
+
+
 def open_kernel(
     cx, cy, u_hbm, material_hbm, eroded_hbm, table_hbm, a, b, ya, yb, u, material, eroded, table, scalars, edge, sems
 ):
-    copies = [
-        pltpu.make_async_copy(source, target, sems.at[i])
-        for i, (source, target) in enumerate(
-            ((table_hbm, scalars), (material_hbm, material), (eroded_hbm, eroded), (u_hbm, u))
-        )
-    ]
-    for copy in copies:
-        copy.start()
+    moves = [(table_hbm, scalars), (material_hbm, material), (eroded_hbm, eroded)]
+    copies = start_copies(moves + [(u_hbm.at[c], u.at[c]) for c in range(3)], sems)
     copies[0].wait()
     for index in range(table.shape[0]):
         table[index : index + 1, :] = jnp.full((1, table.shape[1]), scalars[index], jnp.float32)
@@ -115,7 +116,8 @@
             put_rows(even, x, i, cells[top, :], cells[end, :], edge.at[0], edge.at[1])
     for side, out in enumerate((ya, yb)):
         out[3] = lookup(edge[side, 0], edge[side, 1], table)
-    copies[3].wait()
+    for copy in copies[3:]:
+        copy.wait()
     for face, out in ((fa, a), (fb, b)):
         at = layer(face, cy)
         for c in range(3):
@@ -129,7 +131,7 @@
     yb[c, x : x + 1, :] = jnp.where(even, first, last)
 
 
-def advance(cx, cy, first, count, u, v, load, stiff, rate, u_out, v_out, halo=None):
+def advance(cx, cy, first, count, u, v, load, stiff, rate, u_out, v_out, halo=None, then=None):
     kx, ky_down, ky_up, kz_down, kz_up, total = stiff
     nz = u.shape[-1]
     row = lax.broadcasted_iota(jnp.int32, (TILE, nz), 0)
@@ -166,6 +168,8 @@
                 speed = speed + r * (force + load[c, at, :] - DRAG * speed)
                 v_out[c, at, :] = speed
                 u_out[c, at, :] = here + r * speed
+        if then is not None:
+            then(i)
 
 
 def edge_kernel(cx, cy, u, v, load, kx, kyd, kyu, kzd, kzu, total, rate, u_out, v_out):
@@ -179,6 +183,30 @@
 def rest_kernel(cx, cy, u1, v, u, load, kx, kyd, kyu, kzd, kzu, total, rate, ya, yb, u_out, v_out):
     stiff = kx, kyd, kyu, kzd, kzu, total
     advance(cx, cy, rest_first(cx), cx - 1, u, v, load, stiff, rate, u_out, v_out, (ya, yb))
+
+
+def rest_kernel_last(
+    cx, cy, u1, v, u, load, kx, kyd, kyu, kzd, kzu, total, rate, ya, yb, u_out, v_out, u_hbm, v_hbm, sems
+):
+    stiff = kx, kyd, kyu, kzd, kzu, total
+    start = jnp.where(sides(cx)[0] == 0, 1, 0)
+    half = (cx - 1) // 2
+    copies = []
+    for i, (begin, size) in enumerate(((start, half), (start + half, cx - 1 - half))):
+        at = pl.ds(pl.multiple_of(begin * cy, cy), size * cy)
+        for j, (source, target) in enumerate(((u_out, u_hbm), (v_out, v_hbm))):
+            copies.append(pltpu.make_async_copy(source.at[:, at, :], target.at[:, at, :], sems.at[2 * i + j]))
+
+    def then(i):
+        if i == half:
+            copies[0].start()
+            copies[1].start()
+
+    advance(cx, cy, rest_first(cx), cx - 1, u, v, load, stiff, rate, u_out, v_out, (ya, yb), then)
+    copies[2].start()
+    copies[3].start()
+    for copy in copies:
+        copy.wait()
 
 
 def rest_kernel_first(
@@ -202,37 +230,37 @@
 
 def prepare_kernel(
     cx, cy, u, material, eroded, table, v_hbm, load_hbm, damaged_hbm,
-    u_out, v_out, load, kx, kyd, kyu, kzd, kzu, total, coarse, fine, damaged, sems,
+    u_out, v_out, load, kx, kyd, kyu, kzd, kzu, total, coarse, fine, damaged, k_all, sems,
 ):
-    copies = [
-        pltpu.make_async_copy(source, target, sems.at[i])
-        for i, (source, target) in enumerate(((damaged_hbm, damaged), (v_hbm, v_out), (load_hbm, load)))
-    ]
-    for copy in copies:
-        copy.start()
+    moves = [(damaged_hbm, damaged)]
+    moves += [(h.at[c], w.at[c]) for c in range(3) for h, w in ((v_hbm, v_out), (load_hbm, load))]
+    copies = start_copies(moves, sems)
     nz = u.shape[-1]
-    row = lax.broadcasted_iota(jnp.int32, (cy, nz), 0)
-    lane = lax.broadcasted_iota(jnp.int32, (cy, nz), 1)
-    nothing = jnp.zeros((cy, nz), jnp.float32)
-
-    def stiffness(x):
-        at = slice(x * cy, (x + 1) * cy)
-        return lookup(material[at, :], eroded[at, :], table) if 0 <= x < cx else nothing
-
-    face, k = nothing, stiffness(0)
-    for x in range(cx):
-        at = slice(x * cy, (x + 1) * cy)
-        y_up = jnp.where(row < cy - 1, jnp.minimum(k, pltpu.roll(k, cy - 1, 0)), 0.0)
-        y_down = jnp.where(row > 0, jnp.minimum(k, pltpu.roll(k, 1, 0)), 0.0)
-        z_up = jnp.where(lane < nz - 1, jnp.minimum(k, pltpu.roll(k, nz - 1, 1)), 0.0)
-        z_down = jnp.where(lane > 0, jnp.minimum(k, pltpu.roll(k, 1, 1)), 0.0)
-        above = stiffness(x + 1)
-        face_up = jnp.minimum(k, above)
-        for out, value in ((kx, face), (kyu, y_up), (kyd, y_down), (kzu, z_up), (kzd, z_down)):
-            out[at, :] = value
-        total[at, :] = ((face + face_up) + (y_up + y_down)) + (z_up + z_down)
-        face, k = face_up, above
-    kx[cx * cy : (cx + 1) * cy, :] = nothing
+    row = lax.broadcasted_iota(jnp.int32, (TILE, nz), 0)
+    lane = lax.broadcasted_iota(jnp.int32, (TILE, nz), 1)
+    nothing = jnp.zeros((TILE, nz), jnp.float32)
+    tiles = cy // TILE
+    for start in range(0, cx * cy, TILE):
+        at = slice(start, start + TILE)
+        k_all[at, :] = lookup(material[at, :], eroded[at, :], table)
+    for t in range(tiles):
+        face = nothing
+        for x in range(cx):
+            start = x * cy + t * TILE
+            at = slice(start, start + TILE)
+            k = k_all[at, :]
+            y_up = k_all[start + TILE : start + TILE + 1, :] if t < tiles - 1 else 0.0
+            y_down = k_all[start - 1 : start, :] if t > 0 else 0.0
+            y_up = jnp.minimum(k, jnp.where(row == TILE - 1, y_up, pltpu.roll(k, TILE - 1, 0)))
+            y_down = jnp.minimum(k, jnp.where(row == 0, y_down, pltpu.roll(k, 1, 0)))
+            z_up = jnp.minimum(k, jnp.where(lane == nz - 1, 0.0, pltpu.roll(k, nz - 1, 1)))
+            z_down = jnp.minimum(k, jnp.where(lane == 0, 0.0, pltpu.roll(k, 1, 1)))
+            face_up = jnp.minimum(k, k_all[start + cy : start + cy + TILE, :]) if x < cx - 1 else nothing
+            for out, value in ((kx, face), (kyu, y_up), (kyd, y_down), (kzu, z_up), (kzd, z_down)):
+                out[at, :] = value
+            total[at, :] = ((face + face_up) + (y_up + y_down)) + (z_up + z_down)
+            face = face_up
+    kx[cx * cy : (cx + 1) * cy, :] = jnp.zeros((cy, nz), jnp.float32)
     copies[0].wait()
     for x in range(cx):
         at = slice(x * cy, (x + 1) * cy)
@@ -333,11 +361,12 @@
     return call(hand_on, [array.shape], (array, other), {0: 0})[0]
 
 
-def last_kernel(cx, cy, u1, v1, u, rate, ha, ka, u_new, v_new, u_out, v_out, sems):
-    fix_face(layer(sides(cx)[0], cy), u, rate, ka[...], ha, u_new, v_new, None)
+def last_kernel(cx, cy, u1, v1, u, rate, ha, ka, u_in, v_in, u_new, v_new, u_hbm, v_hbm, sems):
+    at = layer(sides(cx)[0], cy)
+    fix_face(at, u, rate, ka[...], ha, u_new, v_new, None)
     copies = [
-        pltpu.make_async_copy(u_new, u_out, sems.at[0]),
-        pltpu.make_async_copy(v_new, v_out, sems.at[1]),
+        pltpu.make_async_copy(source.at[:, at, :], target.at[:, at, :], sems.at[i])
+        for i, (source, target) in enumerate(((u_new, u_hbm), (v_new, v_hbm)))
     ]
     for copy in copies:
         copy.start()
@@ -373,7 +402,7 @@
         scratch=[
             pltpu.SMEM(stiff_table.shape, jnp.float32),
             pltpu.VMEM((2, 2, cx, nz), jnp.int32),
-            pltpu.SemaphoreType.DMA((4,)),
+            pltpu.SemaphoreType.DMA((6,)),
         ],
     )
     both = {0: 0, 1: 1}
@@ -392,7 +421,11 @@
                 [field] * 3 + [((cx + 1) * cy, nz)] + [cells] * 7,
                 (u, material, eroded, table),
                 in_hbm=(v, load, damaged),
-                scratch=[pltpu.VMEM(cells, jnp.int32), pltpu.SemaphoreType.DMA((3,))],
+                scratch=[
+                    pltpu.VMEM(cells, jnp.int32),
+                    pltpu.VMEM(cells, jnp.float32),
+                    pltpu.SemaphoreType.DMA((7,)),
+                ],
             )
             rate = coarse
             u_new, v, b_next, kb, k_low, k_high = call(
@@ -422,8 +455,13 @@
                 weight=LONG,
             )
             b_next = None if last else sent[0]
-            u_new, v = call(
-                bind(rest_kernel), [field, field], (u_new, v, u, load, *stiff, rate, hya, hyb), both
+            u_new, v, *done = call(
+                bind(rest_kernel_last if last else rest_kernel),
+                [field, field],
+                (u_new, v, u, load, *stiff, rate, hya, hyb),
+                both,
+                scratch=[pltpu.SemaphoreType.DMA((4,))] if last else (),
+                to_hbm=[field, field] if last else (),
             )
         b = b_next
         if sub == 0:
@@ -440,7 +478,8 @@
         bind(last_kernel),
         [field, field],
         (u_new, v, u, fine, ha, ka),
-        {0: 0, 1: 1},
+        {0: 0, 1: 1, 6: 2, 7: 3},
+        in_hbm=done,
         scratch=[pltpu.SemaphoreType.DMA((2,))],
         to_hbm=[field, field],
     )

time: 32.4 us -> 31.7 us (0.978)
  waiting for transfers between devices: 6.48 us -> 5.71 us
  Pallas kernels: 8.48 us -> 8.95 us
  starting transfers between devices: 16.4 us -> 16 us
    ppermute x4, starting transfers between devices: 5.78 us -> 3.6 us  [per_device(): hyb = lax.ppermute(yb, AXES, pb)]
    ppermute x4, starting transfers between devices: 0.32 us -> 2.48 us  [per_device(): hya = lax.ppermute(ya, AXES, pa)]
    ppermute x4, waiting for transfers between devices: 5.76 us -> 5.2 us  [per_device(): ha = lax.ppermute(a, AXES, xa)]
    pallas_call x26, Pallas kernels: 8.48 us -> 8.95 us  [call(): pl.pallas_call(kernel, in_specs=[VMEM] * len(arrays) + [HBM] * len(in_hbm...]
    ppermute x4, starting transfers between devices: 1.17 us -> 0.73 us  [per_device(): hb = lax.ppermute(b, AXES, xb)]
  transfers between devices with their start and end apart: 16 -> 16, of which waited for: 6 -> 6; matrix products, arithmetic and copies ran while one was open for 0% -> 0% of each run, Pallas kernels for 18% -> 22%
where the time goes in v4:
time: 31.7 us; the launch traced here: 31.5 us
  starting transfers between devices  16 us (50%)
  Pallas kernels  8.95 us (28%)
  waiting for transfers between devices  5.71 us (18%)
  between operations  0.83 us (3%)
    ppermute x4, starting transfers between devices, per_device(): ha = lax.ppermute(a, AXES, xa)  9.21 us
    pallas_call x26, Pallas kernels, call(): pl.pallas_call(kernel, in_specs=[VMEM] * len(arrays) + [HBM] * len(in_hbm...  8.95 us
    ppermute x4, waiting for transfers between devices, per_device(): ha = lax.ppermute(a, AXES, xa)  5.2 us
    ppermute x4, starting transfers between devices, per_device(): hyb = lax.ppermute(yb, AXES, pb)  3.6 us
    ppermute x4, starting transfers between devices, per_device(): hya = lax.ppermute(ya, AXES, pa)  2.48 us
    ppermute x4, starting transfers between devices, per_device(): hb = lax.ppermute(b, AXES, xb)  0.73 us
  transfers between devices with their start and end apart: 16, of which 6 were waited for; matrix products, arithmetic and copies ran while one was open for 0% of the time, Pallas kernels for 22%

profile of v4, /device:TPU:0, one launch (start us, length us, event | category | flops | bytes accessed | tf_op | source)
XLA Modules:
  0.0 31.5 jit_solution(944375324783493211)
XLA Ops:
  0.6 1.4 %shard_map.86 = (f32[4,32,256]{2,1,0:T(8,128)S(1)}, f32[4,32,256]{2,1,0:T(8,128)S(1)}, f32[4,8,256]{2,1,0:T(8,128)S(1)}, f32[4,8,256]{2,1,0:T(8,128)S(1)}, f32[3...) custom-call(f32[3,256,256]{2,1,0:T(8,128)} %bitcast.8, ...), custom_call_target="tpu_custom_call" | custom-call | flops 1 | bytes 1 | tf_op jit(solution)/shard_map/pallas_call | solution.py:58
  2.0 0.5 %collective-permute-start = (f32[4,32,256]{2,1,0:T(8,128)S(1)}, f32[4,32,256]{2,1,0:T(8,128)S(1)}, u32[]{:S(2)}, u32[]{:S(2)}) collective-permute-start(f32[4,32,256]{2,1,0:T(8,128)S(1)} %get-tuple-element.79.refs_1_.b_sent), channel_id=1, source_target_pairs={{0,1},{1,0},{2,3},{3,2},{4,8},{5,9},{6,10},{7,11},{8,4},{9,5},{10,... | collective-permute-start | bytes 393224 | tf_op jit(solution)/shard_map/ppermute | solution.py:410
  2.5 0.1 collective-permute-start.1
  2.7 2.6 %collective-permute-start.2 = (f32[4,8,256]{2,1,0:T(8,128)S(1)}, f32[4,8,256]{2,1,0:T(8,128)S(1)}, u32[]{:S(2)}, u32[]{:S(2)}) collective-permute-start(f32[4,8,256]{2,1,0:T(8,128)S(1)} %shard_map.88.refs_1_.yb_sent), channel_id=1, source_target_pairs={{0,3},{1,2},{2,1},{3,0},{4,7},{5,6},{6,5},{7,4},{8,11},{9,10},{10,... | collective-permute-start | bytes 98312 | tf_op jit(solution)/shard_map/ppermute | solution.py:413
  5.3 2.9 %collective-permute-start.3 = (f32[4,32,256]{2,1,0:T(8,128)S(1)}, f32[4,32,256]{2,1,0:T(8,128)S(1)}, u32[]{:S(2)}, u32[]{:S(2)}) collective-permute-start(f32[4,32,256]{2,1,0:T(8,128)S(1)} %shard_map.89.refs_1_.a_sent), channel_id=1, source_target_pairs={{0,4},{1,5},{2,6},{3,7},{4,0},{5,1},{6,2},{7,3},{8,12},{9,13},{10,... | collective-permute-start | bytes 393224 | tf_op jit(solution)/shard_map/ppermute | solution.py:415
  8.2 1.9 %shard_map.87 = (f32[3,256,256]{2,1,0:T(8,128)S(1)}, f32[3,256,256]{2,1,0:T(8,128)S(1)}, f32[3,256,256]{2,1,0:T(8,128)S(1)}, f32[288,256]{1,0:T(8,128)S(1)}, f32...) custom-call(f32[3,256,256]{2,1,0:T(8,128)S(1)} %get-tuple-element.72, ...), custom_call_target="tpu_custom_call" | custom-call | flops 1 | bytes 1 | tf_op jit(solution)/shard_map/pallas_call | solution.py:58
  10.1 0.0 collective-permute-done.1.ya
  10.1 0.0 collective-permute-done.2.yb
  10.1 0.0 collective-permute-done.hb
  10.1 0.1 shard_map.91
  10.2 0.1 collective-permute-start.4
  10.3 0.8 %shard_map.92 = (f32[3,256,256]{2,1,0:T(8,128)S(1)}, f32[3,256,256]{2,1,0:T(8,128)S(1)}, f32[256,256]{1,0:T(8,128)S(1)}, f32[256,256]{1,0:T(8,128)S(1)}, f32[256,256]{1,0:T(8,128)S(1)}) custom-call(f32[3,256,256]{2,1,0:T(8,128)S(1)} %get-tuple-element.83.u1, ...), custom_call_target="tpu_custom_call", output_to_operand_aliasing={{0}: (0, {}), {1}: (1, {}), {2}: (2, {}), {3}: (3, {}), {4}... | custom-call | flops 1 | bytes 1 | tf_op jit(solution)/shard_map/pallas_call | solution.py:58
  11.1 0.8 %collective-permute-done.3.ha = f32[4,32,256]{2,1,0:T(8,128)S(1)} collective-permute-done((f32[4,32,256]{2,1,0:T(8,128)S(1)}, f32[4,32,256]{2,1,0:T(8,128)S(1)}, u32[]{:S(2)}, u32[]{:S(2)}) %collective-permute-start.3) | collective-permute-done | bytes 131104 | tf_op jit(solution)/shard_map/ppermute | solution.py:415
  11.9 0.1 shard_map.93
  12.0 0.8 %collective-permute-start.6 = (f32[3,8,256]{2,1,0:T(8,128)S(1)}, f32[3,8,256]{2,1,0:T(8,128)S(1)}, u32[]{:S(2)}, u32[]{:S(2)}) collective-permute-start(f32[3,8,256]{2,1,0:T(8,128)S(1)} %get-tuple-element.105.refs_1_), channel_id=1, source_target_pairs={{0,3},{1,2},{2,1},{3,0},{4,7},{5,6},{6,5},{7,4},{8,11},{9,10},{10,... | collective-permute-start | bytes 73736 | tf_op jit(solution)/shard_map/ppermute | solution.py:413
  12.8 0.5 %collective-permute-start.5 = (f32[3,8,256]{2,1,0:T(8,128)S(1)}, f32[3,8,256]{2,1,0:T(8,128)S(1)}, u32[]{:S(2)}, u32[]{:S(2)}) collective-permute-start(f32[3,8,256]{2,1,0:T(8,128)S(1)} %shard_map.96), channel_id=1, source_target_pairs={{0,1},{1,0},{2,3},{3,2},{4,5},{5,4},{6,7},{7,6},{8,9},{9,8},{10,11... | collective-permute-start | bytes 73736 | tf_op jit(solution)/shard_map/ppermute | solution.py:417
  13.3 2.5 %collective-permute-start.7 = (f32[3,32,256]{2,1,0:T(8,128)S(1)}, f32[3,32,256]{2,1,0:T(8,128)S(1)}, u32[]{:S(2)}, u32[]{:S(2)}) collective-permute-start(f32[3,32,256]{2,1,0:T(8,128)S(1)} %shard_map.95.refs_1_), channel_id=1, source_target_pairs={{0,4},{1,5},{2,6},{3,7},{4,0},{5,1},{6,2},{7,3},{8,12},{9,13},{10,... | collective-permute-start | bytes 294920 | tf_op jit(solution)/shard_map/ppermute | solution.py:415
  15.8 0.1 shard_map.94
  15.9 0.0 collective-permute-done.6.yb
  15.9 0.0 collective-permute-done.5.ya
  16.0 0.0 collective-permute-done.4.hb
  16.0 0.1 shard_map.97
  16.0 0.1 collective-permute-start.8
  16.1 0.8 %shard_map.98 = (f32[3,256,256]{2,1,0:T(8,128)S(1)}, f32[3,256,256]{2,1,0:T(8,128)S(1)}) custom-call(f32[3,256,256]{2,1,0:T(8,128)S(1)} %get-tuple-element.109.u1, f32[3,256,256]{2,1,0:T(8,128)S(1)} %get-tuple-element.110.v, f32[3,256,256]{2,1,0:T(8,128)S(1)} %get-tuple-element.94.u, ...), custom_call_target="tpu_custom_call", output_to_operand_aliasing={{0}: (0, {}), {1}: (1, {})} | custom-call | flops 1 | bytes 1 | tf_op jit(solution)/shard_map/pallas_call | solution.py:58
  16.9 1.9 %collective-permute-done.7.ha = f32[3,32,256]{2,1,0:T(8,128)S(1)} collective-permute-done((f32[3,32,256]{2,1,0:T(8,128)S(1)}, f32[3,32,256]{2,1,0:T(8,128)S(1)}, u32[]{:S(2)}, u32[]{:S(2)}) %collective-permute-start.7) | collective-permute-done | bytes 98336 | tf_op jit(solution)/shard_map/ppermute | solution.py:415
  18.8 0.1 shard_map.99
  18.9 0.1 collective-permute-start.10
  19.0 0.7 %collective-permute-start.9 = (f32[3,8,256]{2,1,0:T(8,128)S(1)}, f32[3,8,256]{2,1,0:T(8,128)S(1)}, u32[]{:S(2)}, u32[]{:S(2)}) collective-permute-start(f32[3,8,256]{2,1,0:T(8,128)S(1)} %shard_map.102), channel_id=1, source_target_pairs={{0,1},{1,0},{2,3},{3,2},{4,5},{5,4},{6,7},{7,6},{8,9},{9,8},{10,11... | collective-permute-start | bytes 73736 | tf_op jit(solution)/shard_map/ppermute | solution.py:417
  19.7 2.1 %collective-permute-start.11 = (f32[3,32,256]{2,1,0:T(8,128)S(1)}, f32[3,32,256]{2,1,0:T(8,128)S(1)}, u32[]{:S(2)}, u32[]{:S(2)}) collective-permute-start(f32[3,32,256]{2,1,0:T(8,128)S(1)} %shard_map.101.refs_1_), channel_id=1, source_target_pairs={{0,4},{1,5},{2,6},{3,7},{4,0},{5,1},{6,2},{7,3},{8,12},{9,13},{10,... | collective-permute-start | bytes 294920 | tf_op jit(solution)/shard_map/ppermute | solution.py:415
  21.7 0.1 shard_map.100
  21.9 0.3 %collective-permute-done.10.yb = f32[3,8,256]{2,1,0:T(8,128)S(1)} collective-permute-done((f32[3,8,256]{2,1,0:T(8,128)S(1)}, f32[3,8,256]{2,1,0:T(8,128)S(1)}, u32[]{:S(2)}, u32[]{:S(2)}) %collective-permute-start.10) | collective-permute-done | bytes 24608 | tf_op jit(solution)/shard_map/ppermute | solution.py:413
  22.2 0.0 collective-permute-done.9.ya
  22.2 0.0 collective-permute-done.8.hb
  22.2 0.1 shard_map.103
  22.3 0.1 collective-permute-start.12
  22.4 0.8 %shard_map.104 = (f32[3,256,256]{2,1,0:T(8,128)S(1)}, f32[3,256,256]{2,1,0:T(8,128)S(1)}) custom-call(f32[3,256,256]{2,1,0:T(8,128)S(1)} %get-tuple-element.122.u1, f32[3,256,256]{2,1,0:T(8,128)S(1)} %get-tuple-element.123.v, f32[3,256,256]{2,1,0:T(8,128)S(1)} %get-tuple-element.114.u, ...), custom_call_target="tpu_custom_call", output_to_operand_aliasing={{0}: (0, {}), {1}: (1, {})} | custom-call | flops 1 | bytes 1 | tf_op jit(solution)/shard_map/pallas_call | solution.py:58
  23.1 1.6 %collective-permute-done.11.ha = f32[3,32,256]{2,1,0:T(8,128)S(1)} collective-permute-done((f32[3,32,256]{2,1,0:T(8,128)S(1)}, f32[3,32,256]{2,1,0:T(8,128)S(1)}, u32[]{:S(2)}, u32[]{:S(2)}) %collective-permute-start.11) | collective-permute-done | bytes 98336 | tf_op jit(solution)/shard_map/ppermute | solution.py:415
  24.7 0.1 shard_map.105
  24.8 0.1 collective-permute-start.14
  24.9 1.2 %collective-permute-start.13 = (f32[3,8,256]{2,1,0:T(8,128)S(1)}, f32[3,8,256]{2,1,0:T(8,128)S(1)}, u32[]{:S(2)}, u32[]{:S(2)}) collective-permute-start(f32[3,8,256]{2,1,0:T(8,128)S(1)} %shard_map.108), channel_id=1, source_target_pairs={{0,1},{1,0},{2,3},{3,2},{4,5},{5,4},{6,7},{7,6},{8,9},{9,8},{10,11... | collective-permute-start | bytes 73736 | tf_op jit(solution)/shard_map/ppermute | solution.py:417
  26.1 1.7 %collective-permute-start.15 = (f32[3,32,256]{2,1,0:T(8,128)S(1)}, f32[3,32,256]{2,1,0:T(8,128)S(1)}, u32[]{:S(2)}, u32[]{:S(2)}) collective-permute-start(f32[3,32,256]{2,1,0:T(8,128)S(1)} %shard_map.107.refs_1_), channel_id=1, source_target_pairs={{0,4},{1,5},{2,6},{3,7},{4,0},{5,1},{6,2},{7,3},{8,12},{9,13},{10,... | collective-permute-start | bytes 294920 | tf_op jit(solution)/shard_map/ppermute | solution.py:415
  27.8 0.1 shard_map.106
  28.0 0.1 collective-permute-done.14.yb
  28.1 0.0 collective-permute-done.13.ya
  28.1 0.0 collective-permute-done.12.hb
  28.1 0.1 shard_map.109
  28.2 1.7 %shard_map.110 = (f32[3,256,256]{2,1,0:T(8,128)S(1)}, f32[3,256,256]{2,1,0:T(8,128)S(1)}, f32[3,256,256]{2,1,0:T(8,128)}, f32[3,256,256]{2,1,0:T(8,128)}) custom-call(f32[3,256,256]{2,1,0:T(8,128)S(1)} %get-tuple-element.134.u1, f32[3,256,256]{2,1,0:T(8,128)S(1)} %get-tuple-element.135.v, ...), custom_call_target="tpu_custom_call", output_to_operand_aliasing={{0}: (0, {}), {1}: (1, {})} | custom-call | flops 1 | bytes 1 | tf_op jit(solution)/shard_map/pallas_call | solution.py:58
  29.8 0.9 %collective-permute-done.15.ha = f32[3,32,256]{2,1,0:T(8,128)S(1)} collective-permute-done((f32[3,32,256]{2,1,0:T(8,128)S(1)}, f32[3,32,256]{2,1,0:T(8,128)S(1)}, u32[]{:S(2)}, u32[]{:S(2)}) %collective-permute-start.15) | collective-permute-done | bytes 98336 | tf_op jit(solution)/shard_map/ppermute | solution.py:415
  30.8 0.7 %shard_map.111 = (f32[3,256,256]{2,1,0:T(8,128)S(1)}, f32[3,256,256]{2,1,0:T(8,128)S(1)}, f32[3,256,256]{2,1,0:T(8,128)}, f32[3,256,256]{2,1,0:T(8,128)}) custom-call(f32[3,256,256]{2,1,0:T(8,128)S(1)} %get-tuple-element.136.u1, f32[3,256,256]{2,1,0:T(8,128)S(1)} %get-tuple-element.137.v1, ...), custom_call_target="tpu_custom_call", output_to_operand_aliasing={{0}: (0, {}), {1}: (1, {}), {2}: (6, {}), {3}: (7, {})} | custom-call | flops 1 | bytes 1 | tf_op jit(solution)/shard_map/pallas_call | solution.py:58
  (9 shorter events, 0.0 us)
Async XLA Ops:
  2.0 8.1 %collective-permute-start = (f32[4,32,256]{2,1,0:T(8,128)S(1)}, f32[4,32,256]{2,1,0:T(8,128)S(1)}, u32[]{:S(2)}, u32[]{:S(2)}) collective-permute-start(f32[4,32,256]{2,1,0:T(8,128)S(1)} %get-tuple-element.79.refs_1_.b_sent), channel_id=1, source_target_pairs={{0,1},{1,0},{2,3},{3,2},{4,8},{5,9},{6,10},{7,11},{8,4},{9,5},{10,... | collective-permute-start | bytes 393224 | tf_op jit(solution)/shard_map/ppermute | solution.py:410
  2.5 7.5 %collective-permute-start.1 = (f32[4,8,256]{2,1,0:T(8,128)S(1)}, f32[4,8,256]{2,1,0:T(8,128)S(1)}, u32[]{:S(2)}, u32[]{:S(2)}) collective-permute-start(f32[4,8,256]{2,1,0:T(8,128)S(1)} %shard_map.90.ya_sent), channel_id=1, source_target_pairs={{0,1},{1,0},{2,3},{3,2},{4,5},{5,4},{6,7},{7,6},{8,9},{9,8},{10,11... | collective-permute-start | bytes 98312 | tf_op jit(solution)/shard_map/ppermute | solution.py:417
  2.7 7.4 %collective-permute-start.2 = (f32[4,8,256]{2,1,0:T(8,128)S(1)}, f32[4,8,256]{2,1,0:T(8,128)S(1)}, u32[]{:S(2)}, u32[]{:S(2)}) collective-permute-start(f32[4,8,256]{2,1,0:T(8,128)S(1)} %shard_map.88.refs_1_.yb_sent), channel_id=1, source_target_pairs={{0,3},{1,2},{2,1},{3,0},{4,7},{5,6},{6,5},{7,4},{8,11},{9,10},{10,... | collective-permute-start | bytes 98312 | tf_op jit(solution)/shard_map/ppermute | solution.py:413
  5.3 6.6 %collective-permute-start.3 = (f32[4,32,256]{2,1,0:T(8,128)S(1)}, f32[4,32,256]{2,1,0:T(8,128)S(1)}, u32[]{:S(2)}, u32[]{:S(2)}) collective-permute-start(f32[4,32,256]{2,1,0:T(8,128)S(1)} %shard_map.89.refs_1_.a_sent), channel_id=1, source_target_pairs={{0,4},{1,5},{2,6},{3,7},{4,0},{5,1},{6,2},{7,3},{8,12},{9,13},{10,... | collective-permute-start | bytes 393224 | tf_op jit(solution)/shard_map/ppermute | solution.py:415
  10.2 5.8 %collective-permute-start.4 = (f32[3,32,256]{2,1,0:T(8,128)S(1)}, f32[3,32,256]{2,1,0:T(8,128)S(1)}, u32[]{:S(2)}, u32[]{:S(2)}) collective-permute-start(f32[3,32,256]{2,1,0:T(8,128)S(1)} %get-tuple-element.102), channel_id=1, source_target_pairs={{0,1},{1,0},{2,3},{3,2},{4,8},{5,9},{6,10},{7,11},{8,4},{9,5},{10,... | collective-permute-start | bytes 294920 | tf_op jit(solution)/shard_map/ppermute | solution.py:410
  12.0 3.9 %collective-permute-start.6 = (f32[3,8,256]{2,1,0:T(8,128)S(1)}, f32[3,8,256]{2,1,0:T(8,128)S(1)}, u32[]{:S(2)}, u32[]{:S(2)}) collective-permute-start(f32[3,8,256]{2,1,0:T(8,128)S(1)} %get-tuple-element.105.refs_1_), channel_id=1, source_target_pairs={{0,3},{1,2},{2,1},{3,0},{4,7},{5,6},{6,5},{7,4},{8,11},{9,10},{10,... | collective-permute-start | bytes 73736 | tf_op jit(solution)/shard_map/ppermute | solution.py:413
  12.8 3.1 %collective-permute-start.5 = (f32[3,8,256]{2,1,0:T(8,128)S(1)}, f32[3,8,256]{2,1,0:T(8,128)S(1)}, u32[]{:S(2)}, u32[]{:S(2)}) collective-permute-start(f32[3,8,256]{2,1,0:T(8,128)S(1)} %shard_map.96), channel_id=1, source_target_pairs={{0,1},{1,0},{2,3},{3,2},{4,5},{5,4},{6,7},{7,6},{8,9},{9,8},{10,11... | collective-permute-start | bytes 73736 | tf_op jit(solution)/shard_map/ppermute | solution.py:417
  13.3 5.5 %collective-permute-start.7 = (f32[3,32,256]{2,1,0:T(8,128)S(1)}, f32[3,32,256]{2,1,0:T(8,128)S(1)}, u32[]{:S(2)}, u32[]{:S(2)}) collective-permute-start(f32[3,32,256]{2,1,0:T(8,128)S(1)} %shard_map.95.refs_1_), channel_id=1, source_target_pairs={{0,4},{1,5},{2,6},{3,7},{4,0},{5,1},{6,2},{7,3},{8,12},{9,13},{10,... | collective-permute-start | bytes 294920 | tf_op jit(solution)/shard_map/ppermute | solution.py:415
  16.0 6.2 %collective-permute-start.8 = (f32[3,32,256]{2,1,0:T(8,128)S(1)}, f32[3,32,256]{2,1,0:T(8,128)S(1)}, u32[]{:S(2)}, u32[]{:S(2)}) collective-permute-start(f32[3,32,256]{2,1,0:T(8,128)S(1)} %get-tuple-element.118), channel_id=1, source_target_pairs={{0,1},{1,0},{2,3},{3,2},{4,8},{5,9},{6,10},{7,11},{8,4},{9,5},{10,... | collective-permute-start | bytes 294920 | tf_op jit(solution)/shard_map/ppermute | solution.py:410
  18.9 3.3 %collective-permute-start.10 = (f32[3,8,256]{2,1,0:T(8,128)S(1)}, f32[3,8,256]{2,1,0:T(8,128)S(1)}, u32[]{:S(2)}, u32[]{:S(2)}) collective-permute-start(f32[3,8,256]{2,1,0:T(8,128)S(1)} %get-tuple-element.121.refs_1_), channel_id=1, source_target_pairs={{0,3},{1,2},{2,1},{3,0},{4,7},{5,6},{6,5},{7,4},{8,11},{9,10},{10,... | collective-permute-start | bytes 73736 | tf_op jit(solution)/shard_map/ppermute | solution.py:413
  19.0 3.2 %collective-permute-start.9 = (f32[3,8,256]{2,1,0:T(8,128)S(1)}, f32[3,8,256]{2,1,0:T(8,128)S(1)}, u32[]{:S(2)}, u32[]{:S(2)}) collective-permute-start(f32[3,8,256]{2,1,0:T(8,128)S(1)} %shard_map.102), channel_id=1, source_target_pairs={{0,1},{1,0},{2,3},{3,2},{4,5},{5,4},{6,7},{7,6},{8,9},{9,8},{10,11... | collective-permute-start | bytes 73736 | tf_op jit(solution)/shard_map/ppermute | solution.py:417
  19.7 5.0 %collective-permute-start.11 = (f32[3,32,256]{2,1,0:T(8,128)S(1)}, f32[3,32,256]{2,1,0:T(8,128)S(1)}, u32[]{:S(2)}, u32[]{:S(2)}) collective-permute-start(f32[3,32,256]{2,1,0:T(8,128)S(1)} %shard_map.101.refs_1_), channel_id=1, source_target_pairs={{0,4},{1,5},{2,6},{3,7},{4,0},{5,1},{6,2},{7,3},{8,12},{9,13},{10,... | collective-permute-start | bytes 294920 | tf_op jit(solution)/shard_map/ppermute | solution.py:415
  22.3 5.8 %collective-permute-start.12 = (f32[3,32,256]{2,1,0:T(8,128)S(1)}, f32[3,32,256]{2,1,0:T(8,128)S(1)}, u32[]{:S(2)}, u32[]{:S(2)}) collective-permute-start(f32[3,32,256]{2,1,0:T(8,128)S(1)} %get-tuple-element.130), channel_id=1, source_target_pairs={{0,1},{1,0},{2,3},{3,2},{4,8},{5,9},{6,10},{7,11},{8,4},{9,5},{10,... | collective-permute-start | bytes 294920 | tf_op jit(solution)/shard_map/ppermute | solution.py:410
  24.8 3.3 %collective-permute-start.14 = (f32[3,8,256]{2,1,0:T(8,128)S(1)}, f32[3,8,256]{2,1,0:T(8,128)S(1)}, u32[]{:S(2)}, u32[]{:S(2)}) collective-permute-start(f32[3,8,256]{2,1,0:T(8,128)S(1)} %get-tuple-element.133.refs_1_), channel_id=1, source_target_pairs={{0,3},{1,2},{2,1},{3,0},{4,7},{5,6},{6,5},{7,4},{8,11},{9,10},{10,... | collective-permute-start | bytes 73736 | tf_op jit(solution)/shard_map/ppermute | solution.py:413
  24.9 3.2 %collective-permute-start.13 = (f32[3,8,256]{2,1,0:T(8,128)S(1)}, f32[3,8,256]{2,1,0:T(8,128)S(1)}, u32[]{:S(2)}, u32[]{:S(2)}) collective-permute-start(f32[3,8,256]{2,1,0:T(8,128)S(1)} %shard_map.108), channel_id=1, source_target_pairs={{0,1},{1,0},{2,3},{3,2},{4,5},{5,4},{6,7},{7,6},{8,9},{9,8},{10,11... | collective-permute-start | bytes 73736 | tf_op jit(solution)/shard_map/ppermute | solution.py:417
  26.1 4.7 %collective-permute-start.15 = (f32[3,32,256]{2,1,0:T(8,128)S(1)}, f32[3,32,256]{2,1,0:T(8,128)S(1)}, u32[]{:S(2)}, u32[]{:S(2)}) collective-permute-start(f32[3,32,256]{2,1,0:T(8,128)S(1)} %shard_map.107.refs_1_), channel_id=1, source_target_pairs={{0,4},{1,5},{2,6},{3,7},{4,0},{5,1},{6,2},{7,3},{8,12},{9,13},{10,... | collective-permute-start | bytes 294920 | tf_op jit(solution)/shard_map/ppermute | solution.py:415

commit v5 on v4

--- a/solution.py
+++ b/solution.py
@@ -131,7 +131,7 @@
     yb[c, x : x + 1, :] = jnp.where(even, first, last)
 
 
-def advance(cx, cy, first, count, u, v, load, stiff, rate, u_out, v_out, halo=None, then=None):
+def advance(cx, cy, first, count, u, v, load, stiff, rate, u_out, v_out, halo=None, then=None, tiles=None):
     kx, ky_down, ky_up, kz_down, kz_up, total = stiff
     nz = u.shape[-1]
     row = lax.broadcasted_iota(jnp.int32, (TILE, nz), 0)
@@ -142,7 +142,7 @@
 
     for i in range(count):
         x = first + i
-        for t in range(cy // TILE):
+        for t in tiles if tiles is not None else range(cy // TILE):
             at = tile(x, t)
             x_down, x_up = tile(jnp.maximum(x - 1, 0), t), tile(jnp.minimum(x + 1, cx - 1), t)
             r = rate[at, :]
@@ -172,17 +172,31 @@
             then(i)
 
 
-def edge_kernel(cx, cy, u, v, load, kx, kyd, kyu, kzd, kzu, total, rate, u_out, v_out):
-    advance(cx, cy, sides(cx)[1], 1, u, v, load, (kx, kyd, kyu, kzd, kzu, total), rate, u_out, v_out)
-
-
 def rest_first(cx):
     return jnp.where(sides(cx)[1] == 0, 1, 0)
 
 
-def rest_kernel(cx, cy, u1, v, u, load, kx, kyd, kyu, kzd, kzu, total, rate, ya, yb, u_out, v_out):
+def advance_inner(cx, cy, u, v, load, stiff, rate, u_out, v_out):
+    advance(cx, cy, sides(cx)[1], 1, u, v, load, stiff, rate, u_out, v_out)
+    inner = range(1, cy // TILE - 1)
+    advance(cx, cy, rest_first(cx), cx - 1, u, v, load, stiff, rate, u_out, v_out, tiles=inner)
+
+
+def advance_outer(cx, cy, u, v, load, stiff, rate, u_out, v_out, halo, then=None):
+    outer = sorted({0, cy // TILE - 1})
+    advance(cx, cy, rest_first(cx), cx - 1, u, v, load, stiff, rate, u_out, v_out, halo, then, outer)
+
+
+def edge_kernel(cx, cy, u, v, load, kx, kyd, kyu, kzd, kzu, total, rate, u_out, v_out):
+    advance_inner(cx, cy, u, v, load, (kx, kyd, kyu, kzd, kzu, total), rate, u_out, v_out)
+
+
+def rest_kernel(
+    cx, cy, u1, v, u, load, kx, kyd, kyu, kzd, kzu, total, rate, ya, yb, u_out, v_out, ya_send, yb_send
+):
     stiff = kx, kyd, kyu, kzd, kzu, total
-    advance(cx, cy, rest_first(cx), cx - 1, u, v, load, stiff, rate, u_out, v_out, (ya, yb))
+    advance_outer(cx, cy, u, v, load, stiff, rate, u_out, v_out, (ya, yb))
+    pack_rows(cx, cy, u_out, ya_send, yb_send)
 
 
 def rest_kernel_last(
@@ -202,7 +216,7 @@
             copies[0].start()
             copies[1].start()
 
-    advance(cx, cy, rest_first(cx), cx - 1, u, v, load, stiff, rate, u_out, v_out, (ya, yb), then)
+    advance_outer(cx, cy, u, v, load, stiff, rate, u_out, v_out, (ya, yb), then)
     copies[2].start()
     copies[3].start()
     for copy in copies:
@@ -210,8 +224,8 @@
 
 
 def rest_kernel_first(
-    cx, cy, u1, v, kyd, kyu, total, u, load, kx, kzd, kzu, rate, ya, yb, ya_sent, yb_sent,
-    u_out, v_out, kyd_out, kyu_out, total_out,
+    cx, cy, u1, v, kyd, kyu, total, u, load, kx, kzd, kzu, rate, fine, ya, yb, ya_sent, yb_sent,
+    u_out, v_out, kyd_out, kyu_out, total_out, ya_send, yb_send,
 ):
     low, high = row_stiffness(ya_sent, yb_sent, ya, yb)
     row = lax.broadcasted_iota(jnp.int32, (TILE, u.shape[-1]), 0)
@@ -225,7 +239,8 @@
             out[at, :] += extra
             total_out[at, :] += extra
     stiff = kx, kyd_out, kyu_out, kzd, kzu, total_out
-    advance(cx, cy, rest_first(cx), cx - 1, u, v, load, stiff, rate, u_out, v_out, (ya, yb))
+    advance_outer(cx, cy, u, v, load, stiff, rate, u_out, v_out, (ya, yb))
+    pack_rows(cx, cy, u_out, ya_send, yb_send, fine)
 
 
 def prepare_kernel(
@@ -270,18 +285,18 @@
     for copy in copies[1:]:
         copy.wait()
     stiff = kx, kyd, kyu, kzd, kzu, total
-    advance(cx, cy, sides(cx)[1], 1, u, v_out, load, stiff, coarse, u_out, v_out)
-
-
-def fix_face(at, u, rate, k, halo, u_new, v_new, send):
+    advance_inner(cx, cy, u, v_out, load, stiff, coarse, u_out, v_out)
+
+
+def fix_face(at, u, rate, k, halo, u_new, v_new, put=None):
     r = rate[at, :]
     for c in range(3):
-        push = r * (k * (halo[c] - u[c, at, :]))
+        push = r * (k * (halo(c) - u[c, at, :]))
         v_new[c, at, :] += push
         moved = u_new[c, at, :] + r * push
         u_new[c, at, :] = moved
-        if send is not None:
-            send[c] = moved
+        if put is not None:
+            put(c, moved)
 
 
 def fix_rows(cy, x, u, rate, k_low, k_high, ya, yb, u_new, v_new):
@@ -297,12 +312,15 @@
             u_new[c, at, :] += r * push
 
 
-def pack_rows(cx, cy, u_new, ya_send, yb_send):
+def pack_rows(cx, cy, u_new, ya_send, yb_send, cells=None):
     even = plane_even()
-    for c in range(3):
+    for c in range(3 if cells is None else 4):
         for x in range(cx):
-            first = u_new[c, x * cy : x * cy + TILE, :]
-            last = u_new[c, (x + 1) * cy - TILE : (x + 1) * cy, :]
+            top, end = slice(x * cy, x * cy + TILE), slice((x + 1) * cy - TILE, (x + 1) * cy)
+            if c < 3:
+                first, last = u_new[c, top, :], u_new[c, end, :]
+            else:
+                first, last = cells[top, :], cells[end, :]
             put_rows(even, x, c, first, last, ya_send, yb_send)
 
 
@@ -333,24 +351,114 @@
     fix_b(cx, cy, u1, v1, u, rate, hb, ya, yb, kb, k_low, k_high, u_new, v_new, send)
 
 
-def fix_a_first(cx, cy, u1, v1, u, rate, ha, a_sent, u_new, v_new, send, ya_send, yb_send, ka):
-    ka[...] = face_stiffness(a_sent, ha, False)
-    fix_a(cx, cy, u1, v1, u, rate, ha, ka, u_new, v_new, send, ya_send, yb_send)
-
-
-def fix_b(cx, cy, u1, v1, u, rate, hb, ya, yb, kb, k_low, k_high, u_new, v_new, send):
+def fix_b(cx, cy, u1, v1, u, rate, hb, ya, yb, kb, k_low, k_high, u_new, v_new, send=None):
     face = sides(cx)[1]
     fix_rows(cy, face, u, rate, k_low, k_high, ya, yb, u_new, v_new)
-    fix_face(layer(face, cy), u, rate, kb[...], hb, u_new, v_new, send)
-
-
-def fix_b_last(cx, cy, u1, v1, u, rate, hb, ya, yb, kb, k_low, k_high, u_new, v_new):
-    fix_b(cx, cy, u1, v1, u, rate, hb, ya, yb, kb, k_low, k_high, u_new, v_new, None)
-
-
-def fix_a(cx, cy, u1, v1, u, rate, ha, ka, u_new, v_new, send, ya_send, yb_send):
-    fix_face(layer(sides(cx)[0], cy), u, rate, ka[...], ha, u_new, v_new, send)
-    pack_rows(cx, cy, u_new, ya_send, yb_send)
+
+    def put(c, moved):
+        if send is not None:
+            send[c] = moved
+
+    fix_face(layer(face, cy), u, rate, kb[...], lambda c: hb[c], u_new, v_new, put)
+
+
+def put_face(cy, send):
+    def put(c, moved):
+        send[c * cy : (c + 1) * cy, :] = moved
+
+    return put
+
+
+def put_halos(cy, x, ya, yb, send):
+    for c in range(4):
+        if c < ya.shape[0]:
+            rows = halo_rows(ya, yb, c, x)
+        else:
+            rows = [jnp.zeros((1, send.shape[1]), jnp.float32)] * 2
+        for side in range(2):
+            at = 3 * cy + 4 * side + c
+            send[at : at + 1, :] = rows[side]
+
+
+def halo_rows(ya, yb, c, x):
+    even = plane_even()
+    one, two = ya[c, pl.ds(x, 1), :], yb[c, pl.ds(x, 1), :]
+    return jnp.where(even, two, one), jnp.where(even, one, two)
+
+
+def coarse_of(fine):
+    return COARSE + (FINE - COARSE) / FINE * fine
+
+
+def correct(cx, cy, step, rate, ha, ya, yb, kyd, kyu, old_ya, old_yb, state, u_new, v_new, state_out):
+    face = sides(cx)[0]
+    row = lax.broadcasted_iota(jnp.int32, (TILE, rate.shape[1]), 0)
+    for side in range(2):
+        def sent(f, base=3 * cy + 4 * side):
+            return ha[base + f : base + f + 1, :]
+
+        def kept(f, side=side):
+            return state[side, f : f + 1, :]
+
+        if step == 1:
+            k = jnp.minimum(halo_rows(old_ya, old_yb, 3, face)[side], sent(3)) * flag("slab", False)
+            mine = halo_rows(ya, yb, 3, face)[side]
+            other = jnp.zeros_like(mine)
+            scale = coarse_of(mine) * coarse_of(mine) * k
+        else:
+            k, mine = kept(9), kept(10)
+            other = sent(3) if step == 2 else kept(11)
+            scale = mine * mine * k
+            pace = coarse_of(other) if step == 2 else other
+            pace = pace * pace * k
+        start = face * cy if side == 0 else (face + 1) * cy - TILE
+        at = pl.ds(pl.multiple_of(start, TILE), TILE)
+        edge_k = jnp.where(row == (0 if side == 0 else TILE - 1), (kyd if side == 0 else kyu)[at, :], 0.0)
+        r = rate[at, :]
+        for c in range(3):
+            if step == 1:
+                before, across = halo_rows(old_ya, old_yb, c, face)[side], sent(c)
+            else:
+                before = kept(c)
+                across = sent(c) + pace * (kept(3 + c) - kept(6 + c))
+            late = scale * (across - before)
+            push = r * (edge_k * late)
+            v_new[c, at, :] += push
+            u_new[c, at, :] += r * push
+            if state_out is not None:
+                now = halo_rows(ya, yb, c, face)[side] + late
+                for f, value in ((c, now), (3 + c, before), (6 + c, across)):
+                    state_out[side, f : f + 1, :] = value
+        if state_out is not None:
+            for f, value in ((9, k), (10, mine), (11, other)):
+                state_out[side, f : f + 1, :] = value
+
+
+def fix_a_first(cx, cy, u1, v1, u, rate, ha, a_sent, ya, yb, u_new, v_new, send, ka):
+    ka[...] = face_stiffness(a_sent, ha, False)
+    face = sides(cx)[0]
+    put_halos(cy, face, ya, yb, send)
+    fix_face(layer(face, cy), u, rate, ka[...], lambda c: ha[c], u_new, v_new, put_face(cy, send))
+
+
+def fix_a_second(
+    cx, cy, u1, v1, u, rate, ha, ka, ya, yb, kyd, kyu, old_ya, old_yb, u_new, v_new, send, state_out
+):
+    correct(cx, cy, 1, rate, ha, ya, yb, kyd, kyu, old_ya, old_yb, None, u_new, v_new, state_out)
+    finish_a(cx, cy, u, rate, ha, ka, ya, yb, u_new, v_new, send)
+
+
+def fix_a_third(cx, cy, u1, v1, u, rate, ha, ka, ya, yb, kyd, kyu, state, u_new, v_new, send, state_out):
+    correct(cx, cy, 2, rate, ha, ya, yb, kyd, kyu, None, None, state, u_new, v_new, state_out)
+    finish_a(cx, cy, u, rate, ha, ka, ya, yb, u_new, v_new, send)
+
+
+def finish_a(cx, cy, u, rate, ha, ka, ya, yb, u_new, v_new, send):
+    face = sides(cx)[0]
+    put_halos(cy, face, ya, yb, send)
+    fix_face(
+        layer(face, cy), u, rate, ka[...], lambda c: ha[c * cy : (c + 1) * cy, :], u_new, v_new, put_face(cy, send)
+    )
 
 
 def hand_on(*refs):
@@ -361,9 +469,12 @@
     return call(hand_on, [array.shape], (array, other), {0: 0})[0]
 
 
-def last_kernel(cx, cy, u1, v1, u, rate, ha, ka, u_in, v_in, u_new, v_new, u_hbm, v_hbm, sems):
+def last_kernel(
+    cx, cy, u1, v1, u, rate, ha, ka, ya, yb, kyd, kyu, state, u_in, v_in, u_new, v_new, u_hbm, v_hbm, sems
+):
     at = layer(sides(cx)[0], cy)
-    fix_face(at, u, rate, ka[...], ha, u_new, v_new, None)
+    correct(cx, cy, 3, rate, ha, ya, yb, kyd, kyu, None, None, state, u_new, v_new, None)
+    fix_face(at, u, rate, ka[...], lambda c: ha[c * cy : (c + 1) * cy, :], u_new, v_new)
     copies = [
         pltpu.make_async_copy(source.at[:, at, :], target.at[:, at, :], sems.at[i])
         for i, (source, target) in enumerate(((u_new, u_hbm), (v_new, v_hbm)))
@@ -411,9 +522,9 @@
         if sub == 0:
             yb = after(yb, b)
         hyb = lax.ppermute(yb, AXES, pb)
-        a = after(a, yb)
+        if sub == 0:
+            a = after(a, yb)
         ha = lax.ppermute(a, AXES, xa)
-        ya = after(ya, a)
         hya = lax.ppermute(ya, AXES, pa)
         if sub == 0:
             u_new, v, load, kx, kyd, kyu, kzd, kzu, total, coarse, fine = call(
@@ -436,10 +547,10 @@
                 weight=LONG,
                 scratch=[pltpu.VMEM((2, cx, nz), jnp.float32)],
             )
-            u_new, v, kyd, kyu, total = call(
+            u_new, v, kyd, kyu, total, *sides_next = call(
                 bind(rest_kernel_first),
-                [field, field] + [cells] * 3,
-                (u_new, v, kyd, kyu, total, u, load, kx, kzd, kzu, rate, hya, hyb, ya, yb),
+                [field, field] + [cells] * 3 + [(4, cx, nz)] * 2,
+                (u_new, v, kyd, kyu, total, u, load, kx, kzd, kzu, rate, fine, hya, hyb, ya, yb),
                 {i: i for i in range(5)},
             )
         else:
@@ -448,38 +559,48 @@
             u_new, v = call(bind(edge_kernel), [field, field], (u, v, load, *stiff, rate), {1: 1})
             last = sub == SUBSTEPS - 1
             u_new, v, *sent = call(
-                bind(fix_b_last if last else fix_b),
+                bind(fix_b),
                 [field, field] if last else [field, field, face],
                 (u_new, v, u, rate, hb, hya, hyb, kb, k_low, k_high),
                 both,
                 weight=LONG,
             )
             b_next = None if last else sent[0]
-            u_new, v, *done = call(
+            u_new, v, *rest = call(
                 bind(rest_kernel_last if last else rest_kernel),
-                [field, field],
+                [field, field] if last else [field, field, side, side],
                 (u_new, v, u, load, *stiff, rate, hya, hyb),
                 both,
                 scratch=[pltpu.SemaphoreType.DMA((4,))] if last else (),
                 to_hbm=[field, field] if last else (),
             )
+            sides_next = None if last else rest
         b = b_next
+        face_and_halos, state_shape = (3 * cy + TILE, nz), (2, 16, nz)
         if sub == 0:
-            u_new, v, a, ya, yb, ka = call(
-                bind(fix_a_first), [field, field, face, side, side, (cy, nz)], (u_new, v, u, rate, ha, a), both
+            u_new, v, a, ka = call(
+                bind(fix_a_first),
+                [field, field, face_and_halos, (cy, nz)],
+                (u_new, v, u, rate, ha, a, hya, hyb),
+                both,
             )
+            old = hya, hyb
         elif sub < SUBSTEPS - 1:
-            u_new, v, a, ya, yb = call(
-                bind(fix_a), [field, field, face, side, side], (u_new, v, u, rate, ha, ka), both
+            u_new, v, a, *old = call(
+                bind(fix_a_second if sub == 1 else fix_a_third),
+                [field, field, face_and_halos, state_shape],
+                (u_new, v, u, rate, ha, ka, hya, hyb, kyd, kyu, *old),
+                both,
             )
         if sub < SUBSTEPS - 1:
             u = u_new
+            ya, yb = sides_next
     out = call(
         bind(last_kernel),
         [field, field],
-        (u_new, v, u, fine, ha, ka),
-        {0: 0, 1: 1, 6: 2, 7: 3},
-        in_hbm=done,
+        (u_new, v, u, fine, ha, ka, hya, hyb, kyd, kyu, *old),
+        {0: 0, 1: 1, 11: 2, 12: 3},
+        in_hbm=rest,
         scratch=[pltpu.SemaphoreType.DMA((2,))],
         to_hbm=[field, field],
     )

time: 31.7 us -> 31.1 us (0.981)
  waiting for transfers between devices: 5.71 us -> 2.78 us
  starting transfers between devices: 16 us -> 18.3 us
    ppermute x4, waiting for transfers between devices: 5.2 us -> 2.75 us  [per_device(): ha = lax.ppermute(a, AXES, xa)]
    ppermute x4, starting transfers between devices: 9.21 us -> 11.5 us  [per_device(): ha = lax.ppermute(a, AXES, xa)]
    ppermute x4, starting transfers between devices: 3.6 us -> 4.43 us  [per_device(): hyb = lax.ppermute(yb, AXES, pb)]
    ppermute x4, starting transfers between devices: 2.48 us -> 1.69 us  [per_device(): hya = lax.ppermute(ya, AXES, pa)]
    ppermute x4, waiting for transfers between devices: 0.49 us -> 0.01 us  [per_device(): hyb = lax.ppermute(yb, AXES, pb)]
    pallas_call x26 -> x19, Pallas kernels: 8.95 us -> 9 us  [call(): pl.pallas_call(kernel, in_specs=[VMEM] * len(arrays) + [HBM] * len(in_hbm...]
  transfers between devices with their start and end apart: 16 -> 16, of which waited for: 6 -> 3; matrix products, arithmetic and copies ran while one was open for 0% -> 0% of each run, Pallas kernels for 22% -> 22%
where the time goes in v5:
time: 31.1 us; the launch traced here: 30.9 us
  starting transfers between devices  18.3 us (59%)
  Pallas kernels  9 us (29%)
  waiting for transfers between devices  2.78 us (9%)
  between operations  0.82 us (3%)
    ppermute x4, starting transfers between devices, per_device(): ha = lax.ppermute(a, AXES, xa)  11.5 us
    pallas_call x19, Pallas kernels, call(): pl.pallas_call(kernel, in_specs=[VMEM] * len(arrays) + [HBM] * len(in_hbm...  9 us
    ppermute x4, starting transfers between devices, per_device(): hyb = lax.ppermute(yb, AXES, pb)  4.43 us
    ppermute x4, waiting for transfers between devices, per_device(): ha = lax.ppermute(a, AXES, xa)  2.75 us
    ppermute x4, starting transfers between devices, per_device(): hya = lax.ppermute(ya, AXES, pa)  1.69 us
    ppermute x4, starting transfers between devices, per_device(): hb = lax.ppermute(b, AXES, xb)  0.73 us
  transfers between devices with their start and end apart: 16, of which 3 were waited for; matrix products, arithmetic and copies ran while one was open for 0% of the time, Pallas kernels for 22%

profile of v5, /device:TPU:0, one launch (start us, length us, event | category | flops | bytes accessed | tf_op | source)
XLA Modules:
  0.0 30.9 jit_solution(16466829766235122361)
XLA Ops:
  0.6 1.4 %shard_map.86 = (f32[4,32,256]{2,1,0:T(8,128)S(1)}, f32[4,32,256]{2,1,0:T(8,128)S(1)}, f32[4,8,256]{2,1,0:T(8,128)S(1)}, f32[4,8,256]{2,1,0:T(8,128)S(1)}, f32[3...) custom-call(f32[3,256,256]{2,1,0:T(8,128)} %bitcast.10, ...), custom_call_target="tpu_custom_call" | custom-call | flops 1 | bytes 1 | tf_op jit(solution)/shard_map/pallas_call | solution.py:58
  2.0 0.5 %collective-permute-start = (f32[4,32,256]{2,1,0:T(8,128)S(1)}, f32[4,32,256]{2,1,0:T(8,128)S(1)}, u32[]{:S(2)}, u32[]{:S(2)}) collective-permute-start(f32[4,32,256]{2,1,0:T(8,128)S(1)} %get-tuple-element.81.refs_1_.b_sent), channel_id=1, source_target_pairs={{0,1},{1,0},{2,3},{3,2},{4,8},{5,9},{6,10},{7,11},{8,4},{9,5},{10,... | collective-permute-start | bytes 393224 | tf_op jit(solution)/shard_map/ppermute | solution.py:521
  2.5 2.6 %collective-permute-start.2 = (f32[4,8,256]{2,1,0:T(8,128)S(1)}, f32[4,8,256]{2,1,0:T(8,128)S(1)}, u32[]{:S(2)}, u32[]{:S(2)}) collective-permute-start(f32[4,8,256]{2,1,0:T(8,128)S(1)} %shard_map.88.yb_sent.refs_1_), channel_id=1, source_target_pairs={{0,3},{1,2},{2,1},{3,0},{4,7},{5,6},{6,5},{7,4},{8,11},{9,10},{10,... | collective-permute-start | bytes 98312 | tf_op jit(solution)/shard_map/ppermute | solution.py:524
  5.2 0.1 collective-permute-start.1
  5.3 3.0 %collective-permute-start.3 = (f32[4,32,256]{2,1,0:T(8,128)S(1)}, f32[4,32,256]{2,1,0:T(8,128)S(1)}, u32[]{:S(2)}, u32[]{:S(2)}) collective-permute-start(f32[4,32,256]{2,1,0:T(8,128)S(1)} %shard_map.91.a_sent), channel_id=1, source_target_pairs={{0,4},{1,5},{2,6},{3,7},{4,0},{5,1},{6,2},{7,3},{8,12},{9,13},{10,... | collective-permute-start | bytes 393224 | tf_op jit(solution)/shard_map/ppermute | solution.py:527
  8.2 2.1 %shard_map.87 = (f32[3,256,256]{2,1,0:T(8,128)S(1)}, f32[3,256,256]{2,1,0:T(8,128)S(1)}, f32[3,256,256]{2,1,0:T(8,128)S(1)}, f32[288,256]{1,0:T(8,128)S(1)}, f32...) custom-call(f32[3,256,256]{2,1,0:T(8,128)S(1)} %get-tuple-element.74, ...), custom_call_target="tpu_custom_call" | custom-call | flops 1 | bytes 1 | tf_op jit(solution)/shard_map/pallas_call | solution.py:58
  10.4 0.0 collective-permute-done.2.yb.old_yb
  10.4 0.0 collective-permute-done.1.ya.old_ya
  10.4 0.0 collective-permute-done.hb
  10.4 0.1 shard_map.89
  10.5 0.1 collective-permute-start.4
  10.6 0.5 %shard_map.90 = (f32[3,256,256]{2,1,0:T(8,128)S(1)}, f32[3,256,256]{2,1,0:T(8,128)S(1)}, f32[256,256]{1,0:T(8,128)S(1)}, f32[256,256]{1,0:T(8,128)S(1)}, f32[256...) custom-call(f32[3,256,256]{2,1,0:T(8,128)S(1)} %get-tuple-element.84, ...), custom_call_target="tpu_custom_call", output_to_operand_aliasing={{0}: (0, {}), {1}: (1, {}), {2}: (2, {}), {3}: (3, {}), {4}... | custom-call | flops 1 | bytes 1 | tf_op jit(solution)/shard_map/pallas_call | solution.py:58
  11.1 0.5 %collective-permute-start.5 = (f32[4,8,256]{2,1,0:T(8,128)S(1)}, f32[4,8,256]{2,1,0:T(8,128)S(1)}, u32[]{:S(2)}, u32[]{:S(2)}) collective-permute-start(f32[4,8,256]{2,1,0:T(8,128)S(1)} %get-tuple-element.105), channel_id=1, source_target_pairs={{0,1},{1,0},{2,3},{3,2},{4,5},{5,4},{6,7},{7,6},{8,9},{9,8},{10,11... | collective-permute-start | bytes 98312 | tf_op jit(solution)/shard_map/ppermute | solution.py:528
  11.7 0.2 collective-permute-start.6
  11.8 0.0 collective-permute-done.3.ha
  11.9 3.4 %collective-permute-start.7 = (f32[104,256]{1,0:T(8,128)S(1)}, f32[104,256]{1,0:T(8,128)S(1)}, u32[]{:S(2)}, u32[]{:S(2)}) collective-permute-start(f32[104,256]{1,0:T(8,128)S(1)} %get-tuple-element.114), channel_id=1, source_target_pairs={{0,4},{1,5},{2,6},{3,7},{4,0},{5,1},{6,2},{7,3},{8,12},{9,13},{10,... | collective-permute-start | bytes 319496 | tf_op jit(solution)/shard_map/ppermute | solution.py:527
  15.3 0.5 %shard_map.93 = (f32[3,256,256]{2,1,0:T(8,128)S(1)}, f32[3,256,256]{2,1,0:T(8,128)S(1)}) custom-call(f32[3,256,256]{2,1,0:T(8,128)S(1)} %get-tuple-element.97.u, f32[3,256,256]{2,1,0:T(8,128)S(1)} %get-tuple-element.98.v, f32[3,256,256]{2,1,0:T(8,128)S(1)} %get-tuple-element.89.load, ...), custom_call_target="tpu_custom_call", output_to_operand_aliasing={{1}: (1, {})} | custom-call | flops 1 | bytes 1 | tf_op jit(solution)/shard_map/pallas_call | solution.py:58
  15.8 0.0 collective-permute-done.5.ya
  15.8 0.0 collective-permute-done.6.yb
  15.8 0.0 collective-permute-done.4.hb
  15.8 0.1 shard_map.94
  15.9 0.1 collective-permute-start.8
  16.0 0.5 %shard_map.95 = (f32[3,256,256]{2,1,0:T(8,128)S(1)}, f32[3,256,256]{2,1,0:T(8,128)S(1)}, f32[3,8,256]{2,1,0:T(8,128)S(1)}, f32[3,8,256]{2,1,0:T(8,128)S(1)}) custom-call(f32[3,256,256]{2,1,0:T(8,128)S(1)} %get-tuple-element.110.u1, f32[3,256,256]{2,1,0:T(8,128)S(1)} %get-tuple-element.111.v, ...), custom_call_target="tpu_custom_call", output_to_operand_aliasing={{0}: (0, {}), {1}: (1, {})} | custom-call | flops 1 | bytes 1 | tf_op jit(solution)/shard_map/pallas_call | solution.py:58
  16.5 0.5 %collective-permute-start.9 = (f32[3,8,256]{2,1,0:T(8,128)S(1)}, f32[3,8,256]{2,1,0:T(8,128)S(1)}, u32[]{:S(2)}, u32[]{:S(2)}) collective-permute-start(f32[3,8,256]{2,1,0:T(8,128)S(1)} %get-tuple-element.121), channel_id=1, source_target_pairs={{0,1},{1,0},{2,3},{3,2},{4,5},{5,4},{6,7},{7,6},{8,9},{9,8},{10,11... | collective-permute-start | bytes 73736 | tf_op jit(solution)/shard_map/ppermute | solution.py:528
  17.0 1.0 %collective-permute-start.10 = (f32[3,8,256]{2,1,0:T(8,128)S(1)}, f32[3,8,256]{2,1,0:T(8,128)S(1)}, u32[]{:S(2)}, u32[]{:S(2)}) collective-permute-start(f32[3,8,256]{2,1,0:T(8,128)S(1)} %get-tuple-element.122), channel_id=1, source_target_pairs={{0,3},{1,2},{2,1},{3,0},{4,7},{5,6},{6,5},{7,4},{8,11},{9,10},{10,... | collective-permute-start | bytes 73736 | tf_op jit(solution)/shard_map/ppermute | solution.py:524
  18.0 0.5 %collective-permute-done.7.ha = f32[104,256]{1,0:T(8,128)S(1)} collective-permute-done((f32[104,256]{1,0:T(8,128)S(1)}, f32[104,256]{1,0:T(8,128)S(1)}, u32[]{:S(2)}, u32[]{:S(2)}) %collective-permute-start.7) | collective-permute-done | bytes 106528 | tf_op jit(solution)/shard_map/ppermute | solution.py:527
  18.5 0.1 shard_map.96
  18.6 2.6 %collective-permute-start.11 = (f32[104,256]{1,0:T(8,128)S(1)}, f32[104,256]{1,0:T(8,128)S(1)}, u32[]{:S(2)}, u32[]{:S(2)}) collective-permute-start(f32[104,256]{1,0:T(8,128)S(1)} %get-tuple-element.127), channel_id=1, source_target_pairs={{0,4},{1,5},{2,6},{3,7},{4,0},{5,1},{6,2},{7,3},{8,12},{9,13},{10,... | collective-permute-start | bytes 319496 | tf_op jit(solution)/shard_map/ppermute | solution.py:527
  21.2 0.5 %shard_map.97 = (f32[3,256,256]{2,1,0:T(8,128)S(1)}, f32[3,256,256]{2,1,0:T(8,128)S(1)}) custom-call(f32[3,256,256]{2,1,0:T(8,128)S(1)} %get-tuple-element.116.u, f32[3,256,256]{2,1,0:T(8,128)S(1)} %get-tuple-element.117.v, f32[3,256,256]{2,1,0:T(8,128)S(1)} %get-tuple-element.89.load, ...), custom_call_target="tpu_custom_call", output_to_operand_aliasing={{1}: (1, {})} | custom-call | flops 1 | bytes 1 | tf_op jit(solution)/shard_map/pallas_call | solution.py:58
  21.6 0.0 collective-permute-done.9.ya
  21.6 0.0 collective-permute-done.10.yb
  21.7 0.0 collective-permute-done.8.hb
  21.7 0.1 shard_map.98
  21.7 0.1 collective-permute-start.12
  21.8 0.5 %shard_map.99 = (f32[3,256,256]{2,1,0:T(8,128)S(1)}, f32[3,256,256]{2,1,0:T(8,128)S(1)}, f32[3,8,256]{2,1,0:T(8,128)S(1)}, f32[3,8,256]{2,1,0:T(8,128)S(1)}) custom-call(f32[3,256,256]{2,1,0:T(8,128)S(1)} %get-tuple-element.123.u1, f32[3,256,256]{2,1,0:T(8,128)S(1)} %get-tuple-element.124.v, ...), custom_call_target="tpu_custom_call", output_to_operand_aliasing={{0}: (0, {}), {1}: (1, {})} | custom-call | flops 1 | bytes 1 | tf_op jit(solution)/shard_map/pallas_call | solution.py:58
  22.3 0.5 %collective-permute-start.13 = (f32[3,8,256]{2,1,0:T(8,128)S(1)}, f32[3,8,256]{2,1,0:T(8,128)S(1)}, u32[]{:S(2)}, u32[]{:S(2)}) collective-permute-start(f32[3,8,256]{2,1,0:T(8,128)S(1)} %get-tuple-element.134), channel_id=1, source_target_pairs={{0,1},{1,0},{2,3},{3,2},{4,5},{5,4},{6,7},{7,6},{8,9},{9,8},{10,11... | collective-permute-start | bytes 73736 | tf_op jit(solution)/shard_map/ppermute | solution.py:528
  22.8 0.6 %collective-permute-start.14 = (f32[3,8,256]{2,1,0:T(8,128)S(1)}, f32[3,8,256]{2,1,0:T(8,128)S(1)}, u32[]{:S(2)}, u32[]{:S(2)}) collective-permute-start(f32[3,8,256]{2,1,0:T(8,128)S(1)} %get-tuple-element.135), channel_id=1, source_target_pairs={{0,3},{1,2},{2,1},{3,0},{4,7},{5,6},{6,5},{7,4},{8,11},{9,10},{10,... | collective-permute-start | bytes 73736 | tf_op jit(solution)/shard_map/ppermute | solution.py:524
  23.4 0.9 %collective-permute-done.11.ha = f32[104,256]{1,0:T(8,128)S(1)} collective-permute-done((f32[104,256]{1,0:T(8,128)S(1)}, f32[104,256]{1,0:T(8,128)S(1)}, u32[]{:S(2)}, u32[]{:S(2)}) %collective-permute-start.11) | collective-permute-done | bytes 106528 | tf_op jit(solution)/shard_map/ppermute | solution.py:527
  24.4 0.1 shard_map.100
  24.4 2.5 %collective-permute-start.15 = (f32[104,256]{1,0:T(8,128)S(1)}, f32[104,256]{1,0:T(8,128)S(1)}, u32[]{:S(2)}, u32[]{:S(2)}) collective-permute-start(f32[104,256]{1,0:T(8,128)S(1)} %get-tuple-element.140), channel_id=1, source_target_pairs={{0,4},{1,5},{2,6},{3,7},{4,0},{5,1},{6,2},{7,3},{8,12},{9,13},{10,... | collective-permute-start | bytes 319496 | tf_op jit(solution)/shard_map/ppermute | solution.py:527
  27.0 0.5 %shard_map.101 = (f32[3,256,256]{2,1,0:T(8,128)S(1)}, f32[3,256,256]{2,1,0:T(8,128)S(1)}) custom-call(f32[3,256,256]{2,1,0:T(8,128)S(1)} %get-tuple-element.129.u, f32[3,256,256]{2,1,0:T(8,128)S(1)} %get-tuple-element.130.v, f32[3,256,256]{2,1,0:T(8,128)S(1)} %get-tuple-element.89.load, ...), custom_call_target="tpu_custom_call", output_to_operand_aliasing={{1}: (1, {})} | custom-call | flops 1 | bytes 1 | tf_op jit(solution)/shard_map/pallas_call | solution.py:58
  27.4 0.0 collective-permute-done.13.ya
  27.4 0.0 collective-permute-done.14.yb
  27.5 0.0 collective-permute-done.12.hb
  27.5 0.1 shard_map.102
  27.5 1.4 %shard_map.103 = (f32[3,256,256]{2,1,0:T(8,128)S(1)}, f32[3,256,256]{2,1,0:T(8,128)S(1)}, f32[3,256,256]{2,1,0:T(8,128)}, f32[3,256,256]{2,1,0:T(8,128)}) custom-call(f32[3,256,256]{2,1,0:T(8,128)S(1)} %get-tuple-element.136.u1, f32[3,256,256]{2,1,0:T(8,128)S(1)} %get-tuple-element.137.v, ...), custom_call_target="tpu_custom_call", output_to_operand_aliasing={{0}: (0, {}), {1}: (1, {})} | custom-call | flops 1 | bytes 1 | tf_op jit(solution)/shard_map/pallas_call | solution.py:58
  28.9 1.3 %collective-permute-done.15.ha = f32[104,256]{1,0:T(8,128)S(1)} collective-permute-done((f32[104,256]{1,0:T(8,128)S(1)}, f32[104,256]{1,0:T(8,128)S(1)}, u32[]{:S(2)}, u32[]{:S(2)}) %collective-permute-start.15) | collective-permute-done | bytes 106528 | tf_op jit(solution)/shard_map/ppermute | solution.py:527
  30.2 0.7 %shard_map.104 = (f32[3,256,256]{2,1,0:T(8,128)S(1)}, f32[3,256,256]{2,1,0:T(8,128)S(1)}, f32[3,256,256]{2,1,0:T(8,128)}, f32[3,256,256]{2,1,0:T(8,128)}) custom-call(f32[3,256,256]{2,1,0:T(8,128)S(1)} %get-tuple-element.138.u1, f32[3,256,256]{2,1,0:T(8,128)S(1)} %get-tuple-element.139.v1, ...), custom_call_target="tpu_custom_call", output_to_operand_aliasing={{0}: (0, {}), {1}: (1, {}), {2}: (11, {}), {3}: (12, {})} | custom-call | flops 1 | bytes 1 | tf_op jit(solution)/shard_map/pallas_call | solution.py:58
  (3 shorter events, 0.0 us)
Async XLA Ops:
  2.0 8.4 %collective-permute-start = (f32[4,32,256]{2,1,0:T(8,128)S(1)}, f32[4,32,256]{2,1,0:T(8,128)S(1)}, u32[]{:S(2)}, u32[]{:S(2)}) collective-permute-start(f32[4,32,256]{2,1,0:T(8,128)S(1)} %get-tuple-element.81.refs_1_.b_sent), channel_id=1, source_target_pairs={{0,1},{1,0},{2,3},{3,2},{4,8},{5,9},{6,10},{7,11},{8,4},{9,5},{10,... | collective-permute-start | bytes 393224 | tf_op jit(solution)/shard_map/ppermute | solution.py:521
  2.5 7.8 %collective-permute-start.2 = (f32[4,8,256]{2,1,0:T(8,128)S(1)}, f32[4,8,256]{2,1,0:T(8,128)S(1)}, u32[]{:S(2)}, u32[]{:S(2)}) collective-permute-start(f32[4,8,256]{2,1,0:T(8,128)S(1)} %shard_map.88.yb_sent.refs_1_), channel_id=1, source_target_pairs={{0,3},{1,2},{2,1},{3,0},{4,7},{5,6},{6,5},{7,4},{8,11},{9,10},{10,... | collective-permute-start | bytes 98312 | tf_op jit(solution)/shard_map/ppermute | solution.py:524
  5.2 5.2 %collective-permute-start.1 = (f32[4,8,256]{2,1,0:T(8,128)S(1)}, f32[4,8,256]{2,1,0:T(8,128)S(1)}, u32[]{:S(2)}, u32[]{:S(2)}) collective-permute-start(f32[4,8,256]{2,1,0:T(8,128)S(1)} %get-tuple-element.82.ya_sent), channel_id=1, source_target_pairs={{0,1},{1,0},{2,3},{3,2},{4,5},{5,4},{6,7},{7,6},{8,9},{9,8},{10,11... | collective-permute-start | bytes 98312 | tf_op jit(solution)/shard_map/ppermute | solution.py:528
  5.3 6.6 %collective-permute-start.3 = (f32[4,32,256]{2,1,0:T(8,128)S(1)}, f32[4,32,256]{2,1,0:T(8,128)S(1)}, u32[]{:S(2)}, u32[]{:S(2)}) collective-permute-start(f32[4,32,256]{2,1,0:T(8,128)S(1)} %shard_map.91.a_sent), channel_id=1, source_target_pairs={{0,4},{1,5},{2,6},{3,7},{4,0},{5,1},{6,2},{7,3},{8,12},{9,13},{10,... | collective-permute-start | bytes 393224 | tf_op jit(solution)/shard_map/ppermute | solution.py:527
  10.5 5.3 %collective-permute-start.4 = (f32[3,32,256]{2,1,0:T(8,128)S(1)}, f32[3,32,256]{2,1,0:T(8,128)S(1)}, u32[]{:S(2)}, u32[]{:S(2)}) collective-permute-start(f32[3,32,256]{2,1,0:T(8,128)S(1)} %get-tuple-element.104), channel_id=1, source_target_pairs={{0,1},{1,0},{2,3},{3,2},{4,8},{5,9},{6,10},{7,11},{8,4},{9,5},{10,... | collective-permute-start | bytes 294920 | tf_op jit(solution)/shard_map/ppermute | solution.py:521
  11.1 4.7 %collective-permute-start.5 = (f32[4,8,256]{2,1,0:T(8,128)S(1)}, f32[4,8,256]{2,1,0:T(8,128)S(1)}, u32[]{:S(2)}, u32[]{:S(2)}) collective-permute-start(f32[4,8,256]{2,1,0:T(8,128)S(1)} %get-tuple-element.105), channel_id=1, source_target_pairs={{0,1},{1,0},{2,3},{3,2},{4,5},{5,4},{6,7},{7,6},{8,9},{9,8},{10,11... | collective-permute-start | bytes 98312 | tf_op jit(solution)/shard_map/ppermute | solution.py:528
  11.7 4.2 %collective-permute-start.6 = (f32[4,8,256]{2,1,0:T(8,128)S(1)}, f32[4,8,256]{2,1,0:T(8,128)S(1)}, u32[]{:S(2)}, u32[]{:S(2)}) collective-permute-start(f32[4,8,256]{2,1,0:T(8,128)S(1)} %get-tuple-element.106), channel_id=1, source_target_pairs={{0,3},{1,2},{2,1},{3,0},{4,7},{5,6},{6,5},{7,4},{8,11},{9,10},{10,... | collective-permute-start | bytes 98312 | tf_op jit(solution)/shard_map/ppermute | solution.py:524
  11.9 6.6 %collective-permute-start.7 = (f32[104,256]{1,0:T(8,128)S(1)}, f32[104,256]{1,0:T(8,128)S(1)}, u32[]{:S(2)}, u32[]{:S(2)}) collective-permute-start(f32[104,256]{1,0:T(8,128)S(1)} %get-tuple-element.114), channel_id=1, source_target_pairs={{0,4},{1,5},{2,6},{3,7},{4,0},{5,1},{6,2},{7,3},{8,12},{9,13},{10,... | collective-permute-start | bytes 319496 | tf_op jit(solution)/shard_map/ppermute | solution.py:527
  15.9 5.7 %collective-permute-start.8 = (f32[3,32,256]{2,1,0:T(8,128)S(1)}, f32[3,32,256]{2,1,0:T(8,128)S(1)}, u32[]{:S(2)}, u32[]{:S(2)}) collective-permute-start(f32[3,32,256]{2,1,0:T(8,128)S(1)} %get-tuple-element.120), channel_id=1, source_target_pairs={{0,1},{1,0},{2,3},{3,2},{4,8},{5,9},{6,10},{7,11},{8,4},{9,5},{10,... | collective-permute-start | bytes 294920 | tf_op jit(solution)/shard_map/ppermute | solution.py:521
  16.5 5.2 %collective-permute-start.9 = (f32[3,8,256]{2,1,0:T(8,128)S(1)}, f32[3,8,256]{2,1,0:T(8,128)S(1)}, u32[]{:S(2)}, u32[]{:S(2)}) collective-permute-start(f32[3,8,256]{2,1,0:T(8,128)S(1)} %get-tuple-element.121), channel_id=1, source_target_pairs={{0,1},{1,0},{2,3},{3,2},{4,5},{5,4},{6,7},{7,6},{8,9},{9,8},{10,11... | collective-permute-start | bytes 73736 | tf_op jit(solution)/shard_map/ppermute | solution.py:528
  17.0 4.6 %collective-permute-start.10 = (f32[3,8,256]{2,1,0:T(8,128)S(1)}, f32[3,8,256]{2,1,0:T(8,128)S(1)}, u32[]{:S(2)}, u32[]{:S(2)}) collective-permute-start(f32[3,8,256]{2,1,0:T(8,128)S(1)} %get-tuple-element.122), channel_id=1, source_target_pairs={{0,3},{1,2},{2,1},{3,0},{4,7},{5,6},{6,5},{7,4},{8,11},{9,10},{10,... | collective-permute-start | bytes 73736 | tf_op jit(solution)/shard_map/ppermute | solution.py:524
  18.6 5.8 %collective-permute-start.11 = (f32[104,256]{1,0:T(8,128)S(1)}, f32[104,256]{1,0:T(8,128)S(1)}, u32[]{:S(2)}, u32[]{:S(2)}) collective-permute-start(f32[104,256]{1,0:T(8,128)S(1)} %get-tuple-element.127), channel_id=1, source_target_pairs={{0,4},{1,5},{2,6},{3,7},{4,0},{5,1},{6,2},{7,3},{8,12},{9,13},{10,... | collective-permute-start | bytes 319496 | tf_op jit(solution)/shard_map/ppermute | solution.py:527
  21.7 5.7 %collective-permute-start.12 = (f32[3,32,256]{2,1,0:T(8,128)S(1)}, f32[3,32,256]{2,1,0:T(8,128)S(1)}, u32[]{:S(2)}, u32[]{:S(2)}) collective-permute-start(f32[3,32,256]{2,1,0:T(8,128)S(1)} %get-tuple-element.133), channel_id=1, source_target_pairs={{0,1},{1,0},{2,3},{3,2},{4,8},{5,9},{6,10},{7,11},{8,4},{9,5},{10,... | collective-permute-start | bytes 294920 | tf_op jit(solution)/shard_map/ppermute | solution.py:521
  22.3 5.1 %collective-permute-start.13 = (f32[3,8,256]{2,1,0:T(8,128)S(1)}, f32[3,8,256]{2,1,0:T(8,128)S(1)}, u32[]{:S(2)}, u32[]{:S(2)}) collective-permute-start(f32[3,8,256]{2,1,0:T(8,128)S(1)} %get-tuple-element.134), channel_id=1, source_target_pairs={{0,1},{1,0},{2,3},{3,2},{4,5},{5,4},{6,7},{7,6},{8,9},{9,8},{10,11... | collective-permute-start | bytes 73736 | tf_op jit(solution)/shard_map/ppermute | solution.py:528
  22.8 4.6 %collective-permute-start.14 = (f32[3,8,256]{2,1,0:T(8,128)S(1)}, f32[3,8,256]{2,1,0:T(8,128)S(1)}, u32[]{:S(2)}, u32[]{:S(2)}) collective-permute-start(f32[3,8,256]{2,1,0:T(8,128)S(1)} %get-tuple-element.135), channel_id=1, source_target_pairs={{0,3},{1,2},{2,1},{3,0},{4,7},{5,6},{6,5},{7,4},{8,11},{9,10},{10,... | collective-permute-start | bytes 73736 | tf_op jit(solution)/shard_map/ppermute | solution.py:524
  24.4 5.7 %collective-permute-start.15 = (f32[104,256]{1,0:T(8,128)S(1)}, f32[104,256]{1,0:T(8,128)S(1)}, u32[]{:S(2)}, u32[]{:S(2)}) collective-permute-start(f32[104,256]{1,0:T(8,128)S(1)} %get-tuple-element.140), channel_id=1, source_target_pairs={{0,4},{1,5},{2,6},{3,7},{4,0},{5,1},{6,2},{7,3},{8,12},{9,13},{10,... | collective-permute-start | bytes 319496 | tf_op jit(solution)/shard_map/ppermute | solution.py:527

commit v6 on v5

--- a/solution.py
+++ b/solution.py
@@ -74,8 +74,12 @@
     return total * (1 - eroded).astype(jnp.float32)
 
 
+def run(start, rows, step=TILE):
+    return pl.ds(start if isinstance(start, int) else pl.multiple_of(start, step), rows)
+
+
 def layer(index, rows):
-    return pl.ds(pl.multiple_of(index * rows, rows), rows)
+    return run(index * rows, rows, rows)
 
 
 def sides(cx):
@@ -96,10 +100,12 @@
 
 
 def open_kernel(
-    cx, cy, u_hbm, material_hbm, eroded_hbm, table_hbm, a, b, ya, yb, u, material, eroded, table, scalars, edge, sems
+    cx, cy, u_hbm, material_hbm, eroded_hbm, table_hbm, damaged_hbm,
+    a, b, ya, yb, u, material, eroded, table, damaged, scalars, edge, sems,
 ):
     moves = [(table_hbm, scalars), (material_hbm, material), (eroded_hbm, eroded)]
-    copies = start_copies(moves + [(u_hbm.at[c], u.at[c]) for c in range(3)], sems)
+    moves += [(u_hbm.at[c], u.at[c]) for c in range(3)]
+    copies = start_copies(moves + [(damaged_hbm, damaged)], sems)
     copies[0].wait()
     for index in range(table.shape[0]):
         table[index : index + 1, :] = jnp.full((1, table.shape[1]), scalars[index], jnp.float32)
@@ -116,13 +122,14 @@
             put_rows(even, x, i, cells[top, :], cells[end, :], edge.at[0], edge.at[1])
     for side, out in enumerate((ya, yb)):
         out[3] = lookup(edge[side, 0], edge[side, 1], table)
-    for copy in copies[3:]:
+    for copy in copies[3:6]:
         copy.wait()
     for face, out in ((fa, a), (fb, b)):
         at = layer(face, cy)
         for c in range(3):
             out[c] = u[c, at, :]
     pack_rows(cx, cy, u, ya, yb)
+    copies[6].wait()
 
 
 def put_rows(even, x, c, first, last, ya, yb):
@@ -138,13 +145,16 @@
     even = plane_even()
 
     def tile(x, t):
-        return pl.ds(pl.multiple_of(x * cy + t * TILE, TILE), TILE)
+        return run(x * cy + t * TILE, TILE)
+
+    def clamp(x):
+        return min(max(x, 0), cx - 1) if isinstance(x, int) else jnp.clip(x, 0, cx - 1)
 
     for i in range(count):
         x = first + i
         for t in tiles if tiles is not None else range(cy // TILE):
             at = tile(x, t)
-            x_down, x_up = tile(jnp.maximum(x - 1, 0), t), tile(jnp.minimum(x + 1, cx - 1), t)
+            x_down, x_up = tile(clamp(x - 1), t), tile(clamp(x + 1), t)
             r = rate[at, :]
             for c in range(3):
                 here = u[c, at, :]
@@ -199,36 +209,44 @@
     pack_rows(cx, cy, u_out, ya_send, yb_send)
 
 
-def rest_kernel_last(
-    cx, cy, u1, v, u, load, kx, kyd, kyu, kzd, kzu, total, rate, ya, yb, u_out, v_out, u_hbm, v_hbm, sems
-):
+def rest_kernel_plain(cx, cy, u1, v, u, load, kx, kyd, kyu, kzd, kzu, total, rate, ya, yb, u_out, v_out):
     stiff = kx, kyd, kyu, kzd, kzu, total
-    start = jnp.where(sides(cx)[0] == 0, 1, 0)
-    half = (cx - 1) // 2
+    advance_outer(cx, cy, u, v, load, stiff, rate, u_out, v_out, (ya, yb))
+
+
+def last_inner(
+    cx, cy, u, v, load, kx, kyd, kyu, kzd, kzu, total, rate, hb, kb, u_out, v_out, u_hbm, v_hbm, sems
+):
+    stiff = kx, kyd, kyu, kzd, kzu, total
+    fa, fb = sides(cx)
     copies = []
-    for i, (begin, size) in enumerate(((start, half), (start + half, cx - 1 - half))):
-        at = pl.ds(pl.multiple_of(begin * cy, cy), size * cy)
-        for j, (source, target) in enumerate(((u_out, u_hbm), (v_out, v_hbm))):
-            copies.append(pltpu.make_async_copy(source.at[:, at, :], target.at[:, at, :], sems.at[2 * i + j]))
-
-    def then(i):
-        if i == half:
-            copies[0].start()
-            copies[1].start()
-
-    advance_outer(cx, cy, u, v, load, stiff, rate, u_out, v_out, (ya, yb), then)
-    copies[2].start()
-    copies[3].start()
+
+    def send(x):
+        at = run(x * cy + TILE, cy - 2 * TILE)
+        for source, target in ((u_out, u_hbm), (v_out, v_hbm)):
+            copy = pltpu.make_async_copy(source.at[:, at, :], target.at[:, at, :], sems.at[len(copies)])
+            copy.start()
+            copies.append(copy)
+
+    advance(cx, cy, fb, 1, u, v, load, stiff, rate, u_out, v_out)
+    fix_face(layer(fb, cy), u, rate, kb[...], lambda c: hb[c], u_out, v_out)
+    send(fb)
+    advance(cx, cy, 1, cx - 2, u, v, load, stiff, rate, u_out, v_out, then=lambda i: send(1 + i))
+    advance(cx, cy, fa, 1, u, v, load, stiff, rate, u_out, v_out)
     for copy in copies:
         copy.wait()
 
 
 def rest_kernel_first(
-    cx, cy, u1, v, kyd, kyu, total, u, load, kx, kzd, kzu, rate, fine, ya, yb, ya_sent, yb_sent,
-    u_out, v_out, kyd_out, kyu_out, total_out, ya_send, yb_send,
+    cx, cy, u1, v1, kyd, kyu, total, u, v, load, kx, kzd, kzu, rate, ya, yb, ya_sent, yb_sent,
+    u_out, v_out, kyd_out, kyu_out, total_out, k_low, k_high, sides_k,
 ):
     low, high = row_stiffness(ya_sent, yb_sent, ya, yb)
+    sides_k[0], sides_k[1] = low, high
     row = lax.broadcasted_iota(jnp.int32, (TILE, u.shape[-1]), 0)
+    face = sides(cx)[1]
+    k_low[...] = jnp.where(row == 0, sides_k[0, pl.ds(face, 1), :], 0.0)
+    k_high[...] = jnp.where(row == TILE - 1, sides_k[1, pl.ds(face, 1), :], 0.0)
     for x in range(cx):
         for start, edge, k, out in (
             (x * cy, 0, low, kyd_out),
@@ -240,16 +258,16 @@
             total_out[at, :] += extra
     stiff = kx, kyd_out, kyu_out, kzd, kzu, total_out
     advance_outer(cx, cy, u, v, load, stiff, rate, u_out, v_out, (ya, yb))
-    pack_rows(cx, cy, u_out, ya_send, yb_send, fine)
+
+
+def pack_first(cx, cy, u_new, fine, ya_send, yb_send):
+    pack_rows(cx, cy, u_new, ya_send, yb_send, fine)
 
 
 def prepare_kernel(
-    cx, cy, u, material, eroded, table, v_hbm, load_hbm, damaged_hbm,
-    u_out, v_out, load, kx, kyd, kyu, kzd, kzu, total, coarse, fine, damaged, k_all, sems,
-):
-    moves = [(damaged_hbm, damaged)]
-    moves += [(h.at[c], w.at[c]) for c in range(3) for h, w in ((v_hbm, v_out), (load_hbm, load))]
-    copies = start_copies(moves, sems)
+    cx, cy, u, material, eroded, table, v, load, damaged,
+    u_out, v_out, kx, kyd, kyu, kzd, kzu, total, coarse, fine, k_all,
+):
     nz = u.shape[-1]
     row = lax.broadcasted_iota(jnp.int32, (TILE, nz), 0)
     lane = lax.broadcasted_iota(jnp.int32, (TILE, nz), 1)
@@ -276,16 +294,13 @@
             total[at, :] = ((face + face_up) + (y_up + y_down)) + (z_up + z_down)
             face = face_up
     kx[cx * cy : (cx + 1) * cy, :] = jnp.zeros((cy, nz), jnp.float32)
-    copies[0].wait()
     for x in range(cx):
         at = slice(x * cy, (x + 1) * cy)
         hit = damaged[at, :] == 1
         coarse[at, :] = jnp.where(hit, FINE, COARSE)
         fine[at, :] = jnp.where(hit, FINE, 0.0)
-    for copy in copies[1:]:
-        copy.wait()
     stiff = kx, kyd, kyu, kzd, kzu, total
-    advance_inner(cx, cy, u, v_out, load, stiff, coarse, u_out, v_out)
+    advance_inner(cx, cy, u, v, load, stiff, coarse, u_out, v_out)
 
 
 def fix_face(at, u, rate, k, halo, u_new, v_new, put=None):
@@ -339,14 +354,7 @@
     return jnp.where(even, k_b, k_a), jnp.where(even, k_a, k_b)
 
 
-def fix_b_first(
-    cx, cy, u1, v1, u, rate, hb, ya, yb, b_sent, ya_sent, yb_sent, u_new, v_new, send, kb, k_low, k_high, sides_k
-):
-    sides_k[0], sides_k[1] = row_stiffness(ya_sent, yb_sent, ya, yb)
-    row = lax.broadcasted_iota(jnp.int32, k_low.shape, 0)
-    face = sides(cx)[1]
-    k_low[...] = jnp.where(row == 0, sides_k[0, pl.ds(face, 1), :], 0.0)
-    k_high[...] = jnp.where(row == TILE - 1, sides_k[1, pl.ds(face, 1), :], 0.0)
+def fix_b_first(cx, cy, u1, v1, u, rate, hb, ya, yb, b_sent, k_low, k_high, u_new, v_new, send, kb):
     kb[...] = face_stiffness(b_sent, hb, True)
     fix_b(cx, cy, u1, v1, u, rate, hb, ya, yb, kb, k_low, k_high, u_new, v_new, send)
 
@@ -448,17 +456,22 @@
     finish_a(cx, cy, u, rate, ha, ka, ya, yb, u_new, v_new, send)
 
 
-def fix_a_third(cx, cy, u1, v1, u, rate, ha, ka, ya, yb, kyd, kyu, state, u_new, v_new, send, state_out):
-    correct(cx, cy, 2, rate, ha, ya, yb, kyd, kyu, None, None, state, u_new, v_new, state_out)
-    finish_a(cx, cy, u, rate, ha, ka, ya, yb, u_new, v_new, send)
+def fix_a_third(
+    cx, cy, u1, v1, u, rate, ha, ka, ya, yb, kyd, kyu, state, u_new, v_new, send, ya_send, yb_send
+):
+    correct(cx, cy, 2, rate, ha, ya, yb, kyd, kyu, None, None, state, u_new, v_new, None)
+    close_face(cx, cy, u, rate, ha, ka, u_new, v_new, send)
+    pack_rows(cx, cy, u_new, ya_send, yb_send)
 
 
 def finish_a(cx, cy, u, rate, ha, ka, ya, yb, u_new, v_new, send):
-    face = sides(cx)[0]
-    put_halos(cy, face, ya, yb, send)
-    fix_face(
-        layer(face, cy), u, rate, ka[...], lambda c: ha[c * cy : (c + 1) * cy, :], u_new, v_new, put_face(cy, send)
-    )
+    put_halos(cy, sides(cx)[0], ya, yb, send)
+    close_face(cx, cy, u, rate, ha, ka, u_new, v_new, send)
+
+
+def close_face(cx, cy, u, rate, ha, ka, u_new, v_new, send):
+    at = layer(sides(cx)[0], cy)
+    fix_face(at, u, rate, ka[...], lambda c: ha[c * cy : (c + 1) * cy, :], u_new, v_new, put_face(cy, send))
 
 
 def hand_on(*refs):
@@ -469,18 +482,36 @@
     return call(hand_on, [array.shape], (array, other), {0: 0})[0]
 
 
-def last_kernel(
-    cx, cy, u1, v1, u, rate, ha, ka, ya, yb, kyd, kyu, state, u_in, v_in, u_new, v_new, u_hbm, v_hbm, sems
-):
-    at = layer(sides(cx)[0], cy)
-    correct(cx, cy, 3, rate, ha, ya, yb, kyd, kyu, None, None, state, u_new, v_new, None)
-    fix_face(at, u, rate, ka[...], lambda c: ha[c * cy : (c + 1) * cy, :], u_new, v_new)
-    copies = [
-        pltpu.make_async_copy(source.at[:, at, :], target.at[:, at, :], sems.at[i])
-        for i, (source, target) in enumerate(((u_new, u_hbm), (v_new, v_hbm)))
-    ]
-    for copy in copies:
-        copy.start()
+def last_outer(
+    cx, cy, u1, v1, u, rate, ha, ka, ya, yb, kyd, kyu, u_in, v_in, u_new, v_new, u_hbm, v_hbm, sems
+):
+    rows = cx * cy
+    fa = sides(cx)[0]
+    row = lax.broadcasted_iota(jnp.int32, (TILE, u.shape[-1]), 0)
+    copies = []
+
+    def send(start, size):
+        at = run(start, size)
+        for source, target in ((u_new, u_hbm), (v_new, v_hbm)):
+            copy = pltpu.make_async_copy(source.at[:, at, :], target.at[:, at, :], sems.at[len(copies)])
+            copy.start()
+            copies.append(copy)
+
+    fix_face(layer(fa, cy), u, rate, ka[...], lambda c: ha[c * cy : (c + 1) * cy, :], u_new, v_new)
+    send(fa * cy + TILE, cy - 2 * TILE)
+    for x in range(cx):
+        for side, (start, edge, stiff) in enumerate(((x * cy, 0, kyd), ((x + 1) * cy - TILE, TILE - 1, kyu))):
+            at = slice(start, start + TILE)
+            k = jnp.where(row == edge, stiff[at, :], 0.0)
+            r = rate[at, :]
+            for c in range(3):
+                push = r * (k * (halo_rows(ya, yb, c, x)[side] - u[c, at, :]))
+                v_new[c, at, :] += push
+                u_new[c, at, :] += r * push
+            if side == 0:
+                begin = max(start - TILE, 0)
+                send(begin, start + TILE - begin)
+    send(rows - TILE, TILE)
     for copy in copies:
         copy.wait()
 
@@ -504,77 +535,74 @@
         return functools.partial(kernel, cx, cy)
 
     table_shape = (stiff_table.shape[0], nz)
-    a, b, ya, yb, u, material, eroded, table = call(
+    a, b, ya, yb, u, material, eroded, table, damaged = call(
         bind(open_kernel),
-        [(4, cy, nz)] * 2 + [(4, cx, nz)] * 2 + [field, cells, cells, table_shape],
+        [(4, cy, nz)] * 2 + [(4, cx, nz)] * 2 + [field, cells, cells, table_shape, cells],
         (),
-        in_hbm=(u, material, eroded, stiff_table),
-        dtypes=[jnp.float32] * 5 + [jnp.int32] * 2 + [jnp.float32],
+        in_hbm=(u, material, eroded, stiff_table, damaged),
+        dtypes=[jnp.float32] * 5 + [jnp.int32] * 2 + [jnp.float32, jnp.int32],
         scratch=[
             pltpu.SMEM(stiff_table.shape, jnp.float32),
             pltpu.VMEM((2, 2, cx, nz), jnp.int32),
-            pltpu.SemaphoreType.DMA((6,)),
+            pltpu.SemaphoreType.DMA((7,)),
         ],
     )
     both = {0: 0, 1: 1}
     for sub in range(SUBSTEPS):
+        last = sub == SUBSTEPS - 1
         hb = lax.ppermute(b, AXES, xb)
         if sub == 0:
             yb = after(yb, b)
+        if last:
+            yb = after(yb, a)
         hyb = lax.ppermute(yb, AXES, pb)
         if sub == 0:
             a = after(a, yb)
         ha = lax.ppermute(a, AXES, xa)
         hya = lax.ppermute(ya, AXES, pa)
         if sub == 0:
-            u_new, v, load, kx, kyd, kyu, kzd, kzu, total, coarse, fine = call(
+            u_new, v_new, kx, kyd, kyu, kzd, kzu, total, coarse, fine = call(
                 bind(prepare_kernel),
-                [field] * 3 + [((cx + 1) * cy, nz)] + [cells] * 7,
-                (u, material, eroded, table),
-                in_hbm=(v, load, damaged),
-                scratch=[
-                    pltpu.VMEM(cells, jnp.int32),
-                    pltpu.VMEM(cells, jnp.float32),
-                    pltpu.SemaphoreType.DMA((7,)),
-                ],
+                [field] * 2 + [((cx + 1) * cy, nz)] + [cells] * 7,
+                (u, material, eroded, table, v, load, damaged),
+                scratch=[pltpu.VMEM(cells, jnp.float32)],
             )
             rate = coarse
-            u_new, v, b_next, kb, k_low, k_high = call(
+            u_new, v, kyd, kyu, total, k_low, k_high = call(
+                bind(rest_kernel_first),
+                [field, field] + [cells] * 3 + [(TILE, nz)] * 2,
+                (u_new, v_new, kyd, kyu, total, u, v, load, kx, kzd, kzu, rate, hya, hyb, ya, yb),
+                {i: i for i in range(5)},
+                scratch=[pltpu.VMEM((2, cx, nz), jnp.float32)],
+            )
+            u_new, v, b_next, kb = call(
                 bind(fix_b_first),
-                [field, field, face, (cy, nz), (TILE, nz), (TILE, nz)],
-                (u_new, v, u, rate, hb, hya, hyb, b, ya, yb),
+                [field, field, face, (cy, nz)],
+                (u_new, v, u, rate, hb, hya, hyb, b, k_low, k_high),
                 both,
                 weight=LONG,
-                scratch=[pltpu.VMEM((2, cx, nz), jnp.float32)],
-            )
-            u_new, v, kyd, kyu, total, *sides_next = call(
-                bind(rest_kernel_first),
-                [field, field] + [cells] * 3 + [(4, cx, nz)] * 2,
-                (u_new, v, kyd, kyu, total, u, load, kx, kzd, kzu, rate, fine, hya, hyb, ya, yb),
-                {i: i for i in range(5)},
-            )
-        else:
+            )
+            sides_next = call(bind(pack_first), [(4, cx, nz)] * 2, (u_new, fine))
+        elif not last:
             rate = fine
             stiff = kx, kyd, kyu, kzd, kzu, total
             u_new, v = call(bind(edge_kernel), [field, field], (u, v, load, *stiff, rate), {1: 1})
-            last = sub == SUBSTEPS - 1
-            u_new, v, *sent = call(
+            u_new, v, b_next = call(
                 bind(fix_b),
-                [field, field] if last else [field, field, face],
+                [field, field, face],
                 (u_new, v, u, rate, hb, hya, hyb, kb, k_low, k_high),
                 both,
                 weight=LONG,
             )
-            b_next = None if last else sent[0]
-            u_new, v, *rest = call(
-                bind(rest_kernel_last if last else rest_kernel),
-                [field, field] if last else [field, field, side, side],
+            packs = sub < SUBSTEPS - 2
+            u_new, v, *sides_next = call(
+                bind(rest_kernel if packs else rest_kernel_plain),
+                [field, field] + ([side, side] if packs else []),
                 (u_new, v, u, load, *stiff, rate, hya, hyb),
                 both,
-                scratch=[pltpu.SemaphoreType.DMA((4,))] if last else (),
-                to_hbm=[field, field] if last else (),
-            )
-            sides_next = None if last else rest
+            )
+        else:
+            break
         b = b_next
         face_and_halos, state_shape = (3 * cy + TILE, nz), (2, 16, nz)
         if sub == 0:
@@ -585,23 +613,37 @@
                 both,
             )
             old = hya, hyb
-        elif sub < SUBSTEPS - 1:
-            u_new, v, a, *old = call(
-                bind(fix_a_second if sub == 1 else fix_a_third),
+        elif sub == 1:
+            u_new, v, a, state = call(
+                bind(fix_a_second),
                 [field, field, face_and_halos, state_shape],
                 (u_new, v, u, rate, ha, ka, hya, hyb, kyd, kyu, *old),
                 both,
             )
-        if sub < SUBSTEPS - 1:
-            u = u_new
-            ya, yb = sides_next
+        else:
+            u_new, v, a, *sides_next = call(
+                bind(fix_a_third),
+                [field, field, (3 * cy, nz), side, side],
+                (u_new, v, u, rate, ha, ka, hya, hyb, kyd, kyu, state),
+                both,
+            )
+        u = u_new
+        ya, yb = sides_next
+    u_new, v, *out = call(
+        bind(last_inner),
+        [field, field],
+        (u, v, load, *stiff, fine, hb, kb),
+        {1: 1},
+        scratch=[pltpu.SemaphoreType.DMA((2 * (cx - 1),))],
+        to_hbm=[field, field],
+    )
     out = call(
-        bind(last_kernel),
+        bind(last_outer),
         [field, field],
-        (u_new, v, u, fine, ha, ka, hya, hyb, kyd, kyu, *old),
-        {0: 0, 1: 1, 11: 2, 12: 3},
-        in_hbm=rest,
-        scratch=[pltpu.SemaphoreType.DMA((2,))],
+        (u_new, v, u, fine, ha, ka, hya, hyb, kyd, kyu),
+        {0: 0, 1: 1, 10: 2, 11: 3},
+        in_hbm=out,
+        scratch=[pltpu.SemaphoreType.DMA((2 * (cx + 2),))],
         to_hbm=[field, field],
     )
     return out[2].reshape(displacement.shape), out[3].reshape(displacement.shape)

time: 31.1 us -> 30.7 us (0.987)
  waiting for transfers between devices: 2.78 us -> 5.61 us
  starting transfers between devices: 18.3 us -> 16.5 us
  Pallas kernels: 9 us -> 7.68 us
    ppermute x4, waiting for transfers between devices: 2.75 us -> 4.65 us  [per_device(): ha = lax.ppermute(a, AXES, xa)]
    pallas_call x19, Pallas kernels: 9 us -> 7.68 us  [call(): pl.pallas_call(kernel, in_specs=[VMEM] * len(arrays) + [HBM] * len(in_hbm...]
    ppermute x4, starting transfers between devices: 4.43 us -> 3.27 us  [per_device(): hyb = lax.ppermute(yb, AXES, pb)]
    ppermute x4, starting transfers between devices: 11.5 us -> 10.5 us  [per_device(): ha = lax.ppermute(a, AXES, xa)]
    ppermute x4, waiting for transfers between devices: 0.01 us -> 0.94 us  [per_device(): hyb = lax.ppermute(yb, AXES, pb)]
  transfers between devices with their start and end apart: 16 -> 16, of which waited for: 3 -> 4; matrix products, arithmetic and copies ran while one was open for 0% -> 0% of each run, Pallas kernels for 22% -> 16%
where the time goes in v6:
time: 30.7 us; the launch traced here: 30.6 us
  starting transfers between devices  16.5 us (54%)
  Pallas kernels  7.68 us (25%)
  waiting for transfers between devices  5.61 us (18%)
  between operations  0.82 us (3%)
    ppermute x4, starting transfers between devices, per_device(): ha = lax.ppermute(a, AXES, xa)  10.5 us
    pallas_call x19, Pallas kernels, call(): pl.pallas_call(kernel, in_specs=[VMEM] * len(arrays) + [HBM] * len(in_hbm...  7.68 us
    ppermute x4, waiting for transfers between devices, per_device(): ha = lax.ppermute(a, AXES, xa)  4.65 us
    ppermute x4, starting transfers between devices, per_device(): hyb = lax.ppermute(yb, AXES, pb)  3.27 us
    ppermute x4, starting transfers between devices, per_device(): hya = lax.ppermute(ya, AXES, pa)  1.97 us
    ppermute x4, waiting for transfers between devices, per_device(): hyb = lax.ppermute(yb, AXES, pb)  0.94 us
    ppermute x4, starting transfers between devices, per_device(): hb = lax.ppermute(b, AXES, xb)  0.73 us
  transfers between devices with their start and end apart: 16, of which 4 were waited for; matrix products, arithmetic and copies ran while one was open for 0% of the time, Pallas kernels for 16%

profile of v6, /device:TPU:0, one launch (start us, length us, event | category | flops | bytes accessed | tf_op | source)
XLA Modules:
  0.0 30.6 jit_solution(6457378052501440333)
XLA Ops:
  0.6 0.0 copy-start
  0.6 0.0 copy-start.1
  0.7 1.5 %shard_map.86 = (f32[4,32,256]{2,1,0:T(8,128)S(1)}, f32[4,32,256]{2,1,0:T(8,128)S(1)}, f32[4,8,256]{2,1,0:T(8,128)S(1)}, f32[4,8,256]{2,1,0:T(8,128)S(1)}, f32[3...) custom-call(f32[3,256,256]{2,1,0:T(8,128)} %bitcast.19, ...), custom_call_target="tpu_custom_call" | custom-call | flops 1 | bytes 1 | tf_op jit(solution)/shard_map/pallas_call | solution.py:58
  2.2 0.5 %collective-permute-start.2 = (f32[4,32,256]{2,1,0:T(8,128)S(1)}, f32[4,32,256]{2,1,0:T(8,128)S(1)}, u32[]{:S(2)}, u32[]{:S(2)}) collective-permute-start(f32[4,32,256]{2,1,0:T(8,128)S(1)} %get-tuple-element.85.refs_1_.b_sent), channel_id=1, source_target_pairs={{0,1},{1,0},{2,3},{3,2},{4,8},{5,9},{6,10},{7,11},{8,4},{9,5},{10,... | collective-permute-start | bytes 393224 | tf_op jit(solution)/shard_map/ppermute | solution.py:553
  2.7 2.6 %collective-permute-start.1 = (f32[4,8,256]{2,1,0:T(8,128)S(1)}, f32[4,8,256]{2,1,0:T(8,128)S(1)}, u32[]{:S(2)}, u32[]{:S(2)}) collective-permute-start(f32[4,8,256]{2,1,0:T(8,128)S(1)} %shard_map.88.yb_sent.refs_1_), channel_id=1, source_target_pairs={{0,3},{1,2},{2,1},{3,0},{4,7},{5,6},{6,5},{7,4},{8,11},{9,10},{10,... | collective-permute-start | bytes 98312 | tf_op jit(solution)/shard_map/ppermute | solution.py:558
  5.3 0.1 collective-permute-start
  5.4 3.0 %collective-permute-start.3 = (f32[4,32,256]{2,1,0:T(8,128)S(1)}, f32[4,32,256]{2,1,0:T(8,128)S(1)}, u32[]{:S(2)}, u32[]{:S(2)}) collective-permute-start(f32[4,32,256]{2,1,0:T(8,128)S(1)} %shard_map.91.a_sent), channel_id=1, source_target_pairs={{0,4},{1,5},{2,6},{3,7},{4,0},{5,1},{6,2},{7,3},{8,12},{9,13},{10,... | collective-permute-start | bytes 393224 | tf_op jit(solution)/shard_map/ppermute | solution.py:561
  8.4 0.0 copy-done
  8.4 0.0 copy-done.1
  8.4 0.8 %shard_map.87 = (f32[3,256,256]{2,1,0:T(8,128)S(1)}, f32[3,256,256]{2,1,0:T(8,128)S(1)}, f32[288,256]{1,0:T(8,128)S(1)}, f32[256,256]{1,0:T(8,128)S(1)}, f32[256...) custom-call(f32[3,256,256]{2,1,0:T(8,128)S(1)} %get-tuple-element.69, ...), custom_call_target="tpu_custom_call" | custom-call | flops 1 | bytes 1 | tf_op jit(solution)/shard_map/pallas_call | solution.py:58
  9.2 0.0 collective-permute-done.1.yb.old_yb
  9.2 0.0 collective-permute-done.ya.old_ya
  9.2 0.4 %shard_map.89 = (f32[3,256,256]{2,1,0:T(8,128)S(1)}, f32[3,256,256]{2,1,0:T(8,128)S(1)}, f32[256,256]{1,0:T(8,128)S(1)}, f32[256,256]{1,0:T(8,128)S(1)}, f32[256...) custom-call(f32[3,256,256]{2,1,0:T(8,128)S(1)} %get-tuple-element.74, ...), custom_call_target="tpu_custom_call", output_to_operand_aliasing={{0}: (0, {}), {1}: (1, {}), {2}: (2, {}), {3}: (3, {}), {4}... | custom-call | flops 1 | bytes 1 | tf_op jit(solution)/shard_map/pallas_call | solution.py:58
  9.6 0.0 collective-permute-done.2.hb
  9.6 0.1 shard_map.90
  9.7 0.1 collective-permute-start.4
  9.8 0.1 shard_map.94
  9.9 0.6 %collective-permute-start.5 = (f32[4,8,256]{2,1,0:T(8,128)S(1)}, f32[4,8,256]{2,1,0:T(8,128)S(1)}, u32[]{:S(2)}, u32[]{:S(2)}) collective-permute-start(f32[4,8,256]{2,1,0:T(8,128)S(1)} %get-tuple-element.102), channel_id=1, source_target_pairs={{0,1},{1,0},{2,3},{3,2},{4,5},{5,4},{6,7},{7,6},{8,9},{9,8},{10,11... | collective-permute-start | bytes 98312 | tf_op jit(solution)/shard_map/ppermute | solution.py:562
  10.4 0.2 collective-permute-start.6
  10.6 1.4 %collective-permute-done.3.ha = f32[4,32,256]{2,1,0:T(8,128)S(1)} collective-permute-done((f32[4,32,256]{2,1,0:T(8,128)S(1)}, f32[4,32,256]{2,1,0:T(8,128)S(1)}, u32[]{:S(2)}, u32[]{:S(2)}) %collective-permute-start.3) | collective-permute-done | bytes 131104 | tf_op jit(solution)/shard_map/ppermute | solution.py:561
  12.1 2.9 %collective-permute-start.7 = (f32[104,256]{1,0:T(8,128)S(1)}, f32[104,256]{1,0:T(8,128)S(1)}, u32[]{:S(2)}, u32[]{:S(2)}) collective-permute-start(f32[104,256]{1,0:T(8,128)S(1)} %get-tuple-element.109), channel_id=1, source_target_pairs={{0,4},{1,5},{2,6},{3,7},{4,0},{5,1},{6,2},{7,3},{8,12},{9,13},{10,... | collective-permute-start | bytes 319496 | tf_op jit(solution)/shard_map/ppermute | solution.py:561
  15.0 0.5 %shard_map.93 = (f32[3,256,256]{2,1,0:T(8,128)S(1)}, f32[3,256,256]{2,1,0:T(8,128)S(1)}) custom-call(f32[3,256,256]{2,1,0:T(8,128)S(1)} %get-tuple-element.93.u, f32[3,256,256]{2,1,0:T(8,128)S(1)} %get-tuple-element.94.v, f32[3,256,256]{2,1,0:T(8,128)S(1)} %bitcast.10, f32[288,256]{1,0:T(8,128)S(1)} %get-tuple-element.79.kx, ...), custom_call_target="tpu_custom_call", output_to_operand_aliasing={{1}: (1, {})} | custom-call | flops 1 | bytes 1 | tf_op jit(solution)/shard_map/pallas_call | solution.py:58
  15.5 0.0 collective-permute-done.5.ya
  15.5 0.0 collective-permute-done.6.yb
  15.5 0.0 collective-permute-done.4.hb
  15.5 0.1 shard_map.95
  15.6 0.1 collective-permute-start.8
  15.7 0.5 %shard_map.96 = (f32[3,256,256]{2,1,0:T(8,128)S(1)}, f32[3,256,256]{2,1,0:T(8,128)S(1)}, f32[3,8,256]{2,1,0:T(8,128)S(1)}, f32[3,8,256]{2,1,0:T(8,128)S(1)}) custom-call(f32[3,256,256]{2,1,0:T(8,128)S(1)} %get-tuple-element.105.u1, f32[3,256,256]{2,1,0:T(8,128)S(1)} %get-tuple-element.106.v, ...), custom_call_target="tpu_custom_call", output_to_operand_aliasing={{0}: (0, {}), {1}: (1, {})} | custom-call | flops 1 | bytes 1 | tf_op jit(solution)/shard_map/pallas_call | solution.py:58
  16.2 0.5 %collective-permute-start.9 = (f32[3,8,256]{2,1,0:T(8,128)S(1)}, f32[3,8,256]{2,1,0:T(8,128)S(1)}, u32[]{:S(2)}, u32[]{:S(2)}) collective-permute-start(f32[3,8,256]{2,1,0:T(8,128)S(1)} %get-tuple-element.116), channel_id=1, source_target_pairs={{0,1},{1,0},{2,3},{3,2},{4,5},{5,4},{6,7},{7,6},{8,9},{9,8},{10,11... | collective-permute-start | bytes 73736 | tf_op jit(solution)/shard_map/ppermute | solution.py:562
  16.7 0.4 %collective-permute-start.10 = (f32[3,8,256]{2,1,0:T(8,128)S(1)}, f32[3,8,256]{2,1,0:T(8,128)S(1)}, u32[]{:S(2)}, u32[]{:S(2)}) collective-permute-start(f32[3,8,256]{2,1,0:T(8,128)S(1)} %get-tuple-element.117), channel_id=1, source_target_pairs={{0,3},{1,2},{2,1},{3,0},{4,7},{5,6},{6,5},{7,4},{8,11},{9,10},{10,... | collective-permute-start | bytes 73736 | tf_op jit(solution)/shard_map/ppermute | solution.py:558
  17.1 1.1 %collective-permute-done.7.ha = f32[104,256]{1,0:T(8,128)S(1)} collective-permute-done((f32[104,256]{1,0:T(8,128)S(1)}, f32[104,256]{1,0:T(8,128)S(1)}, u32[]{:S(2)}, u32[]{:S(2)}) %collective-permute-start.7) | collective-permute-done | bytes 106528 | tf_op jit(solution)/shard_map/ppermute | solution.py:561
  18.2 0.1 shard_map.97
  18.3 2.8 %collective-permute-start.11 = (f32[104,256]{1,0:T(8,128)S(1)}, f32[104,256]{1,0:T(8,128)S(1)}, u32[]{:S(2)}, u32[]{:S(2)}) collective-permute-start(f32[104,256]{1,0:T(8,128)S(1)} %get-tuple-element.122), channel_id=1, source_target_pairs={{0,4},{1,5},{2,6},{3,7},{4,0},{5,1},{6,2},{7,3},{8,12},{9,13},{10,... | collective-permute-start | bytes 319496 | tf_op jit(solution)/shard_map/ppermute | solution.py:561
  21.1 0.5 %shard_map.98 = (f32[3,256,256]{2,1,0:T(8,128)S(1)}, f32[3,256,256]{2,1,0:T(8,128)S(1)}) custom-call(f32[3,256,256]{2,1,0:T(8,128)S(1)} %get-tuple-element.111.u, f32[3,256,256]{2,1,0:T(8,128)S(1)} %get-tuple-element.112.v, f32[3,256,256]{2,1,0:T(8,128)S(1)} %bitcast.12, f32[288,256]{1,0:T(8,128)S(1)} %get-tuple-element.79.kx, ...), custom_call_target="tpu_custom_call", output_to_operand_aliasing={{1}: (1, {})} | custom-call | flops 1 | bytes 1 | tf_op jit(solution)/shard_map/pallas_call | solution.py:58
  21.5 0.0 collective-permute-done.9.ya
  21.6 0.0 collective-permute-done.10.yb
  21.6 0.0 collective-permute-done.8.hb
  21.6 0.1 shard_map.99
  21.6 0.1 collective-permute-start.12
  21.7 0.4 %shard_map.100 = (f32[3,256,256]{2,1,0:T(8,128)S(1)}, f32[3,256,256]{2,1,0:T(8,128)S(1)}) custom-call(f32[3,256,256]{2,1,0:T(8,128)S(1)} %get-tuple-element.118.u1, f32[3,256,256]{2,1,0:T(8,128)S(1)} %get-tuple-element.119.v, f32[3,256,256]{2,1,0:T(8,128)S(1)} %get-tuple-element.111.u, ...), custom_call_target="tpu_custom_call", output_to_operand_aliasing={{0}: (0, {}), {1}: (1, {})} | custom-call | flops 1 | bytes 1 | tf_op jit(solution)/shard_map/pallas_call | solution.py:58
  22.1 2.1 %collective-permute-done.11.ha = f32[104,256]{1,0:T(8,128)S(1)} collective-permute-done((f32[104,256]{1,0:T(8,128)S(1)}, f32[104,256]{1,0:T(8,128)S(1)}, u32[]{:S(2)}, u32[]{:S(2)}) %collective-permute-start.11) | collective-permute-done | bytes 106528 | tf_op jit(solution)/shard_map/ppermute | solution.py:561
  24.3 0.1 shard_map.101
  24.4 1.8 %collective-permute-start.13 = (f32[96,256]{1,0:T(8,128)S(1)}, f32[96,256]{1,0:T(8,128)S(1)}, u32[]{:S(2)}, u32[]{:S(2)}) collective-permute-start(f32[96,256]{1,0:T(8,128)S(1)} %get-tuple-element.129.refs_1_), channel_id=1, source_target_pairs={{0,4},{1,5},{2,6},{3,7},{4,0},{5,1},{6,2},{7,3},{8,12},{9,13},{10,... | collective-permute-start | bytes 294920 | tf_op jit(solution)/shard_map/ppermute | solution.py:561
  26.2 0.0 collective-permute-start.15
  26.2 0.8 %collective-permute-start.14 = (f32[3,8,256]{2,1,0:T(8,128)S(1)}, f32[3,8,256]{2,1,0:T(8,128)S(1)}, u32[]{:S(2)}, u32[]{:S(2)}) collective-permute-start(f32[3,8,256]{2,1,0:T(8,128)S(1)} %get-tuple-element.130), channel_id=1, source_target_pairs={{0,1},{1,0},{2,3},{3,2},{4,5},{5,4},{6,7},{7,6},{8,9},{9,8},{10,11... | collective-permute-start | bytes 73736 | tf_op jit(solution)/shard_map/ppermute | solution.py:562
  27.0 0.0 collective-permute-done.12.hb
  27.0 1.5 %shard_map.102 = (f32[3,256,256]{2,1,0:T(8,128)S(1)}, f32[3,256,256]{2,1,0:T(8,128)S(1)}, f32[3,256,256]{2,1,0:T(8,128)}, f32[3,256,256]{2,1,0:T(8,128)}) custom-call(f32[3,256,256]{2,1,0:T(8,128)S(1)} %get-tuple-element.124.u, f32[3,256,256]{2,1,0:T(8,128)S(1)} %get-tuple-element.125.v, ...), custom_call_target="tpu_custom_call", output_to_operand_aliasing={{1}: (1, {})} | custom-call | flops 1 | bytes 1 | tf_op jit(solution)/shard_map/pallas_call | solution.py:58
  28.5 0.9 %collective-permute-done.15.yb = f32[3,8,256]{2,1,0:T(8,128)S(1)} collective-permute-done((f32[3,8,256]{2,1,0:T(8,128)S(1)}, f32[3,8,256]{2,1,0:T(8,128)S(1)}, u32[]{:S(2)}, u32[]{:S(2)}) %collective-permute-start.15) | collective-permute-done | bytes 24608 | tf_op jit(solution)/shard_map/ppermute | solution.py:558
  29.5 0.0 collective-permute-done.14.ya
  29.5 0.0 collective-permute-done.13.ha
  29.5 1.1 %shard_map.104 = (f32[3,256,256]{2,1,0:T(8,128)S(1)}, f32[3,256,256]{2,1,0:T(8,128)S(1)}, f32[3,256,256]{2,1,0:T(8,128)}, f32[3,256,256]{2,1,0:T(8,128)}) custom-call(f32[3,256,256]{2,1,0:T(8,128)S(1)} %get-tuple-element.127.u1, f32[3,256,256]{2,1,0:T(8,128)S(1)} %get-tuple-element.128.v1, ...), custom_call_target="tpu_custom_call", output_to_operand_aliasing={{0}: (0, {}), {1}: (1, {}), {2}: (10, {}), {3}: (11, {})} | custom-call | flops 1 | bytes 1 | tf_op jit(solution)/shard_map/pallas_call | solution.py:58
  (4 shorter events, 0.0 us)
Async XLA Ops:
  0.6 7.7 %copy-start = (f32[3,8,32,256]{3,2,1,0:T(8,128)S(1)}, f32[3,8,32,256]{3,2,1,0:T(8,128)}, u32[]{:S(2)}) copy-start(f32[3,8,32,256]{3,2,1,0:T(8,128)} %param.9) | copy-start | bytes 2359300
  0.6 7.7 %copy-start.1 = (f32[3,8,32,256]{3,2,1,0:T(8,128)S(1)}, f32[3,8,32,256]{3,2,1,0:T(8,128)}, u32[]{:S(2)}) copy-start(f32[3,8,32,256]{3,2,1,0:T(8,128)} %param.8) | copy-start | bytes 2359300
  2.2 7.4 %collective-permute-start.2 = (f32[4,32,256]{2,1,0:T(8,128)S(1)}, f32[4,32,256]{2,1,0:T(8,128)S(1)}, u32[]{:S(2)}, u32[]{:S(2)}) collective-permute-start(f32[4,32,256]{2,1,0:T(8,128)S(1)} %get-tuple-element.85.refs_1_.b_sent), channel_id=1, source_target_pairs={{0,1},{1,0},{2,3},{3,2},{4,8},{5,9},{6,10},{7,11},{8,4},{9,5},{10,... | collective-permute-start | bytes 393224 | tf_op jit(solution)/shard_map/ppermute | solution.py:553
  2.7 6.5 %collective-permute-start.1 = (f32[4,8,256]{2,1,0:T(8,128)S(1)}, f32[4,8,256]{2,1,0:T(8,128)S(1)}, u32[]{:S(2)}, u32[]{:S(2)}) collective-permute-start(f32[4,8,256]{2,1,0:T(8,128)S(1)} %shard_map.88.yb_sent.refs_1_), channel_id=1, source_target_pairs={{0,3},{1,2},{2,1},{3,0},{4,7},{5,6},{6,5},{7,4},{8,11},{9,10},{10,... | collective-permute-start | bytes 98312 | tf_op jit(solution)/shard_map/ppermute | solution.py:558
  5.3 3.8 %collective-permute-start = (f32[4,8,256]{2,1,0:T(8,128)S(1)}, f32[4,8,256]{2,1,0:T(8,128)S(1)}, u32[]{:S(2)}, u32[]{:S(2)}) collective-permute-start(f32[4,8,256]{2,1,0:T(8,128)S(1)} %get-tuple-element.83.ya_sent), channel_id=1, source_target_pairs={{0,1},{1,0},{2,3},{3,2},{4,5},{5,4},{6,7},{7,6},{8,9},{9,8},{10,11... | collective-permute-start | bytes 98312 | tf_op jit(solution)/shard_map/ppermute | solution.py:562
  5.4 6.6 %collective-permute-start.3 = (f32[4,32,256]{2,1,0:T(8,128)S(1)}, f32[4,32,256]{2,1,0:T(8,128)S(1)}, u32[]{:S(2)}, u32[]{:S(2)}) collective-permute-start(f32[4,32,256]{2,1,0:T(8,128)S(1)} %shard_map.91.a_sent), channel_id=1, source_target_pairs={{0,4},{1,5},{2,6},{3,7},{4,0},{5,1},{6,2},{7,3},{8,12},{9,13},{10,... | collective-permute-start | bytes 393224 | tf_op jit(solution)/shard_map/ppermute | solution.py:561
  9.7 5.8 %collective-permute-start.4 = (f32[3,32,256]{2,1,0:T(8,128)S(1)}, f32[3,32,256]{2,1,0:T(8,128)S(1)}, u32[]{:S(2)}, u32[]{:S(2)}) collective-permute-start(f32[3,32,256]{2,1,0:T(8,128)S(1)} %get-tuple-element.101), channel_id=1, source_target_pairs={{0,1},{1,0},{2,3},{3,2},{4,8},{5,9},{6,10},{7,11},{8,4},{9,5},{10,... | collective-permute-start | bytes 294920 | tf_op jit(solution)/shard_map/ppermute | solution.py:553
  9.9 5.6 %collective-permute-start.5 = (f32[4,8,256]{2,1,0:T(8,128)S(1)}, f32[4,8,256]{2,1,0:T(8,128)S(1)}, u32[]{:S(2)}, u32[]{:S(2)}) collective-permute-start(f32[4,8,256]{2,1,0:T(8,128)S(1)} %get-tuple-element.102), channel_id=1, source_target_pairs={{0,1},{1,0},{2,3},{3,2},{4,5},{5,4},{6,7},{7,6},{8,9},{9,8},{10,11... | collective-permute-start | bytes 98312 | tf_op jit(solution)/shard_map/ppermute | solution.py:562
  10.4 5.1 %collective-permute-start.6 = (f32[4,8,256]{2,1,0:T(8,128)S(1)}, f32[4,8,256]{2,1,0:T(8,128)S(1)}, u32[]{:S(2)}, u32[]{:S(2)}) collective-permute-start(f32[4,8,256]{2,1,0:T(8,128)S(1)} %get-tuple-element.103), channel_id=1, source_target_pairs={{0,3},{1,2},{2,1},{3,0},{4,7},{5,6},{6,5},{7,4},{8,11},{9,10},{10,... | collective-permute-start | bytes 98312 | tf_op jit(solution)/shard_map/ppermute | solution.py:558
  12.1 6.1 %collective-permute-start.7 = (f32[104,256]{1,0:T(8,128)S(1)}, f32[104,256]{1,0:T(8,128)S(1)}, u32[]{:S(2)}, u32[]{:S(2)}) collective-permute-start(f32[104,256]{1,0:T(8,128)S(1)} %get-tuple-element.109), channel_id=1, source_target_pairs={{0,4},{1,5},{2,6},{3,7},{4,0},{5,1},{6,2},{7,3},{8,12},{9,13},{10,... | collective-permute-start | bytes 319496 | tf_op jit(solution)/shard_map/ppermute | solution.py:561
  15.6 6.0 %collective-permute-start.8 = (f32[3,32,256]{2,1,0:T(8,128)S(1)}, f32[3,32,256]{2,1,0:T(8,128)S(1)}, u32[]{:S(2)}, u32[]{:S(2)}) collective-permute-start(f32[3,32,256]{2,1,0:T(8,128)S(1)} %get-tuple-element.115), channel_id=1, source_target_pairs={{0,1},{1,0},{2,3},{3,2},{4,8},{5,9},{6,10},{7,11},{8,4},{9,5},{10,... | collective-permute-start | bytes 294920 | tf_op jit(solution)/shard_map/ppermute | solution.py:553
  16.2 5.4 %collective-permute-start.9 = (f32[3,8,256]{2,1,0:T(8,128)S(1)}, f32[3,8,256]{2,1,0:T(8,128)S(1)}, u32[]{:S(2)}, u32[]{:S(2)}) collective-permute-start(f32[3,8,256]{2,1,0:T(8,128)S(1)} %get-tuple-element.116), channel_id=1, source_target_pairs={{0,1},{1,0},{2,3},{3,2},{4,5},{5,4},{6,7},{7,6},{8,9},{9,8},{10,11... | collective-permute-start | bytes 73736 | tf_op jit(solution)/shard_map/ppermute | solution.py:562
  16.7 4.9 %collective-permute-start.10 = (f32[3,8,256]{2,1,0:T(8,128)S(1)}, f32[3,8,256]{2,1,0:T(8,128)S(1)}, u32[]{:S(2)}, u32[]{:S(2)}) collective-permute-start(f32[3,8,256]{2,1,0:T(8,128)S(1)} %get-tuple-element.117), channel_id=1, source_target_pairs={{0,3},{1,2},{2,1},{3,0},{4,7},{5,6},{6,5},{7,4},{8,11},{9,10},{10,... | collective-permute-start | bytes 73736 | tf_op jit(solution)/shard_map/ppermute | solution.py:558
  18.3 6.0 %collective-permute-start.11 = (f32[104,256]{1,0:T(8,128)S(1)}, f32[104,256]{1,0:T(8,128)S(1)}, u32[]{:S(2)}, u32[]{:S(2)}) collective-permute-start(f32[104,256]{1,0:T(8,128)S(1)} %get-tuple-element.122), channel_id=1, source_target_pairs={{0,4},{1,5},{2,6},{3,7},{4,0},{5,1},{6,2},{7,3},{8,12},{9,13},{10,... | collective-permute-start | bytes 319496 | tf_op jit(solution)/shard_map/ppermute | solution.py:561
  21.6 5.4 %collective-permute-start.12 = (f32[3,32,256]{2,1,0:T(8,128)S(1)}, f32[3,32,256]{2,1,0:T(8,128)S(1)}, u32[]{:S(2)}, u32[]{:S(2)}) collective-permute-start(f32[3,32,256]{2,1,0:T(8,128)S(1)} %get-tuple-element.126), channel_id=1, source_target_pairs={{0,1},{1,0},{2,3},{3,2},{4,8},{5,9},{6,10},{7,11},{8,4},{9,5},{10,... | collective-permute-start | bytes 294920 | tf_op jit(solution)/shard_map/ppermute | solution.py:553
  24.4 5.1 %collective-permute-start.13 = (f32[96,256]{1,0:T(8,128)S(1)}, f32[96,256]{1,0:T(8,128)S(1)}, u32[]{:S(2)}, u32[]{:S(2)}) collective-permute-start(f32[96,256]{1,0:T(8,128)S(1)} %get-tuple-element.129.refs_1_), channel_id=1, source_target_pairs={{0,4},{1,5},{2,6},{3,7},{4,0},{5,1},{6,2},{7,3},{8,12},{9,13},{10,... | collective-permute-start | bytes 294920 | tf_op jit(solution)/shard_map/ppermute | solution.py:561
  26.2 3.3 %collective-permute-start.15 = (f32[3,8,256]{2,1,0:T(8,128)S(1)}, f32[3,8,256]{2,1,0:T(8,128)S(1)}, u32[]{:S(2)}, u32[]{:S(2)}) collective-permute-start(f32[3,8,256]{2,1,0:T(8,128)S(1)} %shard_map.103), channel_id=1, source_target_pairs={{0,3},{1,2},{2,1},{3,0},{4,7},{5,6},{6,5},{7,4},{8,11},{9,10},{10,... | collective-permute-start | bytes 73736 | tf_op jit(solution)/shard_map/ppermute | solution.py:558
  26.2 3.3 %collective-permute-start.14 = (f32[3,8,256]{2,1,0:T(8,128)S(1)}, f32[3,8,256]{2,1,0:T(8,128)S(1)}, u32[]{:S(2)}, u32[]{:S(2)}) collective-permute-start(f32[3,8,256]{2,1,0:T(8,128)S(1)} %get-tuple-element.130), channel_id=1, source_target_pairs={{0,1},{1,0},{2,3},{3,2},{4,5},{5,4},{6,7},{7,6},{8,9},{9,8},{10,11... | collective-permute-start | bytes 73736 | tf_op jit(solution)/shard_map/ppermute | solution.py:562

commit v7 on v6

--- a/solution.py
+++ b/solution.py
@@ -99,37 +99,36 @@
     return copies
 
 
-def open_kernel(
-    cx, cy, u_hbm, material_hbm, eroded_hbm, table_hbm, damaged_hbm,
-    a, b, ya, yb, u, material, eroded, table, damaged, scalars, edge, sems,
-):
-    moves = [(table_hbm, scalars), (material_hbm, material), (eroded_hbm, eroded)]
-    moves += [(u_hbm.at[c], u.at[c]) for c in range(3)]
-    copies = start_copies(moves + [(damaged_hbm, damaged)], sems)
+def open_b(
+    cx, cy, u_hbm, material_hbm, eroded_hbm, table_hbm, damaged_hbm, b, table, damaged, scalars, cells, sems
+):
+    at = layer(sides(cx)[1], cy)
+    moves = [(table_hbm, scalars), (material_hbm.at[at, :], cells.at[0]), (eroded_hbm.at[at, :], cells.at[1])]
+    moves += [(u_hbm.at[:, at, :], b.at[pl.ds(0, 3)]), (damaged_hbm, damaged)]
+    copies = start_copies(moves, sems)
     copies[0].wait()
     for index in range(table.shape[0]):
         table[index : index + 1, :] = jnp.full((1, table.shape[1]), scalars[index], jnp.float32)
     copies[1].wait()
     copies[2].wait()
-    fa, fb = sides(cx)
+    b[3] = lookup(cells[0], cells[1], table)
+    copies[3].wait()
+    copies[4].wait()
+
+
+def open_rest(cx, cy, b_sent, u, material, eroded, table, a, ya, yb, edge):
     even = plane_even()
-    for face, out in ((fa, a), (fb, b)):
-        at = layer(face, cy)
-        out[3] = lookup(material[at, :], eroded[at, :], table)
+    at = layer(sides(cx)[0], cy)
+    a[3] = lookup(material[at, :], eroded[at, :], table)
+    for c in range(3):
+        a[c] = u[c, at, :]
     for x in range(cx):
         top, end = slice(x * cy, x * cy + TILE), slice((x + 1) * cy - TILE, (x + 1) * cy)
         for i, cells in enumerate((material, eroded)):
             put_rows(even, x, i, cells[top, :], cells[end, :], edge.at[0], edge.at[1])
     for side, out in enumerate((ya, yb)):
         out[3] = lookup(edge[side, 0], edge[side, 1], table)
-    for copy in copies[3:6]:
-        copy.wait()
-    for face, out in ((fa, a), (fb, b)):
-        at = layer(face, cy)
-        for c in range(3):
-            out[c] = u[c, at, :]
     pack_rows(cx, cy, u, ya, yb)
-    copies[6].wait()
 
 
 def put_rows(even, x, c, first, last, ya, yb):
@@ -485,33 +484,30 @@
 def last_outer(
     cx, cy, u1, v1, u, rate, ha, ka, ya, yb, kyd, kyu, u_in, v_in, u_new, v_new, u_hbm, v_hbm, sems
 ):
-    rows = cx * cy
     fa = sides(cx)[0]
     row = lax.broadcasted_iota(jnp.int32, (TILE, u.shape[-1]), 0)
     copies = []
 
-    def send(start, size):
-        at = run(start, size)
+    def send(layers, rows):
         for source, target in ((u_new, u_hbm), (v_new, v_hbm)):
-            copy = pltpu.make_async_copy(source.at[:, at, :], target.at[:, at, :], sems.at[len(copies)])
+            source, target = (ref.reshape(3, cx, cy, ref.shape[-1]).at[:, layers, rows, :] for ref in (source, target))
+            copy = pltpu.make_async_copy(source, target, sems.at[len(copies)])
             copy.start()
             copies.append(copy)
 
     fix_face(layer(fa, cy), u, rate, ka[...], lambda c: ha[c * cy : (c + 1) * cy, :], u_new, v_new)
-    send(fa * cy + TILE, cy - 2 * TILE)
-    for x in range(cx):
-        for side, (start, edge, stiff) in enumerate(((x * cy, 0, kyd), ((x + 1) * cy - TILE, TILE - 1, kyu))):
-            at = slice(start, start + TILE)
+    send(pl.ds(fa, 1), pl.ds(TILE, cy - 2 * TILE))
+    for side, (edge, stiff) in enumerate(((0, kyd), (TILE - 1, kyu))):
+        offset = 0 if side == 0 else cy - TILE
+        for x in range(cx):
+            at = slice(x * cy + offset, x * cy + offset + TILE)
             k = jnp.where(row == edge, stiff[at, :], 0.0)
             r = rate[at, :]
             for c in range(3):
                 push = r * (k * (halo_rows(ya, yb, c, x)[side] - u[c, at, :]))
                 v_new[c, at, :] += push
                 u_new[c, at, :] += r * push
-            if side == 0:
-                begin = max(start - TILE, 0)
-                send(begin, start + TILE - begin)
-    send(rows - TILE, TILE)
+        send(pl.ds(0, cx), pl.ds(offset, TILE))
     for copy in copies:
         copy.wait()
 
@@ -535,24 +531,28 @@
         return functools.partial(kernel, cx, cy)
 
     table_shape = (stiff_table.shape[0], nz)
-    a, b, ya, yb, u, material, eroded, table, damaged = call(
-        bind(open_kernel),
-        [(4, cy, nz)] * 2 + [(4, cx, nz)] * 2 + [field, cells, cells, table_shape, cells],
+    b, table, damaged = call(
+        bind(open_b),
+        [(4, cy, nz), table_shape, cells],
         (),
         in_hbm=(u, material, eroded, stiff_table, damaged),
-        dtypes=[jnp.float32] * 5 + [jnp.int32] * 2 + [jnp.float32, jnp.int32],
+        dtypes=[jnp.float32, jnp.float32, jnp.int32],
         scratch=[
             pltpu.SMEM(stiff_table.shape, jnp.float32),
-            pltpu.VMEM((2, 2, cx, nz), jnp.int32),
-            pltpu.SemaphoreType.DMA((7,)),
+            pltpu.VMEM((2, cy, nz), jnp.int32),
+            pltpu.SemaphoreType.DMA((5,)),
         ],
+    )
+    a, ya, yb = call(
+        bind(open_rest),
+        [(4, cy, nz)] + [(4, cx, nz)] * 2,
+        (b, u, material, eroded, table),
+        scratch=[pltpu.VMEM((2, 2, cx, nz), jnp.int32)],
     )
     both = {0: 0, 1: 1}
     for sub in range(SUBSTEPS):
         last = sub == SUBSTEPS - 1
         hb = lax.ppermute(b, AXES, xb)
-        if sub == 0:
-            yb = after(yb, b)
         if last:
             yb = after(yb, a)
         hyb = lax.ppermute(yb, AXES, pb)
@@ -643,7 +643,7 @@
         (u_new, v, u, fine, ha, ka, hya, hyb, kyd, kyu),
         {0: 0, 1: 1, 10: 2, 11: 3},
         in_hbm=out,
-        scratch=[pltpu.SemaphoreType.DMA((2 * (cx + 2),))],
+        scratch=[pltpu.SemaphoreType.DMA((6,))],
         to_hbm=[field, field],
     )
     return out[2].reshape(displacement.shape), out[3].reshape(displacement.shape)

time: 30.7 us -> 30.4 us (level)
  transfers between devices with their start and end apart: 16 -> 16, of which waited for: 4 -> 4; matrix products, arithmetic and copies ran while one was open for 0% -> 0% of each run, Pallas kernels for 16% -> 17%
where the time goes in v7:
time: 30.4 us; the launch traced here: 30.3 us
  starting transfers between devices  16.4 us (54%)
  Pallas kernels  7.41 us (24%)
  waiting for transfers between devices  5.57 us (18%)
  between operations  0.84 us (3%)
    ppermute x4, starting transfers between devices, per_device(): ha = lax.ppermute(a, AXES, xa)  10.3 us
    pallas_call x19, Pallas kernels, call(): pl.pallas_call(kernel, in_specs=[VMEM] * len(arrays) + [HBM] * len(in_hbm...  7.41 us
    ppermute x4, waiting for transfers between devices, per_device(): ha = lax.ppermute(a, AXES, xa)  4.73 us
    ppermute x4, starting transfers between devices, per_device(): hyb = lax.ppermute(yb, AXES, pb)  3.24 us
    ppermute x4, starting transfers between devices, per_device(): hya = lax.ppermute(ya, AXES, pa)  2.18 us
    ppermute x4, waiting for transfers between devices, per_device(): hyb = lax.ppermute(yb, AXES, pb)  0.81 us
    ppermute x4, starting transfers between devices, per_device(): hb = lax.ppermute(b, AXES, xb)  0.73 us
  transfers between devices with their start and end apart: 16, of which 4 were waited for; matrix products, arithmetic and copies ran while one was open for 0% of the time, Pallas kernels for 17%

profile of v7, /device:TPU:0, one launch (start us, length us, event | category | flops | bytes accessed | tf_op | source)
XLA Modules:
  0.0 30.3 jit_solution(14153648300230054219)
XLA Ops:
  0.6 0.0 copy-start.1
  0.6 0.0 copy-start.3
  0.7 0.0 copy-start.4
  0.7 1.2 %shard_map.86 = (f32[4,32,256]{2,1,0:T(8,128)S(1)}, f32[8,256]{1,0:T(8,128)S(1)}, s32[256,256]{1,0:T(8,128)S(1)}) custom-call(f32[3,256,256]{2,1,0:T(8,128)} %bitcast.15, s32[256,256]{1,0:T(8,128)} %bitcast.23, s32[256,256]{1,0:T(8,128)} %bitcast.26, f32[8]{0:T(128)} %table_hbm.1, s32[256,256]{1,0:T(8,128)} %bitcast.31), custom_call_target="tpu_custom_call" | custom-call | flops 1 | bytes 1 | tf_op jit(solution)/shard_map/pallas_call | solution.py:58
  1.9 0.5 %collective-permute-start.2 = (f32[4,32,256]{2,1,0:T(8,128)S(1)}, f32[4,32,256]{2,1,0:T(8,128)S(1)}, u32[]{:S(2)}, u32[]{:S(2)}) collective-permute-start(f32[4,32,256]{2,1,0:T(8,128)S(1)} %get-tuple-element.77.b_sent), channel_id=1, source_target_pairs={{0,1},{1,0},{2,3},{3,2},{4,8},{5,9},{6,10},{7,11},{8,4},{9,5},{10,... | collective-permute-start | bytes 393224 | tf_op jit(solution)/shard_map/ppermute | solution.py:555
  2.4 0.0 copy-done.1
  2.4 0.0 copy-done.3
  2.4 0.0 copy-done.4
  2.4 0.0 copy-start
  2.4 0.0 copy-start.2
  2.4 0.1 shard_map.88
  2.6 0.2 collective-permute-start
  2.7 2.6 %collective-permute-start.1 = (f32[4,8,256]{2,1,0:T(8,128)S(1)}, f32[4,8,256]{2,1,0:T(8,128)S(1)}, u32[]{:S(2)}, u32[]{:S(2)}) collective-permute-start(f32[4,8,256]{2,1,0:T(8,128)S(1)} %get-tuple-element.79.yb_sent.refs_1_), channel_id=1, source_target_pairs={{0,3},{1,2},{2,1},{3,0},{4,7},{5,6},{6,5},{7,4},{8,11},{9,10},{10,... | collective-permute-start | bytes 98312 | tf_op jit(solution)/shard_map/ppermute | solution.py:558
  5.3 3.0 %collective-permute-start.3 = (f32[4,32,256]{2,1,0:T(8,128)S(1)}, f32[4,32,256]{2,1,0:T(8,128)S(1)}, u32[]{:S(2)}, u32[]{:S(2)}) collective-permute-start(f32[4,32,256]{2,1,0:T(8,128)S(1)} %shard_map.91.a_sent), channel_id=1, source_target_pairs={{0,4},{1,5},{2,6},{3,7},{4,0},{5,1},{6,2},{7,3},{8,12},{9,13},{10,... | collective-permute-start | bytes 393224 | tf_op jit(solution)/shard_map/ppermute | solution.py:561
  8.3 0.0 copy-done
  8.3 0.0 copy-done.2
  8.3 0.8 %shard_map.87 = (f32[3,256,256]{2,1,0:T(8,128)S(1)}, f32[3,256,256]{2,1,0:T(8,128)S(1)}, f32[288,256]{1,0:T(8,128)S(1)}, f32[256,256]{1,0:T(8,128)S(1)}, f32[256...) custom-call(f32[3,256,256]{2,1,0:T(8,128)S(1)} %bitcast.17, ...), custom_call_target="tpu_custom_call" | custom-call | flops 1 | bytes 1 | tf_op jit(solution)/shard_map/pallas_call | solution.py:58
  9.1 0.0 collective-permute-done.ya.old_ya
  9.1 0.0 collective-permute-done.1.yb.old_yb
  9.1 0.4 %shard_map.89 = (f32[3,256,256]{2,1,0:T(8,128)S(1)}, f32[3,256,256]{2,1,0:T(8,128)S(1)}, f32[256,256]{1,0:T(8,128)S(1)}, f32[256,256]{1,0:T(8,128)S(1)}, f32[256...) custom-call(f32[3,256,256]{2,1,0:T(8,128)S(1)} %get-tuple-element.68, ...), custom_call_target="tpu_custom_call", output_to_operand_aliasing={{0}: (0, {}), {1}: (1, {}), {2}: (2, {}), {3}: (3, {}), {4}... | custom-call | flops 1 | bytes 1 | tf_op jit(solution)/shard_map/pallas_call | solution.py:58
  9.6 0.0 collective-permute-done.2.hb
  9.6 0.1 shard_map.90
  9.6 0.1 collective-permute-start.4
  9.7 0.1 shard_map.94
  9.8 0.6 %collective-permute-start.5 = (f32[4,8,256]{2,1,0:T(8,128)S(1)}, f32[4,8,256]{2,1,0:T(8,128)S(1)}, u32[]{:S(2)}, u32[]{:S(2)}) collective-permute-start(f32[4,8,256]{2,1,0:T(8,128)S(1)} %get-tuple-element.96), channel_id=1, source_target_pairs={{0,1},{1,0},{2,3},{3,2},{4,5},{5,4},{6,7},{7,6},{8,9},{9,8},{10,11... | collective-permute-start | bytes 98312 | tf_op jit(solution)/shard_map/ppermute | solution.py:562
  10.4 0.2 collective-permute-start.6
  10.6 1.5 %collective-permute-done.3.ha = f32[4,32,256]{2,1,0:T(8,128)S(1)} collective-permute-done((f32[4,32,256]{2,1,0:T(8,128)S(1)}, f32[4,32,256]{2,1,0:T(8,128)S(1)}, u32[]{:S(2)}, u32[]{:S(2)}) %collective-permute-start.3) | collective-permute-done | bytes 131104 | tf_op jit(solution)/shard_map/ppermute | solution.py:561
  12.1 2.6 %collective-permute-start.7 = (f32[104,256]{1,0:T(8,128)S(1)}, f32[104,256]{1,0:T(8,128)S(1)}, u32[]{:S(2)}, u32[]{:S(2)}) collective-permute-start(f32[104,256]{1,0:T(8,128)S(1)} %get-tuple-element.103), channel_id=1, source_target_pairs={{0,4},{1,5},{2,6},{3,7},{4,0},{5,1},{6,2},{7,3},{8,12},{9,13},{10,... | collective-permute-start | bytes 319496 | tf_op jit(solution)/shard_map/ppermute | solution.py:561
  14.7 0.5 %shard_map.93 = (f32[3,256,256]{2,1,0:T(8,128)S(1)}, f32[3,256,256]{2,1,0:T(8,128)S(1)}) custom-call(f32[3,256,256]{2,1,0:T(8,128)S(1)} %get-tuple-element.87.u, f32[3,256,256]{2,1,0:T(8,128)S(1)} %get-tuple-element.88.v, f32[3,256,256]{2,1,0:T(8,128)S(1)} %bitcast.10, f32[288,256]{1,0:T(8,128)S(1)} %get-tuple-element.73.kx, ...), custom_call_target="tpu_custom_call", output_to_operand_aliasing={{1}: (1, {})} | custom-call | flops 1 | bytes 1 | tf_op jit(solution)/shard_map/pallas_call | solution.py:58
  15.2 0.0 collective-permute-done.5.ya
  15.2 0.0 collective-permute-done.6.yb
  15.2 0.0 collective-permute-done.4.hb
  15.2 0.1 shard_map.95
  15.3 0.1 collective-permute-start.8
  15.4 0.5 %shard_map.96 = (f32[3,256,256]{2,1,0:T(8,128)S(1)}, f32[3,256,256]{2,1,0:T(8,128)S(1)}, f32[3,8,256]{2,1,0:T(8,128)S(1)}, f32[3,8,256]{2,1,0:T(8,128)S(1)}) custom-call(f32[3,256,256]{2,1,0:T(8,128)S(1)} %get-tuple-element.99.u1, f32[3,256,256]{2,1,0:T(8,128)S(1)} %get-tuple-element.100.v, ...), custom_call_target="tpu_custom_call", output_to_operand_aliasing={{0}: (0, {}), {1}: (1, {})} | custom-call | flops 1 | bytes 1 | tf_op jit(solution)/shard_map/pallas_call | solution.py:58
  15.8 0.5 %collective-permute-start.9 = (f32[3,8,256]{2,1,0:T(8,128)S(1)}, f32[3,8,256]{2,1,0:T(8,128)S(1)}, u32[]{:S(2)}, u32[]{:S(2)}) collective-permute-start(f32[3,8,256]{2,1,0:T(8,128)S(1)} %get-tuple-element.110), channel_id=1, source_target_pairs={{0,1},{1,0},{2,3},{3,2},{4,5},{5,4},{6,7},{7,6},{8,9},{9,8},{10,11... | collective-permute-start | bytes 73736 | tf_op jit(solution)/shard_map/ppermute | solution.py:562
  16.4 0.4 %collective-permute-start.10 = (f32[3,8,256]{2,1,0:T(8,128)S(1)}, f32[3,8,256]{2,1,0:T(8,128)S(1)}, u32[]{:S(2)}, u32[]{:S(2)}) collective-permute-start(f32[3,8,256]{2,1,0:T(8,128)S(1)} %get-tuple-element.111), channel_id=1, source_target_pairs={{0,3},{1,2},{2,1},{3,0},{4,7},{5,6},{6,5},{7,4},{8,11},{9,10},{10,... | collective-permute-start | bytes 73736 | tf_op jit(solution)/shard_map/ppermute | solution.py:558
  16.8 1.1 %collective-permute-done.7.ha = f32[104,256]{1,0:T(8,128)S(1)} collective-permute-done((f32[104,256]{1,0:T(8,128)S(1)}, f32[104,256]{1,0:T(8,128)S(1)}, u32[]{:S(2)}, u32[]{:S(2)}) %collective-permute-start.7) | collective-permute-done | bytes 106528 | tf_op jit(solution)/shard_map/ppermute | solution.py:561
  17.9 0.1 shard_map.97
  18.0 2.9 %collective-permute-start.11 = (f32[104,256]{1,0:T(8,128)S(1)}, f32[104,256]{1,0:T(8,128)S(1)}, u32[]{:S(2)}, u32[]{:S(2)}) collective-permute-start(f32[104,256]{1,0:T(8,128)S(1)} %get-tuple-element.116), channel_id=1, source_target_pairs={{0,4},{1,5},{2,6},{3,7},{4,0},{5,1},{6,2},{7,3},{8,12},{9,13},{10,... | collective-permute-start | bytes 319496 | tf_op jit(solution)/shard_map/ppermute | solution.py:561
  20.9 0.5 %shard_map.98 = (f32[3,256,256]{2,1,0:T(8,128)S(1)}, f32[3,256,256]{2,1,0:T(8,128)S(1)}) custom-call(f32[3,256,256]{2,1,0:T(8,128)S(1)} %get-tuple-element.105.u, f32[3,256,256]{2,1,0:T(8,128)S(1)} %get-tuple-element.106.v, f32[3,256,256]{2,1,0:T(8,128)S(1)} %bitcast.12, f32[288,256]{1,0:T(8,128)S(1)} %get-tuple-element.73.kx, ...), custom_call_target="tpu_custom_call", output_to_operand_aliasing={{1}: (1, {})} | custom-call | flops 1 | bytes 1 | tf_op jit(solution)/shard_map/pallas_call | solution.py:58
  21.3 0.0 collective-permute-done.9.ya
  21.3 0.0 collective-permute-done.10.yb
  21.3 0.0 collective-permute-done.8.hb
  21.4 0.1 shard_map.99
  21.4 0.1 collective-permute-start.12
  21.5 0.4 %shard_map.100 = (f32[3,256,256]{2,1,0:T(8,128)S(1)}, f32[3,256,256]{2,1,0:T(8,128)S(1)}) custom-call(f32[3,256,256]{2,1,0:T(8,128)S(1)} %get-tuple-element.112.u1, f32[3,256,256]{2,1,0:T(8,128)S(1)} %get-tuple-element.113.v, f32[3,256,256]{2,1,0:T(8,128)S(1)} %get-tuple-element.105.u, ...), custom_call_target="tpu_custom_call", output_to_operand_aliasing={{0}: (0, {}), {1}: (1, {})} | custom-call | flops 1 | bytes 1 | tf_op jit(solution)/shard_map/pallas_call | solution.py:58
  21.9 2.2 %collective-permute-done.11.ha = f32[104,256]{1,0:T(8,128)S(1)} collective-permute-done((f32[104,256]{1,0:T(8,128)S(1)}, f32[104,256]{1,0:T(8,128)S(1)}, u32[]{:S(2)}, u32[]{:S(2)}) %collective-permute-start.11) | collective-permute-done | bytes 106528 | tf_op jit(solution)/shard_map/ppermute | solution.py:561
  24.1 0.1 shard_map.101
  24.2 1.8 %collective-permute-start.13 = (f32[96,256]{1,0:T(8,128)S(1)}, f32[96,256]{1,0:T(8,128)S(1)}, u32[]{:S(2)}, u32[]{:S(2)}) collective-permute-start(f32[96,256]{1,0:T(8,128)S(1)} %get-tuple-element.123.refs_1_), channel_id=1, source_target_pairs={{0,4},{1,5},{2,6},{3,7},{4,0},{5,1},{6,2},{7,3},{8,12},{9,13},{10,... | collective-permute-start | bytes 294920 | tf_op jit(solution)/shard_map/ppermute | solution.py:561
  26.0 0.0 collective-permute-start.15
  26.0 0.9 %collective-permute-start.14 = (f32[3,8,256]{2,1,0:T(8,128)S(1)}, f32[3,8,256]{2,1,0:T(8,128)S(1)}, u32[]{:S(2)}, u32[]{:S(2)}) collective-permute-start(f32[3,8,256]{2,1,0:T(8,128)S(1)} %get-tuple-element.124), channel_id=1, source_target_pairs={{0,1},{1,0},{2,3},{3,2},{4,5},{5,4},{6,7},{7,6},{8,9},{9,8},{10,11... | collective-permute-start | bytes 73736 | tf_op jit(solution)/shard_map/ppermute | solution.py:562
  26.9 0.0 collective-permute-done.12.hb
  26.9 1.5 %shard_map.102 = (f32[3,256,256]{2,1,0:T(8,128)S(1)}, f32[3,256,256]{2,1,0:T(8,128)S(1)}, f32[3,256,256]{2,1,0:T(8,128)}, f32[3,256,256]{2,1,0:T(8,128)}) custom-call(f32[3,256,256]{2,1,0:T(8,128)S(1)} %get-tuple-element.118.u, f32[3,256,256]{2,1,0:T(8,128)S(1)} %get-tuple-element.119.v, ...), custom_call_target="tpu_custom_call", output_to_operand_aliasing={{1}: (1, {})} | custom-call | flops 1 | bytes 1 | tf_op jit(solution)/shard_map/pallas_call | solution.py:58
  28.4 0.8 %collective-permute-done.15.yb = f32[3,8,256]{2,1,0:T(8,128)S(1)} collective-permute-done((f32[3,8,256]{2,1,0:T(8,128)S(1)}, f32[3,8,256]{2,1,0:T(8,128)S(1)}, u32[]{:S(2)}, u32[]{:S(2)}) %collective-permute-start.15) | collective-permute-done | bytes 24608 | tf_op jit(solution)/shard_map/ppermute | solution.py:558
  29.2 0.0 collective-permute-done.14.ya
  29.2 0.0 collective-permute-done.13.ha
  29.2 1.0 %shard_map.104 = (f32[3,256,256]{2,1,0:T(8,128)S(1)}, f32[3,256,256]{2,1,0:T(8,128)S(1)}, f32[3,256,256]{2,1,0:T(8,128)}, f32[3,256,256]{2,1,0:T(8,128)}) custom-call(f32[3,256,256]{2,1,0:T(8,128)S(1)} %get-tuple-element.121.u1, f32[3,256,256]{2,1,0:T(8,128)S(1)} %get-tuple-element.122.v1, ...), custom_call_target="tpu_custom_call", output_to_operand_aliasing={{0}: (0, {}), {1}: (1, {}), {2}: (10, {}), {3}: (11, {})} | custom-call | flops 1 | bytes 1 | tf_op jit(solution)/shard_map/pallas_call | solution.py:58
  (3 shorter events, 0.0 us)
Async XLA Ops:
  0.6 1.8 %copy-start.1 = (f32[3,8,32,256]{3,2,1,0:T(8,128)S(1)}, f32[3,8,32,256]{3,2,1,0:T(8,128)}, u32[]{:S(2)}) copy-start(f32[3,8,32,256]{3,2,1,0:T(8,128)} %param.7) | copy-start | bytes 2359300
  0.6 1.7 %copy-start.3 = (s32[8,32,256]{2,1,0:T(8,128)S(1)}, s32[8,32,256]{2,1,0:T(8,128)}, u32[]{:S(2)}) copy-start(s32[8,32,256]{2,1,0:T(8,128)} %param.12) | copy-start | bytes 786436
  0.7 1.7 %copy-start.4 = (s32[8,32,256]{2,1,0:T(8,128)S(1)}, s32[8,32,256]{2,1,0:T(8,128)}, u32[]{:S(2)}) copy-start(s32[8,32,256]{2,1,0:T(8,128)} %param.11) | copy-start | bytes 786436
  1.9 7.7 %collective-permute-start.2 = (f32[4,32,256]{2,1,0:T(8,128)S(1)}, f32[4,32,256]{2,1,0:T(8,128)S(1)}, u32[]{:S(2)}, u32[]{:S(2)}) collective-permute-start(f32[4,32,256]{2,1,0:T(8,128)S(1)} %get-tuple-element.77.b_sent), channel_id=1, source_target_pairs={{0,1},{1,0},{2,3},{3,2},{4,8},{5,9},{6,10},{7,11},{8,4},{9,5},{10,... | collective-permute-start | bytes 393224 | tf_op jit(solution)/shard_map/ppermute | solution.py:555
  2.4 5.9 %copy-start = (f32[3,8,32,256]{3,2,1,0:T(8,128)S(1)}, f32[3,8,32,256]{3,2,1,0:T(8,128)}, u32[]{:S(2)}) copy-start(f32[3,8,32,256]{3,2,1,0:T(8,128)} %param.9) | copy-start | bytes 2359300
  2.4 5.9 %copy-start.2 = (f32[3,8,32,256]{3,2,1,0:T(8,128)S(1)}, f32[3,8,32,256]{3,2,1,0:T(8,128)}, u32[]{:S(2)}) copy-start(f32[3,8,32,256]{3,2,1,0:T(8,128)} %param.8) | copy-start | bytes 2359300
  2.6 6.5 %collective-permute-start = (f32[4,8,256]{2,1,0:T(8,128)S(1)}, f32[4,8,256]{2,1,0:T(8,128)S(1)}, u32[]{:S(2)}, u32[]{:S(2)}) collective-permute-start(f32[4,8,256]{2,1,0:T(8,128)S(1)} %get-tuple-element.78.ya_sent), channel_id=1, source_target_pairs={{0,1},{1,0},{2,3},{3,2},{4,5},{5,4},{6,7},{7,6},{8,9},{9,8},{10,11... | collective-permute-start | bytes 98312 | tf_op jit(solution)/shard_map/ppermute | solution.py:562
  2.7 6.4 %collective-permute-start.1 = (f32[4,8,256]{2,1,0:T(8,128)S(1)}, f32[4,8,256]{2,1,0:T(8,128)S(1)}, u32[]{:S(2)}, u32[]{:S(2)}) collective-permute-start(f32[4,8,256]{2,1,0:T(8,128)S(1)} %get-tuple-element.79.yb_sent.refs_1_), channel_id=1, source_target_pairs={{0,3},{1,2},{2,1},{3,0},{4,7},{5,6},{6,5},{7,4},{8,11},{9,10},{10,... | collective-permute-start | bytes 98312 | tf_op jit(solution)/shard_map/ppermute | solution.py:558
  5.3 6.7 %collective-permute-start.3 = (f32[4,32,256]{2,1,0:T(8,128)S(1)}, f32[4,32,256]{2,1,0:T(8,128)S(1)}, u32[]{:S(2)}, u32[]{:S(2)}) collective-permute-start(f32[4,32,256]{2,1,0:T(8,128)S(1)} %shard_map.91.a_sent), channel_id=1, source_target_pairs={{0,4},{1,5},{2,6},{3,7},{4,0},{5,1},{6,2},{7,3},{8,12},{9,13},{10,... | collective-permute-start | bytes 393224 | tf_op jit(solution)/shard_map/ppermute | solution.py:561
  9.6 5.6 %collective-permute-start.4 = (f32[3,32,256]{2,1,0:T(8,128)S(1)}, f32[3,32,256]{2,1,0:T(8,128)S(1)}, u32[]{:S(2)}, u32[]{:S(2)}) collective-permute-start(f32[3,32,256]{2,1,0:T(8,128)S(1)} %get-tuple-element.95), channel_id=1, source_target_pairs={{0,1},{1,0},{2,3},{3,2},{4,8},{5,9},{6,10},{7,11},{8,4},{9,5},{10,... | collective-permute-start | bytes 294920 | tf_op jit(solution)/shard_map/ppermute | solution.py:555
  9.8 5.4 %collective-permute-start.5 = (f32[4,8,256]{2,1,0:T(8,128)S(1)}, f32[4,8,256]{2,1,0:T(8,128)S(1)}, u32[]{:S(2)}, u32[]{:S(2)}) collective-permute-start(f32[4,8,256]{2,1,0:T(8,128)S(1)} %get-tuple-element.96), channel_id=1, source_target_pairs={{0,1},{1,0},{2,3},{3,2},{4,5},{5,4},{6,7},{7,6},{8,9},{9,8},{10,11... | collective-permute-start | bytes 98312 | tf_op jit(solution)/shard_map/ppermute | solution.py:562
  10.4 4.8 %collective-permute-start.6 = (f32[4,8,256]{2,1,0:T(8,128)S(1)}, f32[4,8,256]{2,1,0:T(8,128)S(1)}, u32[]{:S(2)}, u32[]{:S(2)}) collective-permute-start(f32[4,8,256]{2,1,0:T(8,128)S(1)} %get-tuple-element.97), channel_id=1, source_target_pairs={{0,3},{1,2},{2,1},{3,0},{4,7},{5,6},{6,5},{7,4},{8,11},{9,10},{10,... | collective-permute-start | bytes 98312 | tf_op jit(solution)/shard_map/ppermute | solution.py:558
  12.1 5.8 %collective-permute-start.7 = (f32[104,256]{1,0:T(8,128)S(1)}, f32[104,256]{1,0:T(8,128)S(1)}, u32[]{:S(2)}, u32[]{:S(2)}) collective-permute-start(f32[104,256]{1,0:T(8,128)S(1)} %get-tuple-element.103), channel_id=1, source_target_pairs={{0,4},{1,5},{2,6},{3,7},{4,0},{5,1},{6,2},{7,3},{8,12},{9,13},{10,... | collective-permute-start | bytes 319496 | tf_op jit(solution)/shard_map/ppermute | solution.py:561
  15.3 6.1 %collective-permute-start.8 = (f32[3,32,256]{2,1,0:T(8,128)S(1)}, f32[3,32,256]{2,1,0:T(8,128)S(1)}, u32[]{:S(2)}, u32[]{:S(2)}) collective-permute-start(f32[3,32,256]{2,1,0:T(8,128)S(1)} %get-tuple-element.109), channel_id=1, source_target_pairs={{0,1},{1,0},{2,3},{3,2},{4,8},{5,9},{6,10},{7,11},{8,4},{9,5},{10,... | collective-permute-start | bytes 294920 | tf_op jit(solution)/shard_map/ppermute | solution.py:555
  15.8 5.5 %collective-permute-start.9 = (f32[3,8,256]{2,1,0:T(8,128)S(1)}, f32[3,8,256]{2,1,0:T(8,128)S(1)}, u32[]{:S(2)}, u32[]{:S(2)}) collective-permute-start(f32[3,8,256]{2,1,0:T(8,128)S(1)} %get-tuple-element.110), channel_id=1, source_target_pairs={{0,1},{1,0},{2,3},{3,2},{4,5},{5,4},{6,7},{7,6},{8,9},{9,8},{10,11... | collective-permute-start | bytes 73736 | tf_op jit(solution)/shard_map/ppermute | solution.py:562
  16.4 5.0 %collective-permute-start.10 = (f32[3,8,256]{2,1,0:T(8,128)S(1)}, f32[3,8,256]{2,1,0:T(8,128)S(1)}, u32[]{:S(2)}, u32[]{:S(2)}) collective-permute-start(f32[3,8,256]{2,1,0:T(8,128)S(1)} %get-tuple-element.111), channel_id=1, source_target_pairs={{0,3},{1,2},{2,1},{3,0},{4,7},{5,6},{6,5},{7,4},{8,11},{9,10},{10,... | collective-permute-start | bytes 73736 | tf_op jit(solution)/shard_map/ppermute | solution.py:558
  18.0 6.1 %collective-permute-start.11 = (f32[104,256]{1,0:T(8,128)S(1)}, f32[104,256]{1,0:T(8,128)S(1)}, u32[]{:S(2)}, u32[]{:S(2)}) collective-permute-start(f32[104,256]{1,0:T(8,128)S(1)} %get-tuple-element.116), channel_id=1, source_target_pairs={{0,4},{1,5},{2,6},{3,7},{4,0},{5,1},{6,2},{7,3},{8,12},{9,13},{10,... | collective-permute-start | bytes 319496 | tf_op jit(solution)/shard_map/ppermute | solution.py:561
  21.4 5.5 %collective-permute-start.12 = (f32[3,32,256]{2,1,0:T(8,128)S(1)}, f32[3,32,256]{2,1,0:T(8,128)S(1)}, u32[]{:S(2)}, u32[]{:S(2)}) collective-permute-start(f32[3,32,256]{2,1,0:T(8,128)S(1)} %get-tuple-element.120), channel_id=1, source_target_pairs={{0,1},{1,0},{2,3},{3,2},{4,8},{5,9},{6,10},{7,11},{8,4},{9,5},{10,... | collective-permute-start | bytes 294920 | tf_op jit(solution)/shard_map/ppermute | solution.py:555
  24.2 5.1 %collective-permute-start.13 = (f32[96,256]{1,0:T(8,128)S(1)}, f32[96,256]{1,0:T(8,128)S(1)}, u32[]{:S(2)}, u32[]{:S(2)}) collective-permute-start(f32[96,256]{1,0:T(8,128)S(1)} %get-tuple-element.123.refs_1_), channel_id=1, source_target_pairs={{0,4},{1,5},{2,6},{3,7},{4,0},{5,1},{6,2},{7,3},{8,12},{9,13},{10,... | collective-permute-start | bytes 294920 | tf_op jit(solution)/shard_map/ppermute | solution.py:561
  26.0 3.3 %collective-permute-start.15 = (f32[3,8,256]{2,1,0:T(8,128)S(1)}, f32[3,8,256]{2,1,0:T(8,128)S(1)}, u32[]{:S(2)}, u32[]{:S(2)}) collective-permute-start(f32[3,8,256]{2,1,0:T(8,128)S(1)} %shard_map.103), channel_id=1, source_target_pairs={{0,3},{1,2},{2,1},{3,0},{4,7},{5,6},{6,5},{7,4},{8,11},{9,10},{10,... | collective-permute-start | bytes 73736 | tf_op jit(solution)/shard_map/ppermute | solution.py:558
  26.0 3.3 %collective-permute-start.14 = (f32[3,8,256]{2,1,0:T(8,128)S(1)}, f32[3,8,256]{2,1,0:T(8,128)S(1)}, u32[]{:S(2)}, u32[]{:S(2)}) collective-permute-start(f32[3,8,256]{2,1,0:T(8,128)S(1)} %get-tuple-element.124), channel_id=1, source_target_pairs={{0,1},{1,0},{2,3},{3,2},{4,5},{5,4},{6,7},{7,6},{8,9},{9,8},{10,11... | collective-permute-start | bytes 73736 | tf_op jit(solution)/shard_map/ppermute | solution.py:562

commit v8 on v7

--- a/solution.py
+++ b/solution.py
@@ -482,10 +482,9 @@
 
 
 def last_outer(
-    cx, cy, u1, v1, u, rate, ha, ka, ya, yb, kyd, kyu, u_in, v_in, u_new, v_new, u_hbm, v_hbm, sems
+    cx, cy, u1, v1, u, rate, ha, ka, yb, kyd, kyu, u_in, v_in, u_new, v_new, u_hbm, v_hbm, sems
 ):
     fa = sides(cx)[0]
-    row = lax.broadcasted_iota(jnp.int32, (TILE, u.shape[-1]), 0)
     copies = []
 
     def send(layers, rows):
@@ -496,20 +495,34 @@
             copies.append(copy)
 
     fix_face(layer(fa, cy), u, rate, ka[...], lambda c: ha[c * cy : (c + 1) * cy, :], u_new, v_new)
+    even = plane_even()
+    ready = jnp.where(even, cy - TILE, 0)
+    send(pl.ds(0, cx), run(ready, TILE))
     send(pl.ds(fa, 1), pl.ds(TILE, cy - 2 * TILE))
-    for side, (edge, stiff) in enumerate(((0, kyd), (TILE - 1, kyu))):
-        offset = 0 if side == 0 else cy - TILE
-        for x in range(cx):
-            at = slice(x * cy + offset, x * cy + offset + TILE)
-            k = jnp.where(row == edge, stiff[at, :], 0.0)
-            r = rate[at, :]
-            for c in range(3):
-                push = r * (k * (halo_rows(ya, yb, c, x)[side] - u[c, at, :]))
-                v_new[c, at, :] += push
-                u_new[c, at, :] += r * push
-        send(pl.ds(0, cx), pl.ds(offset, TILE))
+    for x in range(cx):
+        fix_edge(cx, cy, x, True, u, rate, yb, kyd, kyu, u_new, v_new)
+    send(pl.ds(0, cx), run(cy - TILE - ready, TILE))
     for copy in copies:
         copy.wait()
+
+
+def last_first_plane(cx, cy, u1, v1, u, rate, ya, kyd, kyu, u_new, v_new):
+    for x in range(cx):
+        fix_edge(cx, cy, x, False, u, rate, ya, kyd, kyu, u_new, v_new)
+
+
+def fix_edge(cx, cy, x, second, u, rate, halo, kyd, kyu, u_new, v_new):
+    even = plane_even()
+    high = jnp.logical_not(even) if second else even
+    at = run(jnp.where(high, (x + 1) * cy - TILE, x * cy), TILE)
+    row = lax.broadcasted_iota(jnp.int32, (TILE, u.shape[-1]), 0)
+    edge = jnp.where(high, TILE - 1, 0)
+    k = jnp.where(row == edge, jnp.where(high, kyu[at, :], kyd[at, :]), 0.0)
+    r = rate[at, :]
+    for c in range(3):
+        push = r * (k * (halo[c, x : x + 1, :] - u[c, at, :]))
+        v_new[c, at, :] += push
+        u_new[c, at, :] += r * push
 
 
 def per_device(displacement, velocity, body_load, damaged, eroded, material, stiff_table):
@@ -637,11 +650,12 @@
         scratch=[pltpu.SemaphoreType.DMA((2 * (cx - 1),))],
         to_hbm=[field, field],
     )
+    u_new, v = call(bind(last_first_plane), [field, field], (u_new, v, u, fine, hya, kyd, kyu), both)
     out = call(
         bind(last_outer),
         [field, field],
-        (u_new, v, u, fine, ha, ka, hya, hyb, kyd, kyu),
-        {0: 0, 1: 1, 10: 2, 11: 3},
+        (u_new, v, u, fine, ha, ka, hyb, kyd, kyu),
+        {0: 0, 1: 1, 9: 2, 10: 3},
         in_hbm=out,
         scratch=[pltpu.SemaphoreType.DMA((6,))],
         to_hbm=[field, field],

time: 30.4 us -> 30.4 us (level)
    ppermute x4, starting transfers between devices: 2.18 us -> 1.26 us  [per_device(): hya = lax.ppermute(ya, AXES, pa)]
    ppermute x4, starting transfers between devices: 3.24 us -> 4.16 us  [per_device(): hyb = lax.ppermute(yb, AXES, pb)]
    pallas_call x19 -> x20, Pallas kernels: 7.41 us -> 7.46 us  [call(): pl.pallas_call(kernel, in_specs=[VMEM] * len(arrays) + [HBM] * len(in_hbm...]
where the time goes in v8:
time: 30.4 us; the launch traced here: 30.2 us
  starting transfers between devices  16.4 us (54%)
  Pallas kernels  7.46 us (25%)
  waiting for transfers between devices  5.46 us (18%)
  between operations  0.85 us (3%)
    ppermute x4, starting transfers between devices, per_device(): ha = lax.ppermute(a, AXES, xa)  10.3 us
    pallas_call x20, Pallas kernels, call(): pl.pallas_call(kernel, in_specs=[VMEM] * len(arrays) + [HBM] * len(in_hbm...  7.46 us
    ppermute x4, waiting for transfers between devices, per_device(): ha = lax.ppermute(a, AXES, xa)  4.73 us
    ppermute x4, starting transfers between devices, per_device(): hyb = lax.ppermute(yb, AXES, pb)  4.16 us
    ppermute x4, starting transfers between devices, per_device(): hya = lax.ppermute(ya, AXES, pa)  1.26 us
    ppermute x4, starting transfers between devices, per_device(): hb = lax.ppermute(b, AXES, xb)  0.73 us
    ppermute x4, waiting for transfers between devices, per_device(): hyb = lax.ppermute(yb, AXES, pb)  0.71 us
  transfers between devices with their start and end apart: 16, of which 4 were waited for; matrix products, arithmetic and copies ran while one was open for 0% of the time, Pallas kernels for 17%

profile of v8, /device:TPU:0, one launch (start us, length us, event | category | flops | bytes accessed | tf_op | source)
XLA Modules:
  0.0 30.2 jit_solution(14761598576619347473)
XLA Ops:
  0.6 0.0 copy-start.1
  0.6 0.0 copy-start.3
  0.7 0.0 copy-start.4
  0.7 1.2 %shard_map.86 = (f32[4,32,256]{2,1,0:T(8,128)S(1)}, f32[8,256]{1,0:T(8,128)S(1)}, s32[256,256]{1,0:T(8,128)S(1)}) custom-call(f32[3,256,256]{2,1,0:T(8,128)} %bitcast.15, s32[256,256]{1,0:T(8,128)} %bitcast.23, s32[256,256]{1,0:T(8,128)} %bitcast.26, f32[8]{0:T(128)} %table_hbm.1, s32[256,256]{1,0:T(8,128)} %bitcast.31), custom_call_target="tpu_custom_call" | custom-call | flops 1 | bytes 1 | tf_op jit(solution)/shard_map/pallas_call | solution.py:58
  1.9 0.5 %collective-permute-start.2 = (f32[4,32,256]{2,1,0:T(8,128)S(1)}, f32[4,32,256]{2,1,0:T(8,128)S(1)}, u32[]{:S(2)}, u32[]{:S(2)}) collective-permute-start(f32[4,32,256]{2,1,0:T(8,128)S(1)} %get-tuple-element.79.b_sent), channel_id=1, source_target_pairs={{0,1},{1,0},{2,3},{3,2},{4,8},{5,9},{6,10},{7,11},{8,4},{9,5},{10,... | collective-permute-start | bytes 393224 | tf_op jit(solution)/shard_map/ppermute | solution.py:568
  2.4 0.0 copy-done.1
  2.4 0.0 copy-done.3
  2.4 0.0 copy-done.4
  2.4 0.0 copy-start
  2.4 0.0 copy-start.2
  2.4 0.1 shard_map.88
  2.6 0.2 collective-permute-start
  2.7 2.6 %collective-permute-start.1 = (f32[4,8,256]{2,1,0:T(8,128)S(1)}, f32[4,8,256]{2,1,0:T(8,128)S(1)}, u32[]{:S(2)}, u32[]{:S(2)}) collective-permute-start(f32[4,8,256]{2,1,0:T(8,128)S(1)} %get-tuple-element.81.yb_sent.refs_1_), channel_id=1, source_target_pairs={{0,3},{1,2},{2,1},{3,0},{4,7},{5,6},{6,5},{7,4},{8,11},{9,10},{10,... | collective-permute-start | bytes 98312 | tf_op jit(solution)/shard_map/ppermute | solution.py:571
  5.3 3.0 %collective-permute-start.3 = (f32[4,32,256]{2,1,0:T(8,128)S(1)}, f32[4,32,256]{2,1,0:T(8,128)S(1)}, u32[]{:S(2)}, u32[]{:S(2)}) collective-permute-start(f32[4,32,256]{2,1,0:T(8,128)S(1)} %shard_map.91.a_sent), channel_id=1, source_target_pairs={{0,4},{1,5},{2,6},{3,7},{4,0},{5,1},{6,2},{7,3},{8,12},{9,13},{10,... | collective-permute-start | bytes 393224 | tf_op jit(solution)/shard_map/ppermute | solution.py:574
  8.3 0.0 copy-done
  8.3 0.0 copy-done.2
  8.3 0.8 %shard_map.87 = (f32[3,256,256]{2,1,0:T(8,128)S(1)}, f32[3,256,256]{2,1,0:T(8,128)S(1)}, f32[288,256]{1,0:T(8,128)S(1)}, f32[256,256]{1,0:T(8,128)S(1)}, f32[256...) custom-call(f32[3,256,256]{2,1,0:T(8,128)S(1)} %bitcast.17, ...), custom_call_target="tpu_custom_call" | custom-call | flops 1 | bytes 1 | tf_op jit(solution)/shard_map/pallas_call | solution.py:58
  9.1 0.0 collective-permute-done.ya.old_ya
  9.1 0.0 collective-permute-done.1.yb.old_yb
  9.1 0.4 %shard_map.89 = (f32[3,256,256]{2,1,0:T(8,128)S(1)}, f32[3,256,256]{2,1,0:T(8,128)S(1)}, f32[256,256]{1,0:T(8,128)S(1)}, f32[256,256]{1,0:T(8,128)S(1)}, f32[256...) custom-call(f32[3,256,256]{2,1,0:T(8,128)S(1)} %get-tuple-element.70, ...), custom_call_target="tpu_custom_call", output_to_operand_aliasing={{0}: (0, {}), {1}: (1, {}), {2}: (2, {}), {3}: (3, {}), {4}... | custom-call | flops 1 | bytes 1 | tf_op jit(solution)/shard_map/pallas_call | solution.py:58
  9.6 0.0 collective-permute-done.2.hb
  9.6 0.1 shard_map.90
  9.6 0.1 collective-permute-start.4
  9.7 0.1 shard_map.94
  9.8 0.6 %collective-permute-start.5 = (f32[4,8,256]{2,1,0:T(8,128)S(1)}, f32[4,8,256]{2,1,0:T(8,128)S(1)}, u32[]{:S(2)}, u32[]{:S(2)}) collective-permute-start(f32[4,8,256]{2,1,0:T(8,128)S(1)} %get-tuple-element.98), channel_id=1, source_target_pairs={{0,1},{1,0},{2,3},{3,2},{4,5},{5,4},{6,7},{7,6},{8,9},{9,8},{10,11... | collective-permute-start | bytes 98312 | tf_op jit(solution)/shard_map/ppermute | solution.py:575
  10.4 0.2 collective-permute-start.6
  10.6 1.5 %collective-permute-done.3.ha = f32[4,32,256]{2,1,0:T(8,128)S(1)} collective-permute-done((f32[4,32,256]{2,1,0:T(8,128)S(1)}, f32[4,32,256]{2,1,0:T(8,128)S(1)}, u32[]{:S(2)}, u32[]{:S(2)}) %collective-permute-start.3) | collective-permute-done | bytes 131104 | tf_op jit(solution)/shard_map/ppermute | solution.py:574
  12.1 2.6 %collective-permute-start.7 = (f32[104,256]{1,0:T(8,128)S(1)}, f32[104,256]{1,0:T(8,128)S(1)}, u32[]{:S(2)}, u32[]{:S(2)}) collective-permute-start(f32[104,256]{1,0:T(8,128)S(1)} %get-tuple-element.105), channel_id=1, source_target_pairs={{0,4},{1,5},{2,6},{3,7},{4,0},{5,1},{6,2},{7,3},{8,12},{9,13},{10,... | collective-permute-start | bytes 319496 | tf_op jit(solution)/shard_map/ppermute | solution.py:574
  14.7 0.5 %shard_map.93 = (f32[3,256,256]{2,1,0:T(8,128)S(1)}, f32[3,256,256]{2,1,0:T(8,128)S(1)}) custom-call(f32[3,256,256]{2,1,0:T(8,128)S(1)} %get-tuple-element.89.u, f32[3,256,256]{2,1,0:T(8,128)S(1)} %get-tuple-element.90.v, f32[3,256,256]{2,1,0:T(8,128)S(1)} %bitcast.10, f32[288,256]{1,0:T(8,128)S(1)} %get-tuple-element.75.kx, ...), custom_call_target="tpu_custom_call", output_to_operand_aliasing={{1}: (1, {})} | custom-call | flops 1 | bytes 1 | tf_op jit(solution)/shard_map/pallas_call | solution.py:58
  15.2 0.0 collective-permute-done.5.ya
  15.2 0.0 collective-permute-done.6.yb
  15.2 0.0 collective-permute-done.4.hb
  15.2 0.1 shard_map.95
  15.3 0.1 collective-permute-start.8
  15.4 0.5 %shard_map.96 = (f32[3,256,256]{2,1,0:T(8,128)S(1)}, f32[3,256,256]{2,1,0:T(8,128)S(1)}, f32[3,8,256]{2,1,0:T(8,128)S(1)}, f32[3,8,256]{2,1,0:T(8,128)S(1)}) custom-call(f32[3,256,256]{2,1,0:T(8,128)S(1)} %get-tuple-element.101.u1, f32[3,256,256]{2,1,0:T(8,128)S(1)} %get-tuple-element.102.v, ...), custom_call_target="tpu_custom_call", output_to_operand_aliasing={{0}: (0, {}), {1}: (1, {})} | custom-call | flops 1 | bytes 1 | tf_op jit(solution)/shard_map/pallas_call | solution.py:58
  15.8 0.5 %collective-permute-start.9 = (f32[3,8,256]{2,1,0:T(8,128)S(1)}, f32[3,8,256]{2,1,0:T(8,128)S(1)}, u32[]{:S(2)}, u32[]{:S(2)}) collective-permute-start(f32[3,8,256]{2,1,0:T(8,128)S(1)} %get-tuple-element.112), channel_id=1, source_target_pairs={{0,1},{1,0},{2,3},{3,2},{4,5},{5,4},{6,7},{7,6},{8,9},{9,8},{10,11... | collective-permute-start | bytes 73736 | tf_op jit(solution)/shard_map/ppermute | solution.py:575
  16.4 0.4 %collective-permute-start.10 = (f32[3,8,256]{2,1,0:T(8,128)S(1)}, f32[3,8,256]{2,1,0:T(8,128)S(1)}, u32[]{:S(2)}, u32[]{:S(2)}) collective-permute-start(f32[3,8,256]{2,1,0:T(8,128)S(1)} %get-tuple-element.113), channel_id=1, source_target_pairs={{0,3},{1,2},{2,1},{3,0},{4,7},{5,6},{6,5},{7,4},{8,11},{9,10},{10,... | collective-permute-start | bytes 73736 | tf_op jit(solution)/shard_map/ppermute | solution.py:571
  16.8 1.1 %collective-permute-done.7.ha = f32[104,256]{1,0:T(8,128)S(1)} collective-permute-done((f32[104,256]{1,0:T(8,128)S(1)}, f32[104,256]{1,0:T(8,128)S(1)}, u32[]{:S(2)}, u32[]{:S(2)}) %collective-permute-start.7) | collective-permute-done | bytes 106528 | tf_op jit(solution)/shard_map/ppermute | solution.py:574
  17.9 0.1 shard_map.97
  18.0 2.9 %collective-permute-start.11 = (f32[104,256]{1,0:T(8,128)S(1)}, f32[104,256]{1,0:T(8,128)S(1)}, u32[]{:S(2)}, u32[]{:S(2)}) collective-permute-start(f32[104,256]{1,0:T(8,128)S(1)} %get-tuple-element.118), channel_id=1, source_target_pairs={{0,4},{1,5},{2,6},{3,7},{4,0},{5,1},{6,2},{7,3},{8,12},{9,13},{10,... | collective-permute-start | bytes 319496 | tf_op jit(solution)/shard_map/ppermute | solution.py:574
  20.9 0.5 %shard_map.98 = (f32[3,256,256]{2,1,0:T(8,128)S(1)}, f32[3,256,256]{2,1,0:T(8,128)S(1)}) custom-call(f32[3,256,256]{2,1,0:T(8,128)S(1)} %get-tuple-element.107.u, f32[3,256,256]{2,1,0:T(8,128)S(1)} %get-tuple-element.108.v, f32[3,256,256]{2,1,0:T(8,128)S(1)} %bitcast.12, f32[288,256]{1,0:T(8,128)S(1)} %get-tuple-element.75.kx, ...), custom_call_target="tpu_custom_call", output_to_operand_aliasing={{1}: (1, {})} | custom-call | flops 1 | bytes 1 | tf_op jit(solution)/shard_map/pallas_call | solution.py:58
  21.3 0.0 collective-permute-done.9.ya
  21.3 0.0 collective-permute-done.10.yb
  21.3 0.0 collective-permute-done.8.hb
  21.4 0.1 shard_map.99
  21.4 0.1 collective-permute-start.12
  21.5 0.4 %shard_map.100 = (f32[3,256,256]{2,1,0:T(8,128)S(1)}, f32[3,256,256]{2,1,0:T(8,128)S(1)}) custom-call(f32[3,256,256]{2,1,0:T(8,128)S(1)} %get-tuple-element.114.u1, f32[3,256,256]{2,1,0:T(8,128)S(1)} %get-tuple-element.115.v, f32[3,256,256]{2,1,0:T(8,128)S(1)} %get-tuple-element.107.u, ...), custom_call_target="tpu_custom_call", output_to_operand_aliasing={{0}: (0, {}), {1}: (1, {})} | custom-call | flops 1 | bytes 1 | tf_op jit(solution)/shard_map/pallas_call | solution.py:58
  21.9 2.2 %collective-permute-done.11.ha = f32[104,256]{1,0:T(8,128)S(1)} collective-permute-done((f32[104,256]{1,0:T(8,128)S(1)}, f32[104,256]{1,0:T(8,128)S(1)}, u32[]{:S(2)}, u32[]{:S(2)}) %collective-permute-start.11) | collective-permute-done | bytes 106528 | tf_op jit(solution)/shard_map/ppermute | solution.py:574
  24.1 0.1 shard_map.101
  24.2 1.8 %collective-permute-start.14 = (f32[96,256]{1,0:T(8,128)S(1)}, f32[96,256]{1,0:T(8,128)S(1)}, u32[]{:S(2)}, u32[]{:S(2)}) collective-permute-start(f32[96,256]{1,0:T(8,128)S(1)} %get-tuple-element.128.refs_1_), channel_id=1, source_target_pairs={{0,4},{1,5},{2,6},{3,7},{4,0},{5,1},{6,2},{7,3},{8,12},{9,13},{10,... | collective-permute-start | bytes 294920 | tf_op jit(solution)/shard_map/ppermute | solution.py:574
  26.0 0.0 collective-permute-start.13
  26.0 0.9 %collective-permute-start.15 = (f32[3,8,256]{2,1,0:T(8,128)S(1)}, f32[3,8,256]{2,1,0:T(8,128)S(1)}, u32[]{:S(2)}, u32[]{:S(2)}) collective-permute-start(f32[3,8,256]{2,1,0:T(8,128)S(1)} %shard_map.104), channel_id=1, source_target_pairs={{0,3},{1,2},{2,1},{3,0},{4,7},{5,6},{6,5},{7,4},{8,11},{9,10},{10,... | collective-permute-start | bytes 73736 | tf_op jit(solution)/shard_map/ppermute | solution.py:571
  26.9 0.0 collective-permute-done.12.hb
  26.9 1.5 %shard_map.102 = (f32[3,256,256]{2,1,0:T(8,128)S(1)}, f32[3,256,256]{2,1,0:T(8,128)S(1)}, f32[3,256,256]{2,1,0:T(8,128)}, f32[3,256,256]{2,1,0:T(8,128)}) custom-call(f32[3,256,256]{2,1,0:T(8,128)S(1)} %get-tuple-element.120.u, f32[3,256,256]{2,1,0:T(8,128)S(1)} %get-tuple-element.121.v, ...), custom_call_target="tpu_custom_call", output_to_operand_aliasing={{1}: (1, {})} | custom-call | flops 1 | bytes 1 | tf_op jit(solution)/shard_map/pallas_call | solution.py:58
  28.4 0.0 collective-permute-done.13.ya
  28.4 0.1 shard_map.103
  28.5 0.7 %collective-permute-done.15.yb = f32[3,8,256]{2,1,0:T(8,128)S(1)} collective-permute-done((f32[3,8,256]{2,1,0:T(8,128)S(1)}, f32[3,8,256]{2,1,0:T(8,128)S(1)}, u32[]{:S(2)}, u32[]{:S(2)}) %collective-permute-start.15) | collective-permute-done | bytes 24608 | tf_op jit(solution)/shard_map/ppermute | solution.py:571
  29.2 0.0 collective-permute-done.14.ha
  29.2 1.0 %shard_map.105 = (f32[3,256,256]{2,1,0:T(8,128)S(1)}, f32[3,256,256]{2,1,0:T(8,128)S(1)}, f32[3,256,256]{2,1,0:T(8,128)}, f32[3,256,256]{2,1,0:T(8,128)}) custom-call(f32[3,256,256]{2,1,0:T(8,128)S(1)} %get-tuple-element.126.u1, f32[3,256,256]{2,1,0:T(8,128)S(1)} %get-tuple-element.127.v1, ...), custom_call_target="tpu_custom_call", output_to_operand_aliasing={{0}: (0, {}), {1}: (1, {}), {2}: (9, {}), {3}: (10, {})} | custom-call | flops 1 | bytes 1 | tf_op jit(solution)/shard_map/pallas_call | solution.py:58
  (3 shorter events, 0.0 us)
Async XLA Ops:
  0.6 1.8 %copy-start.1 = (f32[3,8,32,256]{3,2,1,0:T(8,128)S(1)}, f32[3,8,32,256]{3,2,1,0:T(8,128)}, u32[]{:S(2)}) copy-start(f32[3,8,32,256]{3,2,1,0:T(8,128)} %param.7) | copy-start | bytes 2359300
  0.6 1.7 %copy-start.3 = (s32[8,32,256]{2,1,0:T(8,128)S(1)}, s32[8,32,256]{2,1,0:T(8,128)}, u32[]{:S(2)}) copy-start(s32[8,32,256]{2,1,0:T(8,128)} %param.12) | copy-start | bytes 786436
  0.7 1.7 %copy-start.4 = (s32[8,32,256]{2,1,0:T(8,128)S(1)}, s32[8,32,256]{2,1,0:T(8,128)}, u32[]{:S(2)}) copy-start(s32[8,32,256]{2,1,0:T(8,128)} %param.11) | copy-start | bytes 786436
  1.9 7.7 %collective-permute-start.2 = (f32[4,32,256]{2,1,0:T(8,128)S(1)}, f32[4,32,256]{2,1,0:T(8,128)S(1)}, u32[]{:S(2)}, u32[]{:S(2)}) collective-permute-start(f32[4,32,256]{2,1,0:T(8,128)S(1)} %get-tuple-element.79.b_sent), channel_id=1, source_target_pairs={{0,1},{1,0},{2,3},{3,2},{4,8},{5,9},{6,10},{7,11},{8,4},{9,5},{10,... | collective-permute-start | bytes 393224 | tf_op jit(solution)/shard_map/ppermute | solution.py:568
  2.4 5.9 %copy-start = (f32[3,8,32,256]{3,2,1,0:T(8,128)S(1)}, f32[3,8,32,256]{3,2,1,0:T(8,128)}, u32[]{:S(2)}) copy-start(f32[3,8,32,256]{3,2,1,0:T(8,128)} %param.9) | copy-start | bytes 2359300
  2.4 5.9 %copy-start.2 = (f32[3,8,32,256]{3,2,1,0:T(8,128)S(1)}, f32[3,8,32,256]{3,2,1,0:T(8,128)}, u32[]{:S(2)}) copy-start(f32[3,8,32,256]{3,2,1,0:T(8,128)} %param.8) | copy-start | bytes 2359300
  2.6 6.5 %collective-permute-start = (f32[4,8,256]{2,1,0:T(8,128)S(1)}, f32[4,8,256]{2,1,0:T(8,128)S(1)}, u32[]{:S(2)}, u32[]{:S(2)}) collective-permute-start(f32[4,8,256]{2,1,0:T(8,128)S(1)} %get-tuple-element.80.ya_sent), channel_id=1, source_target_pairs={{0,1},{1,0},{2,3},{3,2},{4,5},{5,4},{6,7},{7,6},{8,9},{9,8},{10,11... | collective-permute-start | bytes 98312 | tf_op jit(solution)/shard_map/ppermute | solution.py:575
  2.7 6.4 %collective-permute-start.1 = (f32[4,8,256]{2,1,0:T(8,128)S(1)}, f32[4,8,256]{2,1,0:T(8,128)S(1)}, u32[]{:S(2)}, u32[]{:S(2)}) collective-permute-start(f32[4,8,256]{2,1,0:T(8,128)S(1)} %get-tuple-element.81.yb_sent.refs_1_), channel_id=1, source_target_pairs={{0,3},{1,2},{2,1},{3,0},{4,7},{5,6},{6,5},{7,4},{8,11},{9,10},{10,... | collective-permute-start | bytes 98312 | tf_op jit(solution)/shard_map/ppermute | solution.py:571
  5.3 6.7 %collective-permute-start.3 = (f32[4,32,256]{2,1,0:T(8,128)S(1)}, f32[4,32,256]{2,1,0:T(8,128)S(1)}, u32[]{:S(2)}, u32[]{:S(2)}) collective-permute-start(f32[4,32,256]{2,1,0:T(8,128)S(1)} %shard_map.91.a_sent), channel_id=1, source_target_pairs={{0,4},{1,5},{2,6},{3,7},{4,0},{5,1},{6,2},{7,3},{8,12},{9,13},{10,... | collective-permute-start | bytes 393224 | tf_op jit(solution)/shard_map/ppermute | solution.py:574
  9.6 5.6 %collective-permute-start.4 = (f32[3,32,256]{2,1,0:T(8,128)S(1)}, f32[3,32,256]{2,1,0:T(8,128)S(1)}, u32[]{:S(2)}, u32[]{:S(2)}) collective-permute-start(f32[3,32,256]{2,1,0:T(8,128)S(1)} %get-tuple-element.97), channel_id=1, source_target_pairs={{0,1},{1,0},{2,3},{3,2},{4,8},{5,9},{6,10},{7,11},{8,4},{9,5},{10,... | collective-permute-start | bytes 294920 | tf_op jit(solution)/shard_map/ppermute | solution.py:568
  9.8 5.4 %collective-permute-start.5 = (f32[4,8,256]{2,1,0:T(8,128)S(1)}, f32[4,8,256]{2,1,0:T(8,128)S(1)}, u32[]{:S(2)}, u32[]{:S(2)}) collective-permute-start(f32[4,8,256]{2,1,0:T(8,128)S(1)} %get-tuple-element.98), channel_id=1, source_target_pairs={{0,1},{1,0},{2,3},{3,2},{4,5},{5,4},{6,7},{7,6},{8,9},{9,8},{10,11... | collective-permute-start | bytes 98312 | tf_op jit(solution)/shard_map/ppermute | solution.py:575
  10.4 4.8 %collective-permute-start.6 = (f32[4,8,256]{2,1,0:T(8,128)S(1)}, f32[4,8,256]{2,1,0:T(8,128)S(1)}, u32[]{:S(2)}, u32[]{:S(2)}) collective-permute-start(f32[4,8,256]{2,1,0:T(8,128)S(1)} %get-tuple-element.99), channel_id=1, source_target_pairs={{0,3},{1,2},{2,1},{3,0},{4,7},{5,6},{6,5},{7,4},{8,11},{9,10},{10,... | collective-permute-start | bytes 98312 | tf_op jit(solution)/shard_map/ppermute | solution.py:571
  12.1 5.8 %collective-permute-start.7 = (f32[104,256]{1,0:T(8,128)S(1)}, f32[104,256]{1,0:T(8,128)S(1)}, u32[]{:S(2)}, u32[]{:S(2)}) collective-permute-start(f32[104,256]{1,0:T(8,128)S(1)} %get-tuple-element.105), channel_id=1, source_target_pairs={{0,4},{1,5},{2,6},{3,7},{4,0},{5,1},{6,2},{7,3},{8,12},{9,13},{10,... | collective-permute-start | bytes 319496 | tf_op jit(solution)/shard_map/ppermute | solution.py:574
  15.3 6.1 %collective-permute-start.8 = (f32[3,32,256]{2,1,0:T(8,128)S(1)}, f32[3,32,256]{2,1,0:T(8,128)S(1)}, u32[]{:S(2)}, u32[]{:S(2)}) collective-permute-start(f32[3,32,256]{2,1,0:T(8,128)S(1)} %get-tuple-element.111), channel_id=1, source_target_pairs={{0,1},{1,0},{2,3},{3,2},{4,8},{5,9},{6,10},{7,11},{8,4},{9,5},{10,... | collective-permute-start | bytes 294920 | tf_op jit(solution)/shard_map/ppermute | solution.py:568
  15.8 5.5 %collective-permute-start.9 = (f32[3,8,256]{2,1,0:T(8,128)S(1)}, f32[3,8,256]{2,1,0:T(8,128)S(1)}, u32[]{:S(2)}, u32[]{:S(2)}) collective-permute-start(f32[3,8,256]{2,1,0:T(8,128)S(1)} %get-tuple-element.112), channel_id=1, source_target_pairs={{0,1},{1,0},{2,3},{3,2},{4,5},{5,4},{6,7},{7,6},{8,9},{9,8},{10,11... | collective-permute-start | bytes 73736 | tf_op jit(solution)/shard_map/ppermute | solution.py:575
  16.4 5.0 %collective-permute-start.10 = (f32[3,8,256]{2,1,0:T(8,128)S(1)}, f32[3,8,256]{2,1,0:T(8,128)S(1)}, u32[]{:S(2)}, u32[]{:S(2)}) collective-permute-start(f32[3,8,256]{2,1,0:T(8,128)S(1)} %get-tuple-element.113), channel_id=1, source_target_pairs={{0,3},{1,2},{2,1},{3,0},{4,7},{5,6},{6,5},{7,4},{8,11},{9,10},{10,... | collective-permute-start | bytes 73736 | tf_op jit(solution)/shard_map/ppermute | solution.py:571
  18.0 6.1 %collective-permute-start.11 = (f32[104,256]{1,0:T(8,128)S(1)}, f32[104,256]{1,0:T(8,128)S(1)}, u32[]{:S(2)}, u32[]{:S(2)}) collective-permute-start(f32[104,256]{1,0:T(8,128)S(1)} %get-tuple-element.118), channel_id=1, source_target_pairs={{0,4},{1,5},{2,6},{3,7},{4,0},{5,1},{6,2},{7,3},{8,12},{9,13},{10,... | collective-permute-start | bytes 319496 | tf_op jit(solution)/shard_map/ppermute | solution.py:574
  21.4 5.5 %collective-permute-start.12 = (f32[3,32,256]{2,1,0:T(8,128)S(1)}, f32[3,32,256]{2,1,0:T(8,128)S(1)}, u32[]{:S(2)}, u32[]{:S(2)}) collective-permute-start(f32[3,32,256]{2,1,0:T(8,128)S(1)} %get-tuple-element.122), channel_id=1, source_target_pairs={{0,1},{1,0},{2,3},{3,2},{4,8},{5,9},{6,10},{7,11},{8,4},{9,5},{10,... | collective-permute-start | bytes 294920 | tf_op jit(solution)/shard_map/ppermute | solution.py:568
  24.2 5.1 %collective-permute-start.14 = (f32[96,256]{1,0:T(8,128)S(1)}, f32[96,256]{1,0:T(8,128)S(1)}, u32[]{:S(2)}, u32[]{:S(2)}) collective-permute-start(f32[96,256]{1,0:T(8,128)S(1)} %get-tuple-element.128.refs_1_), channel_id=1, source_target_pairs={{0,4},{1,5},{2,6},{3,7},{4,0},{5,1},{6,2},{7,3},{8,12},{9,13},{10,... | collective-permute-start | bytes 294920 | tf_op jit(solution)/shard_map/ppermute | solution.py:574
  26.0 2.4 %collective-permute-start.13 = (f32[3,8,256]{2,1,0:T(8,128)S(1)}, f32[3,8,256]{2,1,0:T(8,128)S(1)}, u32[]{:S(2)}, u32[]{:S(2)}) collective-permute-start(f32[3,8,256]{2,1,0:T(8,128)S(1)} %get-tuple-element.125), channel_id=1, source_target_pairs={{0,1},{1,0},{2,3},{3,2},{4,5},{5,4},{6,7},{7,6},{8,9},{9,8},{10,11... | collective-permute-start | bytes 73736 | tf_op jit(solution)/shard_map/ppermute | solution.py:575
  26.0 3.3 %collective-permute-start.15 = (f32[3,8,256]{2,1,0:T(8,128)S(1)}, f32[3,8,256]{2,1,0:T(8,128)S(1)}, u32[]{:S(2)}, u32[]{:S(2)}) collective-permute-start(f32[3,8,256]{2,1,0:T(8,128)S(1)} %shard_map.104), channel_id=1, source_target_pairs={{0,3},{1,2},{2,1},{3,0},{4,7},{5,6},{6,5},{7,4},{8,11},{9,10},{10,... | collective-permute-start | bytes 73736 | tf_op jit(solution)/shard_map/ppermute | solution.py:571
